TPU v7x, 32 devices: a whole 2x2x4 slice. The times are simulated.
32 devices in a mesh: lat: 4 (over z), slab: 8 (over y, x, core).
Axes of the slice: x: 2, y: 2, z: 4, core: 2. Of those that a mesh axis runs over, the one named last changes fastest.
Arguments:
- field_state: float32 [4, 32, 32, 5, 128], P('lat', 'slab'), may hold values from -6 to 6
- cotangent: float32 [4, 32, 32, 5, 128], P('lat', None, 'slab'), may hold values from -6 to 6
- vertical_weight: float32 [4, 32, 32, 128], P('lat', 'slab'), may hold values from 0 to 1
- diffusion_inverse: float32 [4, 5, 32, 32], P('lat'), as said below
- source_row: int32 [4, 8, 4, 8, 8], P('lat', 'slab'), may hold values from 0 to 95, as said below
- dest_slot: int32 [4, 8, 128], P('lat', 'slab'), may hold values from 0 to 255, as said below
Outputs:
- tangent_out: float32 [4, 32, 32, 5, 128], P('lat', None, 'slab')
- adjoint_out: float32 [4, 32, 32, 5, 128], P('lat', 'slab')
Inputs may be any that keep to these rules, and one draw needn't show every extreme that they name: `source_row`: from one sender to one receiver at most 8 slots are used, the used ones first; unused slots hold 0. Every value is below (3) * 32. `dest_slot`: each device's arrival rows name distinct used slots, and every used slot aimed at that device is named once; some sender fills all 8 slots to a receiver in every draw. `diffusion_inverse`: dense matrices of order one.
All inputs are finite; a program needn't handle non-finite values.
Results may differ from a plain program's by a relative error of at most 0.00007.
Values sent between devices are 32-bit elements; how exact they have to be, the bound alone decides.
No kernel may reach another device: no remote copies, remote signals or barrier semaphores. Data moves between devices by JAX's collectives and lax.ppermute only.
A program may use at most 128 MiB of HBM per device.

v0:
```python
import jax
import jax.numpy as jnp
from jax import lax
from jax.sharding import PartitionSpec as P


def select(table, values):
    return jnp.dot(
        table, values, precision=lax.Precision.HIGHEST, preferred_element_type=jnp.float32
    )


def select_back(table, values):
    return lax.dot_general(
        table,
        values,
        (((0,), (0,)), ((), ())),
        precision=lax.Precision.HIGHEST,
        preferred_element_type=jnp.float32,
    )


def body(field_state, cotangent, vertical_weight, diffusion_inverse, source_row, dest_slot):
    highest = lax.Precision.HIGHEST
    levels_here = field_state.shape[1]
    blocks = field_state.shape[2]
    fields = field_state.shape[3]
    width = field_state.shape[4]
    row_total = levels_here * blocks
    low_total = row_total - blocks
    flat_width = fields * width
    inverse = diffusion_inverse[0]
    level_rows = field_state.reshape(row_total, flat_width)
    weights = vertical_weight.reshape(row_total, width)
    lower_idx = source_row[0, 0]
    slots = dest_slot[0, 0]
    slot_total = lower_idx.size
    lower_flat = lower_idx.reshape(-1)
    row_ids = jnp.arange(low_total, dtype=jnp.int32)
    slot_ids = jnp.arange(slot_total, dtype=jnp.int32)
    source_table = (lower_flat[:, None] == row_ids[None, :]).astype(jnp.float32)
    arrival_table = (slots[:, None] == slot_ids[None, :]).astype(jnp.float32)
    stacked = jnp.concatenate([level_rows[:low_total], level_rows[blocks:]], axis=1)
    paired = select(source_table, stacked)
    paired = paired.reshape(lower_idx.shape + (2, fields, width))
    arrived = lax.all_to_all(
        lax.all_to_all(paired, "lat", split_axis=0, concat_axis=0, tiled=True),
        "slab",
        split_axis=1,
        concat_axis=1,
        tiled=True,
    )
    picked = select(arrival_table, arrived.reshape(slot_total, 2 * flat_width))
    picked = picked.reshape(row_total, 2, fields, width)
    scale = weights[:, None, :]
    moved = (1.0 - scale) * picked[:, 0] + scale * picked[:, 1]
    tangent_out = jnp.einsum(
        "flk,gkbfc->glbfc",
        inverse,
        lax.all_to_all(
            moved.reshape(field_state.shape), "slab", split_axis=2, concat_axis=1, tiled=True
        ),
        precision=highest,
    )
    back = jnp.einsum("flk,glbfc->gkbfc", inverse, cotangent, precision=highest)
    back = lax.all_to_all(back, "slab", split_axis=1, concat_axis=2, tiled=True)
    back = back.reshape(row_total, fields, width)
    scale = weights[:, None, :]
    pair_back = jnp.concatenate(
        [
            ((1.0 - scale) * back).reshape(row_total, flat_width),
            (scale * back).reshape(row_total, flat_width),
        ],
        axis=1,
    )
    slot_back = select_back(arrival_table, pair_back)
    returned = lax.all_to_all(
        lax.all_to_all(
            slot_back.reshape(lower_idx.shape + (2, fields, width)),
            "lat",
            split_axis=0,
            concat_axis=0,
            tiled=True,
        ),
        "slab",
        split_axis=1,
        concat_axis=1,
        tiled=True,
    )
    both_back = returned.reshape(slot_total, 2 * flat_width)
    gathered = select_back(source_table, both_back)
    lower_part = jnp.pad(gathered[:, :flat_width], ((0, blocks), (0, 0)))
    upper_part = jnp.pad(gathered[:, flat_width:], ((blocks, 0), (0, 0)))
    adjoint = lower_part + upper_part
    return (tangent_out, adjoint.reshape(field_state.shape))


def solution(mesh):
    placed = (
        P("lat", "slab", None, None, None),
        P("lat", None, "slab", None, None),
        P("lat", "slab", None, None),
        P("lat", None, None, None),
        P("lat", "slab", None, None, None),
        P("lat", "slab", None),
    )
    return jax.shard_map(
        body,
        mesh=mesh,
        in_specs=placed,
        out_specs=(P("lat", None, "slab", None, None), P("lat", "slab", None, None, None)),
        check_vma=False,
    )
```

profile of v0, /device:TPU:0, one launch (start us, length us, event | category | flops | bytes accessed | tf_op | source)
XLA Modules:
  0.0 143.4 jit_solution(10964748174673176605)
XLA Ops:
  0.6 0.0 copy-start
  0.6 0.0 copy-start.2
  0.7 0.9 copy-done
  1.5 1.4 %convolution_bitcast_fusion = f32[1,32,4,5,128]{4,1,2,3,0:T(8,128)S(1)} fusion(f32[32,4,5,128]{3,1,2,0:T(4,128)} %bitcast.82, f32[1,5,32,32]{3,2,1,0:T(8,128)S(1)} %copy-done), kind=kOutput, calls=%fused_computation | convolution fusion | flops 31457280 | bytes 675840 | tf_op jit(solution)/shard_map/flk,glbfc->gkbfc/dot_general | solution.py:65
  3.0 0.9 copy.82
  3.9 5.2 %all-to-all-start.3 = ((f32[1,32,4,5,128]{4,2,3,0,1:T(4,128)}), f32[1,32,4,5,128]{4,2,3,0,1:T(4,128)S(1)}, u32[]{:S(2)}, u32[]{:S(2)}) async-start(f32[1,32,4,5,128]{4,2,3,0,1:T(4,128)} %copy.82), calls=%async_computation.3 | async-start | bytes 655360 | tf_op jit(solution)/shard_map/all_to_all | solution.py:66
  9.1 0.0 copy-done.2
  9.1 0.0 copy-start.4
  9.2 0.1 copy.70
  9.3 0.1 copy.71
  9.5 0.1 copy_bitcast_fusion.1
  9.6 0.3 copy-done.4
  9.9 0.1 eq.34
  9.9 1.8 %fusion.4 = f32[256,1280]{1,0:T(8,128)} fusion(f32[96,640]{1,0:T(8,128)S(1)} %get-tuple-element.20, f32[96,640]{1,0:T(8,128)S(1)} %get-tuple-element.21, s32[256]{0:T(256)S(1)} %eq.34), kind=kOutput, calls=%fused_computation.6 | convolution fusion | flops 377634816 | bytes 1803264 | tf_op jit(solution)/shard_map/dot_general | solution.py:8
  11.7 5.0 %all-to-all-done.3 = f32[1,32,4,5,128]{4,2,3,0,1:T(4,128)S(1)} async-done(((f32[1,32,4,5,128]{4,2,3,0,1:T(4,128)}), f32[1,32,4,5,128]{4,2,3,0,1:T(4,128)S(1)}, u32[]{:S(2)}, u32[]{:S(2)}) %all-to-all-start.3) | async-done | bytes 327712 | tf_op jit(solution)/shard_map/all_to_all | solution.py:66
  16.7 0.0 copy-start.3
  16.7 5.0 %all-to-all-start = ((f32[4,8,8,2,5,128]{5,2,4,3,1,0:T(8,128)}), f32[4,8,8,2,5,128]{5,2,4,3,1,0:T(8,128)S(1)}, u32[]{:S(2)}, u32[]{:S(2)}) async-start(f32[4,8,8,2,5,128]{5,2,4,3,1,0:T(8,128)} %bitcast.4), calls=%async_computation | async-start | bytes 2621440 | tf_op jit(solution)/shard_map/all_to_all | solution.py:47
  21.7 0.0 copy-done.3
  21.7 0.1 copy.79
  21.8 0.1 copy.83
  21.9 0.0 copy-start.5
  21.9 0.1 copy.110
  22.0 0.2 copy.84
  22.2 0.4 copy-done.5
  22.6 1.8 %fusion = f32[256,1280]{1,0:T(8,128)} fusion(f32[128,640]{0,1:T(8,128)S(1)} %get-tuple-element.17, f32[128,640]{0,1:T(8,128)S(1)} %get-tuple-element.16, s32[128]{0:T(128)S(1)} %bitcast.83), kind=kOutput, calls=%fused_computation.2 | convolution fusion | flops 503545856 | bytes 1966592 | tf_op jit(solution)/shard_map/dot_general | solution.py:14
  24.4 27.6 %all-to-all-done = f32[4,8,8,2,5,128]{5,2,4,3,1,0:T(8,128)S(1)} async-done(((f32[4,8,8,2,5,128]{5,2,4,3,1,0:T(8,128)}), f32[4,8,8,2,5,128]{5,2,4,3,1,0:T(8,128)S(1)}, u32[]{:S(2)}, u32[]{:S(2)}) %all-to-all-start) | async-done | bytes 1310752 | tf_op jit(solution)/shard_map/all_to_all | solution.py:47
  52.1 3.5 %all-to-all-start.4 = ((f32[4,8,8,2,5,128]{5,2,4,3,1,0:T(8,128)}), f32[4,8,8,2,5,128]{5,2,4,3,1,0:T(8,128)S(1)}, u32[]{:S(2)}, u32[]{:S(2)}) async-start(f32[4,8,8,2,5,128]{5,2,4,3,1,0:T(8,128)} %bitcast.67), calls=%async_computation.4 | async-start | bytes 2621440 | tf_op jit(solution)/shard_map/all_to_all | solution.py:78
  55.6 1.2 copy.72
  56.8 29.6 %all-to-all-done.4 = f32[4,8,8,2,5,128]{5,2,4,3,1,0:T(8,128)S(1)} async-done(((f32[4,8,8,2,5,128]{5,2,4,3,1,0:T(8,128)}), f32[4,8,8,2,5,128]{5,2,4,3,1,0:T(8,128)S(1)}, u32[]{:S(2)}, u32[]{:S(2)}) %all-to-all-start.4) | async-done | bytes 1310752 | tf_op jit(solution)/shard_map/all_to_all | solution.py:78
  86.4 0.0 copy-start.1
  86.4 1.1 copy-done.1
  87.5 3.6 %all-to-all-start.1 = ((f32[4,8,8,2,5,128]{5,2,4,3,0,1:T(8,128)}), f32[4,8,8,2,5,128]{5,2,4,3,0,1:T(8,128)S(1)}, u32[]{:S(2)}, u32[]{:S(2)}) async-start(f32[4,8,8,2,5,128]{5,2,4,3,0,1:T(8,128)} %copy.72), calls=%async_computation.1 | async-start | bytes 2621440 | tf_op jit(solution)/shard_map/all_to_all | solution.py:46
  91.1 2.5 %copy.87 = f32[4,8,8,2,5,128]{5,2,4,3,0,1:T(8,128)} copy(f32[4,8,8,2,5,128]{5,2,4,3,1,0:T(8,128)} %copy-done.1) | data formatting | bytes 2621440 | tf_op jit(solution)/shard_map/all_to_all | solution.py:78
  93.5 15.7 %all-to-all-done.1 = f32[4,8,8,2,5,128]{5,2,4,3,0,1:T(8,128)S(1)} async-done(((f32[4,8,8,2,5,128]{5,2,4,3,0,1:T(8,128)}), f32[4,8,8,2,5,128]{5,2,4,3,0,1:T(8,128)S(1)}, u32[]{:S(2)}, u32[]{:S(2)}) %all-to-all-start.1) | async-done | bytes 1310752 | tf_op jit(solution)/shard_map/all_to_all | solution.py:46
  109.2 3.6 %all-to-all-start.5 = ((f32[4,8,8,2,5,128]{5,2,4,3,0,1:T(8,128)}), f32[4,8,8,2,5,128]{5,2,4,3,0,1:T(8,128)S(1)}, u32[]{:S(2)}, u32[]{:S(2)}) async-start(f32[4,8,8,2,5,128]{5,2,4,3,0,1:T(8,128)} %copy.87), calls=%async_computation.5 | async-start | bytes 2621440 | tf_op jit(solution)/shard_map/all_to_all | solution.py:77
  112.9 1.2 copy.73
  114.1 1.7 %copy.74 = f32[1280,256]{1,0:T(8,128)S(1)} copy(f32[1280,256]{0,1:T(8,128)} %bitcast.69) | data formatting | bytes 2621440 | tf_op jit(solution)/shard_map/dot_general | solution.py:8
  115.8 0.9 fusion.13
  116.7 1.2 fusion.9
  117.9 13.0 %all-to-all-done.5 = f32[4,8,8,2,5,128]{5,2,4,3,0,1:T(8,128)S(1)} async-done(((f32[4,8,8,2,5,128]{5,2,4,3,0,1:T(8,128)}), f32[4,8,8,2,5,128]{5,2,4,3,0,1:T(8,128)S(1)}, u32[]{:S(2)}, u32[]{:S(2)}) %all-to-all-start.5) | async-done | bytes 1310752 | tf_op jit(solution)/shard_map/all_to_all | solution.py:77
  130.9 3.4 %all-to-all-start.2 = ((f32[1,4,32,5,128]{4,1,3,0,2:T(4,128)}), f32[1,4,32,5,128]{4,1,3,0,2:T(4,128)S(1)}, u32[]{:S(2)}, u32[]{:S(2)}) async-start(f32[1,4,32,5,128]{4,1,3,0,2:T(4,128)} %fusion.9), calls=%async_computation.2 | async-start | bytes 655360 | tf_op jit(solution)/shard_map/all_to_all | solution.py:60
  134.4 0.1 copy.88
  134.5 0.7 fusion.10
  135.2 0.1 reshape.89
  135.3 0.8 copy.90
  136.1 5.9 %all-to-all-done.2 = f32[1,4,32,5,128]{4,1,3,0,2:T(4,128)S(1)} async-done(((f32[1,4,32,5,128]{4,1,3,0,2:T(4,128)}), f32[1,4,32,5,128]{4,1,3,0,2:T(4,128)S(1)}, u32[]{:S(2)}, u32[]{:S(2)}) %all-to-all-start.2) | async-done | bytes 327712 | tf_op jit(solution)/shard_map/all_to_all | solution.py:60
  141.9 0.1 copy.78
  142.0 0.4 convolution_bitcast_fusion.1
  142.4 0.9 copy.89
  (9 shorter events, 0.3 us)
Async XLA Ops:
  0.6 0.9 copy-start
  0.6 8.4 %copy-start.2 = (f32[1,4,32,5,128]{4,2,3,1,0:T(8,128)S(1)}, f32[1,4,32,5,128]{4,2,3,1,0:T(8,128)}, u32[]{:S(2)}) copy-start(f32[1,4,32,5,128]{4,2,3,1,0:T(8,128)} %param.6) | copy-start | bytes 983044
  3.9 12.8 %all-to-all-start.3 = ((f32[1,32,4,5,128]{4,2,3,0,1:T(4,128)}), f32[1,32,4,5,128]{4,2,3,0,1:T(4,128)S(1)}, u32[]{:S(2)}, u32[]{:S(2)}) async-start(f32[1,32,4,5,128]{4,2,3,0,1:T(4,128)} %copy.82), calls=%async_computation.3 | async-start | bytes 655360 | tf_op jit(solution)/shard_map/all_to_all | solution.py:66
  9.1 0.7 copy-start.4
  16.7 5.0 %copy-start.3 = (f32[1,4,32,128]{3,2,1,0:T(8,128)S(1)}, f32[1,4,32,128]{3,2,1,0:T(8,128)}, u32[]{:S(2)}) copy-start(f32[1,4,32,128]{3,2,1,0:T(8,128)} %param.8) | copy-start | bytes 196612
  16.7 35.3 %all-to-all-start = ((f32[4,8,8,2,5,128]{5,2,4,3,1,0:T(8,128)}), f32[4,8,8,2,5,128]{5,2,4,3,1,0:T(8,128)S(1)}, u32[]{:S(2)}, u32[]{:S(2)}) async-start(f32[4,8,8,2,5,128]{5,2,4,3,1,0:T(8,128)} %bitcast.4), calls=%async_computation | async-start | bytes 2621440 | tf_op jit(solution)/shard_map/all_to_all | solution.py:47
  21.9 0.7 copy-start.5
  52.1 34.4 %all-to-all-start.4 = ((f32[4,8,8,2,5,128]{5,2,4,3,1,0:T(8,128)}), f32[4,8,8,2,5,128]{5,2,4,3,1,0:T(8,128)S(1)}, u32[]{:S(2)}, u32[]{:S(2)}) async-start(f32[4,8,8,2,5,128]{5,2,4,3,1,0:T(8,128)} %bitcast.67), calls=%async_computation.4 | async-start | bytes 2621440 | tf_op jit(solution)/shard_map/all_to_all | solution.py:78
  86.4 1.1 copy-start.1
  87.5 21.7 %all-to-all-start.1 = ((f32[4,8,8,2,5,128]{5,2,4,3,0,1:T(8,128)}), f32[4,8,8,2,5,128]{5,2,4,3,0,1:T(8,128)S(1)}, u32[]{:S(2)}, u32[]{:S(2)}) async-start(f32[4,8,8,2,5,128]{5,2,4,3,0,1:T(8,128)} %copy.72), calls=%async_computation.1 | async-start | bytes 2621440 | tf_op jit(solution)/shard_map/all_to_all | solution.py:46
  109.2 21.7 %all-to-all-start.5 = ((f32[4,8,8,2,5,128]{5,2,4,3,0,1:T(8,128)}), f32[4,8,8,2,5,128]{5,2,4,3,0,1:T(8,128)S(1)}, u32[]{:S(2)}, u32[]{:S(2)}) async-start(f32[4,8,8,2,5,128]{5,2,4,3,0,1:T(8,128)} %copy.87), calls=%async_computation.5 | async-start | bytes 2621440 | tf_op jit(solution)/shard_map/all_to_all | solution.py:77
  130.9 11.0 %all-to-all-start.2 = ((f32[1,4,32,5,128]{4,1,3,0,2:T(4,128)}), f32[1,4,32,5,128]{4,1,3,0,2:T(4,128)S(1)}, u32[]{:S(2)}, u32[]{:S(2)}) async-start(f32[1,4,32,5,128]{4,1,3,0,2:T(4,128)} %fusion.9), calls=%async_computation.2 | async-start | bytes 655360 | tf_op jit(solution)/shard_map/all_to_all | solution.py:60
where the time goes:
time: 144 us; the launch traced here: 143 us
  waiting for transfers between devices  96.7 us (67%)
  starting transfers between devices  24.3 us (17%)
  local copies, waits for them, and re-layouts  13.2 us (9%)
  matrix products  7.04 us (5%)
    all_to_all x1, waiting for transfers between devices, body(): lax.all_to_all(slot_back.reshape(lower_idx.shape + (2, fields, width)), '...  29.6 us
    all_to_all x1, waiting for transfers between devices, body(): lax.all_to_all(paired, 'lat', split_axis=0, concat_axis=0, tiled=True)  27.6 us
    all_to_all x1, waiting for transfers between devices, body(): lax.all_to_all(lax.all_to_all(paired, 'lat', split_axis=0, concat_axis=0,...  15.7 us
    all_to_all x1, waiting for transfers between devices, body(): lax.all_to_all(lax.all_to_all(slot_back.reshape(lower_idx.shape + (2, fie...  13 us
    all_to_all x1, waiting for transfers between devices, body(): lax.all_to_all(moved.reshape(field_state.shape), 'slab', split_axis=2, co...  5.85 us
    all_to_all x1, starting transfers between devices, body(): back = lax.all_to_all(back, 'slab', split_axis=1, concat_axis=2, tiled=True)  5.17 us
    all_to_all x1, starting transfers between devices, body(): lax.all_to_all(paired, 'lat', split_axis=0, concat_axis=0, tiled=True)  4.99 us
    all_to_all x1, waiting for transfers between devices, body(): back = lax.all_to_all(back, 'slab', split_axis=1, concat_axis=2, tiled=True)  4.97 us
  transfers between devices with their start and end apart: 6, of which 6 were waited for; matrix products, arithmetic and copies ran while one was open for 11% of the time, Pallas kernels for 0%

commit v1 on v0

v1 whole, which is shorter than its diff:
```python
import functools

import jax
import jax.numpy as jnp
from jax import lax
from jax.experimental import pallas as pl
from jax.experimental.pallas import tpu as pltpu
from jax.sharding import PartitionSpec as P

LANES = 128
HIGHEST = lax.Precision.HIGHEST


def parts_of(values):
    high = values.astype(jnp.bfloat16)
    rest = values - high.astype(jnp.float32)
    mid = rest.astype(jnp.bfloat16)
    low = (rest - mid.astype(jnp.float32)).astype(jnp.bfloat16)
    return low, mid, high


def pick(table, values, contract):
    total = None
    for part in parts_of(values):
        term = lax.dot_general(
            table, part, ((contract, (0,)), ((), ())), preferred_element_type=jnp.float32
        )
        total = term if total is None else total + term
    return total


def hot(rows, wanted):
    return jnp.where(rows == wanted, 1.0, 0.0).astype(jnp.bfloat16)


def sizes(mesh_lat, mesh_slab, cap):
    return mesh_lat, mesh_slab, mesh_slab // 2, cap


def start_kernel(dims, me, cot, inverse, weights, dest, *rest):
    lats, slabs, chips, cap, lev_dev, here, fields = dims
    out_back, out_w = rest[:chips], rest[chips : 2 * chips]
    back, = rest[2 * chips :]
    chip = me[1]
    levels = slabs * lev_dev
    step = fields * here
    span = lev_dev * here
    for f in range(fields):
        wide = jnp.concatenate(
            [cot[pl.ds(f * here + b, levels, stride=step), :] for b in range(here)], axis=1
        )
        res = lax.dot_general(
            inverse[f], wide, (((0,), (0,)), ((), ())), precision=HIGHEST, preferred_element_type=jnp.float32
        )
        for b in range(here):
            back[f, pl.ds(b, levels, stride=here), :] = res[:, b * LANES : (b + 1) * LANES]
    for k in range(chips):
        other = jnp.bitwise_xor(chip, k)
        for h in range(2):
            first = pl.multiple_of((other * 2 + h) * span, span)
            for f in range(fields):
                out_back[k][h, f] = back[f, pl.ds(first, span), :]
    slots = slabs * cap
    rows = lax.broadcasted_iota(jnp.int32, (slots, dest.shape[1]), 0)
    for k in range(chips):
        other = jnp.bitwise_xor(chip, k)
        per = lats * cap
        local = lax.broadcasted_iota(jnp.int32, (2 * per, dest.shape[1]), 0)
        half = local // per
        lat = (local - half * per) // cap
        slot = local - half * per - lat * cap
        wanted = lat * slots + (other * 2 + half) * cap + slot
        res = pick(hot(wanted, dest[...]), weights[...], (1,))
        for h in range(2):
            for g in range(lats):
                at = (h * lats + g) * cap
                out_w[k][h, g] = res[at : at + cap]


def back_kernel(dims, me, dest, *rest):
    lats, slabs, chips, cap, lev_dev, here, fields = dims
    got, out, rows = rest[: 2 * chips], rest[2 * chips : 3 * chips], rest[3 * chips]
    chip, core = me[1], me[2]
    span = lev_dev * here
    for k in range(chips):
        for x in range(2):
            src = jnp.bitwise_xor(chip, k) * 2 + jnp.bitwise_xor(core, x)
            first = pl.multiple_of(src * span, span)
            for f in range(fields):
                rows[pl.ds(first, span), f * LANES : (f + 1) * LANES] = got[2 * k + x][core, f]
    values = rows[...]
    slots = slabs * cap
    per = lats * cap
    local = lax.broadcasted_iota(jnp.int32, (2 * per, dest.shape[1]), 0)
    half = local // per
    lat = (local - half * per) // cap
    slot = local - half * per - lat * cap
    tables = []
    for k in range(chips):
        wanted = lat * slots + (jnp.bitwise_xor(chip, k) * 2 + half) * cap + slot
        tables.append(hot(wanted, dest[...]))
    res = pick(jnp.concatenate(tables, axis=0), values, (1,))
    for k in range(chips):
        for h in range(2):
            for g in range(lats):
                at = ((k * 2 + h) * lats + g) * cap
                for f in range(fields):
                    out[k][h, g, f] = res[at : at + cap, f * LANES : (f + 1) * LANES]


def gather_kernel(dims, me, *rest):
    lats, slabs, chips, cap, lev_dev, here, fields = dims
    got, got_w, out = rest[: 2 * chips], rest[2 * chips : 4 * chips], rest[4 * chips :]
    lat, chip, core = me[0], me[1], me[2]
    for j in range(lats):
        other = jnp.bitwise_xor(lat, j)
        for k in range(chips):
            for x in range(2):
                src = jnp.bitwise_xor(chip, k) * 2 + jnp.bitwise_xor(core, x)
                for f in range(fields):
                    out[j][f, src] = got[2 * k + x][core, other, f]
                out[j][fields, src] = got_w[2 * k + x][core, other]


def add_kernel(dims, me, source, *rest):
    lats, slabs, chips, cap, lev_dev, here, fields = dims
    got, out = rest[:lats], rest[lats]
    blocks = slabs * here
    row_total = lev_dev * blocks
    slots = slabs * cap
    lat = me[0]
    row = lax.broadcasted_iota(jnp.int32, (row_total, slots), 0)
    total = None
    for j in range(lats):
        low = source[jnp.bitwise_xor(lat, j)]
        weight = got[j][fields].reshape(slots, LANES)
        scale = jnp.concatenate([weight] * fields, axis=1)
        values = jnp.concatenate([got[j][f].reshape(slots, LANES) for f in range(fields)], axis=1)
        both = jnp.concatenate([(1.0 - scale) * values, scale * values], axis=0)
        table = jnp.concatenate([hot(row, low), hot(row, low + blocks)], axis=1)
        term = pick(table, both, (1,))
        total = term if total is None else total + term
    for l in range(lev_dev):
        for f in range(fields):
            out[l, f] = total[l * blocks : (l + 1) * blocks, f * LANES : (f + 1) * LANES]


def mix_kernel(dims, me, *rest):
    lats, slabs, chips, cap, lev_dev, here, fields = dims
    state, source, got_w = rest[:lats], rest[lats : 2 * lats], rest[2 * lats : 2 * lats + 2 * chips]
    out = rest[2 * lats + 2 * chips : 2 * lats + 3 * chips]
    weight, mixed = rest[2 * lats + 3 * chips :]
    lat, chip, core = me[0], me[1], me[2]
    blocks = slabs * here
    row_total = lev_dev * blocks
    slots = slabs * cap
    for k in range(chips):
        for x in range(2):
            src = jnp.bitwise_xor(chip, k) * 2 + jnp.bitwise_xor(core, x)
            for g in range(lats):
                weight[g, src] = got_w[2 * k + x][core, g]
    row = lax.broadcasted_iota(jnp.int32, (row_total, slots), 0)
    for j in range(lats):
        sender = jnp.bitwise_xor(lat, j)
        low = source[j][lat]
        values = jnp.concatenate(
            [state[j][:, f].reshape(row_total, LANES) for f in range(fields)], axis=1
        )
        table = jnp.concatenate([hot(row, low), hot(row, low + blocks)], axis=1)
        both = pick(table, values, (0,))
        scale = jnp.concatenate([weight[sender].reshape(slots, LANES)] * fields, axis=1)
        res = (1.0 - scale) * both[:slots] + scale * both[slots:]
        for s in range(slabs):
            for f in range(fields):
                mixed[s, f] = res[s * cap : (s + 1) * cap, f * LANES : (f + 1) * LANES]
        for k in range(chips):
            for h in range(2):
                to = jnp.bitwise_xor(chip, k) * 2 + h
                out[k][h, sender] = mixed[to]


def arrive_kernel(dims, me, dest, *rest):
    lats, slabs, chips, cap, lev_dev, here, fields = dims
    got, out = rest[: 2 * chips], rest[2 * chips : 3 * chips]
    rows, moved = rest[3 * chips :]
    chip, core = me[1], me[2]
    span = lev_dev * here
    slots = slabs * cap
    for k in range(chips):
        for x in range(2):
            src = jnp.bitwise_xor(chip, k) * 2 + jnp.bitwise_xor(core, x)
            for g in range(lats):
                for f in range(fields):
                    rows[f, g * slabs + src] = got[2 * k + x][core, g, f]
    values = jnp.concatenate([rows[f].reshape(lats * slots, LANES) for f in range(fields)], axis=1)
    slot = lax.broadcasted_iota(jnp.int32, (lats * slots, dest.shape[1]), 0)
    res = pick(hot(slot, dest[...]), values, (0,))
    for s in range(slabs):
        for f in range(fields):
            moved[s, f] = res[s * span : (s + 1) * span, f * LANES : (f + 1) * LANES]
    for k in range(chips):
        for h in range(2):
            out[k][h] = moved[jnp.bitwise_xor(chip, k) * 2 + h]


def diffuse_kernel(dims, me, inverse, *rest):
    lats, slabs, chips, cap, lev_dev, here, fields = dims
    got, out, rows = rest[: 2 * chips], rest[2 * chips], rest[2 * chips + 1]
    chip, core = me[1], me[2]
    span = lev_dev * here
    levels = slabs * lev_dev
    for k in range(chips):
        for x in range(2):
            src = jnp.bitwise_xor(chip, k) * 2 + jnp.bitwise_xor(core, x)
            first = pl.multiple_of(src * span, span)
            for f in range(fields):
                rows[f, pl.ds(first, span), :] = got[2 * k + x][core, f]
    for f in range(fields):
        wide = jnp.concatenate(
            [rows[f, pl.ds(b, levels, stride=here), :] for b in range(here)], axis=1
        )
        res = jnp.dot(inverse[f], wide, precision=HIGHEST, preferred_element_type=jnp.float32)
        for b in range(here):
            out[pl.ds(f * here + b, levels, stride=fields * here), :] = res[:, b * LANES : (b + 1) * LANES]


def call(kernel, dims, args, outs, scratch=()):
    f32 = jnp.float32
    specs = [pl.BlockSpec(memory_space=pltpu.SMEM)] + [pl.BlockSpec(memory_space=pltpu.VMEM)] * (len(args) - 1)
    return pl.pallas_call(
        functools.partial(kernel, dims),
        out_shape=[jax.ShapeDtypeStruct(shape, f32) for shape in outs],
        in_specs=specs,
        out_specs=[pl.BlockSpec(memory_space=pltpu.VMEM)] * len(outs),
        scratch_shapes=[pltpu.VMEM(shape, f32) for shape in scratch],
        compiler_params=pltpu.CompilerParams(vmem_limit_bytes=48 * 1024 * 1024),
    )(*args)


def swap(array, axis, bit, count):
    return lax.ppermute(array, axis, [(i, i ^ bit) for i in range(count)])


def over_slab(messages, slabs):
    got = []
    for k, message in enumerate(messages):
        arrived = message if k == 0 else swap(message, "slab", 2 * k, slabs)
        got += [arrived, swap(arrived, "slab", 1, slabs)]
    return got


def body(lats, slabs, field_state, cotangent, vertical_weight, diffusion_inverse, source_row, dest_slot):
    _, lev_dev, blocks, fields, width = field_state.shape
    cap = source_row.shape[-1]
    chips = slabs // 2
    here = blocks // slabs
    levels = slabs * lev_dev
    row_total = lev_dev * blocks
    span = lev_dev * here
    dims = (lats, slabs, chips, cap, lev_dev, here, fields)
    lat, slab = lax.axis_index("lat"), lax.axis_index("slab")
    me = jnp.stack([lat, slab // 2, slab % 2]).astype(jnp.int32)

    state = field_state[0].transpose(0, 2, 1, 3)
    cot = cotangent[0].transpose(0, 2, 1, 3).reshape(levels * fields * here, width)
    weights = vertical_weight.reshape(row_total, width)
    inverse = diffusion_inverse[0]
    dest = dest_slot[0]
    dest_sorted = dest.reshape(lev_dev, slabs, here).transpose(1, 0, 2).reshape(1, row_total)
    source = source_row.reshape(lats, 1, slabs * cap)

    states, sources = [state], [source]
    for j in range(1, lats):
        if j % 2 == 0 or j == 1:
            states.append(swap(state, "lat", j, lats))
        else:
            states.append(swap(states[j - 1], "lat", 1, lats))
        sources.append(swap(source, "lat", j, lats))

    first = call(
        start_kernel,
        dims,
        (me, cot, inverse, weights, dest),
        [(2, fields, span, width)] * chips + [(2, lats, cap, width)] * chips,
        [(fields, levels * here, width)],
    )
    back = over_slab(first[:chips], slabs)
    slot_weight = over_slab(first[chips:], slabs)

    slot_back = call(
        back_kernel,
        dims,
        (me, dest_sorted, *back),
        [(2, lats, fields, cap, width)] * chips,
        [(row_total, fields * width)],
    )
    sorted_back = call(
        gather_kernel,
        dims,
        (me, *over_slab(slot_back, slabs), *slot_weight),
        [(fields + 1, slabs, cap, width)] * lats,
    )
    returned = [message if j == 0 else swap(message, "lat", j, lats) for j, message in enumerate(sorted_back)]
    (adjoint,) = call(add_kernel, dims, (me, source, *returned), [(lev_dev, fields, blocks, width)])

    mixed = call(
        mix_kernel,
        dims,
        (me, *states, *sources, *slot_weight),
        [(2, lats, fields, cap, width)] * chips,
        [(lats, slabs, cap, width), (slabs, fields, cap, width)],
    )
    moved = call(
        arrive_kernel,
        dims,
        (me, dest_sorted, *over_slab(mixed, slabs)),
        [(2, fields, span, width)] * chips,
        [(fields, lats * slabs, cap, width), (slabs, fields, span, width)],
    )
    (tangent,) = call(
        diffuse_kernel,
        dims,
        (me, inverse, *over_slab(moved, slabs)),
        [(levels * fields * here, width)],
        [(fields, levels * here, width)],
    )
    tangent_out = tangent.reshape(1, levels, fields, here, width).transpose(0, 1, 3, 2, 4)
    adjoint_out = adjoint.transpose(0, 2, 1, 3)[None]
    return tangent_out, adjoint_out


def solution(mesh):
    placed = (
        P("lat", "slab", None, None, None),
        P("lat", None, "slab", None, None),
        P("lat", "slab", None, None),
        P("lat", None, None, None),
        P("lat", "slab", None, None, None),
        P("lat", "slab", None),
    )
    return jax.shard_map(
        functools.partial(body, mesh.shape["lat"], mesh.shape["slab"]),
        mesh=mesh,
        in_specs=placed,
        out_specs=(P("lat", None, "slab", None, None), P("lat", "slab", None, None, None)),
        check_vma=False,
    )
```

time: 144 us -> 82.2 us (0.57)
  waiting for transfers between devices: 96.7 us -> 29.6 us
  starting transfers between devices: 24.3 us -> 37.3 us
  local copies, waits for them, and re-layouts: 13.2 us -> 3.99 us
  Pallas kernels: 0 us -> 8.88 us
  matrix products: 7.04 us -> 0 us
    all_to_all x6 -> x0, waiting for transfers between devices: 96.7 us -> none  [the longest x1 29.6 us: body(): lax.all_to_all(slot_back.reshape(lower_idx.shape + (2, fields, width)), '...]
    ppermute x0 -> x44, starting transfers between devices: none -> 37.3 us  [swap(): return lax.ppermute(array, axis, [(i, i ^ bit) for i in range(count)])]
    ppermute x0 -> x44, waiting for transfers between devices: none -> 29.6 us  [swap(): return lax.ppermute(array, axis, [(i, i ^ bit) for i in range(count)])]
    all_to_all x6 -> x0, starting transfers between devices: 24.3 us -> none  [the longest x1 5.17 us: body(): back = lax.all_to_all(back, 'slab', split_axis=1, concat_axis=2, tiled=True)]
    pallas_call x0 -> x7, Pallas kernels: none -> 8.88 us  [call(): pl.pallas_call(functools.partial(kernel, dims), out_shape=[jax.ShapeDtype...]
    dot_general x6 -> x0, matrix products: 7.04 us -> none  [the longest x2 2.68 us: select(): jnp.dot(table, values, precision=lax.Precision.HIGHEST, preferred_element...]
    all_to_all x6 -> x0, local copies, waits for them, and re-layouts: 5.13 us -> none  [the longest x1 2.49 us: body(): lax.all_to_all(slot_back.reshape(lower_idx.shape + (2, fields, width)), '...]
    dot_general x1 -> x0, local copies, waits for them, and re-layouts: 1.71 us -> none  [select(): jnp.dot(table, values, precision=lax.Precision.HIGHEST, preferred_element...]
  transfers between devices with their start and end apart: 6 -> 44, of which waited for: 6 -> 11; matrix products, arithmetic and copies ran while one was open for 11% -> 3% of each run, Pallas kernels for 0% -> 9%
where the time goes in v1:
time: 82.2 us; the launch traced here: 81.4 us
  starting transfers between devices  37.3 us (45%)
  waiting for transfers between devices  29.6 us (36%)
  Pallas kernels  8.88 us (11%)
  local copies, waits for them, and re-layouts  3.99 us (5%)
    ppermute x44, starting transfers between devices, swap(): return lax.ppermute(array, axis, [(i, i ^ bit) for i in range(count)])  37.3 us
    ppermute x44, waiting for transfers between devices, swap(): return lax.ppermute(array, axis, [(i, i ^ bit) for i in range(count)])  29.6 us
    pallas_call x7, Pallas kernels, call(): pl.pallas_call(functools.partial(kernel, dims), out_shape=[jax.ShapeDtype...  8.88 us
    unnamed x11, local copies, waits for them, and re-layouts  2.98 us
  transfers between devices with their start and end apart: 44, of which 11 were waited for; matrix products, arithmetic and copies ran while one was open for 3% of the time, Pallas kernels for 9%

profile of v1, /device:TPU:0, one launch (start us, length us, event | category | flops | bytes accessed | tf_op | source)
XLA Modules:
  0.0 81.4 jit_solution(11948631926742317788)
XLA Ops:
  0.6 4.1 %collective-permute-start.1 = (f32[4,5,32,128]{3,2,1,0:T(8,128)}, f32[4,5,32,128]{3,2,1,0:T(8,128)S(1)}, u32[]{:S(2)}, u32[]{:S(2)}) collective-permute-start(f32[4,5,32,128]{3,2,1,0:T(8,128)} %bitcast.24), channel_id=1, source_target_pairs={{0,16},{8,24},{16,0},{24,8},{1,17},{9,25},{17,1},{25,9},{2,18},{10... | collective-permute-start | bytes 983048 | tf_op jit(solution)/shard_map/ppermute | solution.py:241
  4.7 0.8 reshape.20.rest_4_.source
  5.5 1.6 %collective-permute-start.3 = (s32[4,1,64]{2,1,0:T(1,128)S(1)}, s32[4,1,64]{2,1,0:T(1,128)S(1)}, u32[]{:S(2)}, u32[]{:S(2)}) collective-permute-start(s32[4,1,64]{2,1,0:T(1,128)S(1)} %reshape.20.rest_4_.source), channel_id=1, source_target_pairs={{0,8},{8,0},{16,24},{24,16},{1,9},{9,1},{17,25},{25,17},{2,10},{10... | collective-permute-start | bytes 3080 | tf_op jit(solution)/shard_map/ppermute | solution.py:241
  7.1 0.3 collective-permute-start.4
  7.5 2.5 %collective-permute-start.5 = (s32[4,1,64]{2,1,0:T(1,128)S(1)}, s32[4,1,64]{2,1,0:T(1,128)S(1)}, u32[]{:S(2)}, u32[]{:S(2)}) collective-permute-start(s32[4,1,64]{2,1,0:T(1,128)S(1)} %reshape.20.rest_4_.source), channel_id=1, source_target_pairs={{0,24},{8,16},{16,8},{24,0},{1,25},{9,17},{17,9},{25,1},{2,26},{10... | collective-permute-start | bytes 3080 | tf_op jit(solution)/shard_map/ppermute | solution.py:241
  9.9 0.1 pad_add_fusion.me
  10.0 0.7 copy-done.4
  10.7 1.0 %copy-done = f32[1,32,4,5,128]{4,2,3,1,0:T(4,128)S(1)} copy-done((f32[1,32,4,5,128]{4,2,3,1,0:T(4,128)S(1)}, f32[1,32,4,5,128]{4,2,3,1,0:T(4,128)}, u32[]{:S(2)}) %copy-start) | copy-done | bytes 327704
  11.7 0.8 %copy-done.3 = f32[1,4,32,128]{3,2,1,0:T(8,128)S(1)} copy-done((f32[1,4,32,128]{3,2,1,0:T(8,128)S(1)}, f32[1,4,32,128]{3,2,1,0:T(8,128)}, u32[]{:S(2)}) %copy-start.3) | copy-done | bytes 65560
  12.5 1.1 %shard_map.77 = (f32[2,5,16,128]{3,2,1,0:T(8,128)S(1)}, f32[2,5,16,128]{3,2,1,0:T(8,128)S(1)}, f32[2,5,16,128]{3,2,1,0:T(8,128)S(1)}, f32[2,5,16,128]{3,2,1,0:T(...) custom-call(s32[3]{0:T(128)S(1)} %pad_add_fusion.me, ...), custom_call_target="tpu_custom_call" | custom-call | tf_op jit(solution)/shard_map/pallas_call | solution.py:230
  13.6 1.5 %collective-permute-start.28 = (f32[2,5,16,128]{3,2,1,0:T(8,128)S(1)}, f32[2,5,16,128]{3,2,1,0:T(8,128)S(1)}, u32[]{:S(2)}, u32[]{:S(2)}) collective-permute-start(f32[2,5,16,128]{3,2,1,0:T(8,128)S(1)} %get-tuple-element.39), channel_id=1, source_target_pairs={{0,2},{1,3},{2,0},{3,1},{4,6},{5,7},{6,4},{7,5},{8,10},{9,11},{10,... | collective-permute-start | bytes 245768 | tf_op jit(solution)/shard_map/ppermute | solution.py:241
  15.1 1.5 %collective-permute-start.30 = (f32[2,5,16,128]{3,2,1,0:T(8,128)S(1)}, f32[2,5,16,128]{3,2,1,0:T(8,128)S(1)}, u32[]{:S(2)}, u32[]{:S(2)}) collective-permute-start(f32[2,5,16,128]{3,2,1,0:T(8,128)S(1)} %get-tuple-element.40), channel_id=1, source_target_pairs={{0,4},{1,5},{2,6},{3,7},{4,0},{5,1},{6,2},{7,3},{8,12},{9,13},{10,... | collective-permute-start | bytes 245768 | tf_op jit(solution)/shard_map/ppermute | solution.py:241
  16.6 3.2 %collective-permute-done.4.rest_6_ = s32[4,1,64]{2,1,0:T(1,128)S(1)} collective-permute-done((s32[4,1,64]{2,1,0:T(1,128)S(1)}, s32[4,1,64]{2,1,0:T(1,128)S(1)}, u32[]{:S(2)}, u32[]{:S(2)}) %collective-permute-start.4) | collective-permute-done | bytes 1056 | tf_op jit(solution)/shard_map/ppermute | solution.py:241
  19.8 2.5 %collective-permute-start.32 = (f32[2,5,16,128]{3,2,1,0:T(8,128)S(1)}, f32[2,5,16,128]{3,2,1,0:T(8,128)S(1)}, u32[]{:S(2)}, u32[]{:S(2)}) collective-permute-start(f32[2,5,16,128]{3,2,1,0:T(8,128)S(1)} %get-tuple-element.41), channel_id=1, source_target_pairs={{0,6},{1,7},{2,4},{3,5},{4,2},{5,3},{6,0},{7,1},{8,14},{9,15},{10,... | collective-permute-start | bytes 245768 | tf_op jit(solution)/shard_map/ppermute | solution.py:241
  22.3 0.0 collective-permute-done.5.rest_7_
  22.3 0.0 collective-permute-start.27
  22.3 0.5 collective-permute-start.29
  22.9 0.1 collective-permute-start.31
  22.9 2.3 %collective-permute-done.32.rest_6_ = f32[2,5,16,128]{3,2,1,0:T(8,128)S(1)} collective-permute-done((f32[2,5,16,128]{3,2,1,0:T(8,128)S(1)}, f32[2,5,16,128]{3,2,1,0:T(8,128)S(1)}, u32[]{:S(2)}, u32[]{:S(2)}) %collective-permute-start.32) | collective-permute-done | bytes 81952 | tf_op jit(solution)/shard_map/ppermute | solution.py:241
  25.2 0.9 %collective-permute-start = (f32[4,5,32,128]{3,2,1,0:T(8,128)S(1)}, f32[4,5,32,128]{3,2,1,0:T(8,128)S(1)}, u32[]{:S(2)}, u32[]{:S(2)}) collective-permute-start(f32[4,5,32,128]{3,2,1,0:T(8,128)S(1)} %bitcast.25), channel_id=1, source_target_pairs={{0,8},{8,0},{16,24},{24,16},{1,9},{9,1},{17,25},{25,17},{2,10},{10... | collective-permute-start | bytes 983048 | tf_op jit(solution)/shard_map/ppermute | solution.py:241
  26.1 1.5 %collective-permute-start.9 = (f32[2,4,8,128]{3,2,1,0:T(8,128)S(1)}, f32[2,4,8,128]{3,2,1,0:T(8,128)S(1)}, u32[]{:S(2)}, u32[]{:S(2)}) collective-permute-start(f32[2,4,8,128]{3,2,1,0:T(8,128)S(1)} %get-tuple-element.28), channel_id=1, source_target_pairs={{0,4},{1,5},{2,6},{3,7},{4,0},{5,1},{6,2},{7,3},{8,12},{9,13},{10,... | collective-permute-start | bytes 98312 | tf_op jit(solution)/shard_map/ppermute | solution.py:241
  27.6 1.4 %collective-permute-start.11 = (f32[2,4,8,128]{3,2,1,0:T(8,128)S(1)}, f32[2,4,8,128]{3,2,1,0:T(8,128)S(1)}, u32[]{:S(2)}, u32[]{:S(2)}) collective-permute-start(f32[2,4,8,128]{3,2,1,0:T(8,128)S(1)} %get-tuple-element.29), channel_id=1, source_target_pairs={{0,6},{1,7},{2,4},{3,5},{4,2},{5,3},{6,0},{7,1},{8,14},{9,15},{10,... | collective-permute-start | bytes 98312 | tf_op jit(solution)/shard_map/ppermute | solution.py:241
  29.0 0.5 collective-permute-start.7
  29.6 1.2 %collective-permute-start.2 = (f32[4,5,32,128]{3,2,1,0:T(8,128)S(1)}, f32[4,5,32,128]{3,2,1,0:T(8,128)S(1)}, u32[]{:S(2)}, u32[]{:S(2)}) collective-permute-start(f32[4,5,32,128]{3,2,1,0:T(8,128)S(1)} %collective-permute-done.1.rest_2_), channel_id=1, source_target_pairs={{0,8},{8,0},{16,24},{24,16},{1,9},{9,1},{17,25},{25,17},{2,10},{10... | collective-permute-start | bytes 983048 | tf_op jit(solution)/shard_map/ppermute | solution.py:241
  30.8 0.5 broadcast.5
  31.3 0.7 reduce.3
  32.0 0.1 reshape_squeeze.3
  32.1 0.1 reshape.19.dest
  32.2 1.0 %shard_map.81 = (f32[2,4,5,8,128]{4,3,2,1,0:T(8,128)S(1)}, f32[2,4,5,8,128]{4,3,2,1,0:T(8,128)S(1)}, f32[2,4,5,8,128]{4,3,2,1,0:T(8,128)S(1)}, f32[2,4,5,8,128]{4,3,2,1,0:T(8,128)S(1)}) custom-call(s32[3]{0:T(128)S(1)} %pad_add_fusion.me, s32[1,128]{1,0:T(1,128)S(1)} %reshape.19.dest, f32[2,5,16,128]{3,2,1,0:T(8,128)S(1)} %get-tuple-element.38.rest_0_, ...), custom_call_target="tpu_custom_call" | custom-call | tf_op jit(solution)/shard_map/pallas_call | solution.py:230
  33.2 1.6 %collective-permute-start.35 = (f32[2,4,5,8,128]{4,3,2,1,0:T(8,128)S(1)}, f32[2,4,5,8,128]{4,3,2,1,0:T(8,128)S(1)}, u32[]{:S(2)}, u32[]{:S(2)}) collective-permute-start(f32[2,4,5,8,128]{4,3,2,1,0:T(8,128)S(1)} %get-tuple-element.43), channel_id=1, source_target_pairs={{0,2},{1,3},{2,0},{3,1},{4,6},{5,7},{6,4},{7,5},{8,10},{9,11},{10,... | collective-permute-start | bytes 491528 | tf_op jit(solution)/shard_map/ppermute | solution.py:241
  34.8 1.5 %collective-permute-start.37 = (f32[2,4,5,8,128]{4,3,2,1,0:T(8,128)S(1)}, f32[2,4,5,8,128]{4,3,2,1,0:T(8,128)S(1)}, u32[]{:S(2)}, u32[]{:S(2)}) collective-permute-start(f32[2,4,5,8,128]{4,3,2,1,0:T(8,128)S(1)} %get-tuple-element.44), channel_id=1, source_target_pairs={{0,4},{1,5},{2,6},{3,7},{4,0},{5,1},{6,2},{7,3},{8,12},{9,13},{10,... | collective-permute-start | bytes 491528 | tf_op jit(solution)/shard_map/ppermute | solution.py:241
  36.3 1.2 %collective-permute-done.6.rest_9_ = f32[2,4,8,128]{3,2,1,0:T(8,128)S(1)} collective-permute-done((f32[2,4,8,128]{3,2,1,0:T(8,128)S(1)}, f32[2,4,8,128]{3,2,1,0:T(8,128)S(1)}, u32[]{:S(2)}, u32[]{:S(2)}) %collective-permute-start.6) | collective-permute-done | bytes 32800 | tf_op jit(solution)/shard_map/ppermute | solution.py:241
  37.5 0.2 collective-permute-start.10
  37.7 1.0 %collective-permute-done.10.rest_13_ = f32[2,4,8,128]{3,2,1,0:T(8,128)S(1)} collective-permute-done((f32[2,4,8,128]{3,2,1,0:T(8,128)S(1)}, f32[2,4,8,128]{3,2,1,0:T(8,128)S(1)}, u32[]{:S(2)}, u32[]{:S(2)}) %collective-permute-start.10) | collective-permute-done | bytes 32800 | tf_op jit(solution)/shard_map/ppermute | solution.py:241
  38.8 0.2 collective-permute-start.12
  38.9 1.0 %collective-permute-done.12.rest_15_ = f32[2,4,8,128]{3,2,1,0:T(8,128)S(1)} collective-permute-done((f32[2,4,8,128]{3,2,1,0:T(8,128)S(1)}, f32[2,4,8,128]{3,2,1,0:T(8,128)S(1)}, u32[]{:S(2)}, u32[]{:S(2)}) %collective-permute-start.12) | collective-permute-done | bytes 32800 | tf_op jit(solution)/shard_map/ppermute | solution.py:241
  40.0 0.2 collective-permute-start.8
  40.1 1.0 %collective-permute-done.8.rest_11_ = f32[2,4,8,128]{3,2,1,0:T(8,128)S(1)} collective-permute-done((f32[2,4,8,128]{3,2,1,0:T(8,128)S(1)}, f32[2,4,8,128]{3,2,1,0:T(8,128)S(1)}, u32[]{:S(2)}, u32[]{:S(2)}) %collective-permute-start.8) | collective-permute-done | bytes 32800 | tf_op jit(solution)/shard_map/ppermute | solution.py:241
  41.2 0.4 collective-permute-start.39
  41.6 0.5 collective-permute-start.36
  42.1 0.1 collective-permute-start.38
  42.2 0.1 collective-permute-done.2.rest_3_
  42.3 1.4 %shard_map.78 = (f32[2,4,5,8,128]{4,3,2,1,0:T(8,128)S(1)}, f32[2,4,5,8,128]{4,3,2,1,0:T(8,128)S(1)}, f32[2,4,5,8,128]{4,3,2,1,0:T(8,128)S(1)}, f32[2,4,5,8,128]{4,3,2,1,0:T(8,128)S(1)}) custom-call(s32[3]{0:T(128)S(1)} %pad_add_fusion.me, f32[4,5,32,128]{3,2,1,0:T(8,128)S(1)} %bitcast.26, f32[4,5,32,128]{3,2,1,0:T(8,128)S(1)} %collective-permute-done.rest_1_, ...), custom_call_target="tpu_custom_call" | custom-call | tf_op jit(solution)/shard_map/pallas_call | solution.py:230
  43.7 1.6 %collective-permute-start.14 = (f32[2,4,5,8,128]{4,3,2,1,0:T(8,128)S(1)}, f32[2,4,5,8,128]{4,3,2,1,0:T(8,128)S(1)}, u32[]{:S(2)}, u32[]{:S(2)}) collective-permute-start(f32[2,4,5,8,128]{4,3,2,1,0:T(8,128)S(1)} %get-tuple-element.31), channel_id=1, source_target_pairs={{0,2},{1,3},{2,0},{3,1},{4,6},{5,7},{6,4},{7,5},{8,10},{9,11},{10,... | collective-permute-start | bytes 491528 | tf_op jit(solution)/shard_map/ppermute | solution.py:241
  45.3 3.6 %collective-permute-done.39.rest_6_ = f32[2,4,5,8,128]{4,3,2,1,0:T(8,128)S(1)} collective-permute-done((f32[2,4,5,8,128]{4,3,2,1,0:T(8,128)S(1)}, f32[2,4,5,8,128]{4,3,2,1,0:T(8,128)S(1)}, u32[]{:S(2)}, u32[]{:S(2)}) %collective-permute-start.39) | collective-permute-done | bytes 163872 | tf_op jit(solution)/shard_map/ppermute | solution.py:241
  48.9 0.6 collective-permute-start.16
  49.5 0.9 %collective-permute-start.18 = (f32[2,4,5,8,128]{4,3,2,1,0:T(8,128)S(1)}, f32[2,4,5,8,128]{4,3,2,1,0:T(8,128)S(1)}, u32[]{:S(2)}, u32[]{:S(2)}) collective-permute-start(f32[2,4,5,8,128]{4,3,2,1,0:T(8,128)S(1)} %get-tuple-element.33), channel_id=1, source_target_pairs={{0,6},{1,7},{2,4},{3,5},{4,2},{5,3},{6,0},{7,1},{8,14},{9,15},{10,... | collective-permute-start | bytes 491528 | tf_op jit(solution)/shard_map/ppermute | solution.py:241
  50.4 0.5 collective-permute-done.14.rest_2_
  50.9 0.7 shard_map.82
  51.6 0.8 %collective-permute-start.41 = (f32[6,8,8,128]{3,2,1,0:T(8,128)S(1)}, f32[6,8,8,128]{3,2,1,0:T(8,128)S(1)}, u32[]{:S(2)}, u32[]{:S(2)}) collective-permute-start(f32[6,8,8,128]{3,2,1,0:T(8,128)S(1)} %get-tuple-element.47), channel_id=1, source_target_pairs={{0,8},{8,0},{16,24},{24,16},{1,9},{9,1},{17,25},{25,17},{2,10},{10... | collective-permute-start | bytes 589832 | tf_op jit(solution)/shard_map/ppermute | solution.py:241
  52.4 6.6 %collective-permute-done.16.rest_4_ = f32[2,4,5,8,128]{4,3,2,1,0:T(8,128)S(1)} collective-permute-done((f32[2,4,5,8,128]{4,3,2,1,0:T(8,128)S(1)}, f32[2,4,5,8,128]{4,3,2,1,0:T(8,128)S(1)}, u32[]{:S(2)}, u32[]{:S(2)}) %collective-permute-start.16) | collective-permute-done | bytes 163872 | tf_op jit(solution)/shard_map/ppermute | solution.py:241
  59.0 0.5 collective-permute-start.19
  59.5 2.1 %collective-permute-start.42 = (f32[6,8,8,128]{3,2,1,0:T(8,128)S(1)}, f32[6,8,8,128]{3,2,1,0:T(8,128)S(1)}, u32[]{:S(2)}, u32[]{:S(2)}) collective-permute-start(f32[6,8,8,128]{3,2,1,0:T(8,128)S(1)} %get-tuple-element.48), channel_id=1, source_target_pairs={{0,16},{8,24},{16,0},{24,8},{1,17},{9,25},{17,1},{25,9},{2,18},{10... | collective-permute-start | bytes 589832 | tf_op jit(solution)/shard_map/ppermute | solution.py:241
  61.7 1.5 %collective-permute-start.43 = (f32[6,8,8,128]{3,2,1,0:T(8,128)S(1)}, f32[6,8,8,128]{3,2,1,0:T(8,128)S(1)}, u32[]{:S(2)}, u32[]{:S(2)}) collective-permute-start(f32[6,8,8,128]{3,2,1,0:T(8,128)S(1)} %get-tuple-element.49), channel_id=1, source_target_pairs={{0,24},{8,16},{16,8},{24,0},{1,25},{9,17},{17,9},{25,1},{2,26},{10... | collective-permute-start | bytes 589832 | tf_op jit(solution)/shard_map/ppermute | solution.py:241
  63.1 1.0 %shard_map.79 = (f32[2,5,16,128]{3,2,1,0:T(8,128)S(1)}, f32[2,5,16,128]{3,2,1,0:T(8,128)S(1)}, f32[2,5,16,128]{3,2,1,0:T(8,128)S(1)}, f32[2,5,16,128]{3,2,1,0:T(8,128)S(1)}) custom-call(s32[3]{0:T(128)S(1)} %pad_add_fusion.me, s32[1,128]{1,0:T(1,128)S(1)} %reshape.19.dest, f32[2,4,5,8,128]{4,3,2,1,0:T(8,128)S(1)} %get-tuple-element.30.rest_0_, ...), custom_call_target="tpu_custom_call" | custom-call | tf_op jit(solution)/shard_map/pallas_call | solution.py:230
  64.2 0.1 collective-permute-start.21
  64.2 0.6 collective-permute-start.23
  64.8 2.9 %collective-permute-start.25 = (f32[2,5,16,128]{3,2,1,0:T(8,128)S(1)}, f32[2,5,16,128]{3,2,1,0:T(8,128)S(1)}, u32[]{:S(2)}, u32[]{:S(2)}) collective-permute-start(f32[2,5,16,128]{3,2,1,0:T(8,128)S(1)} %get-tuple-element.37), channel_id=1, source_target_pairs={{0,6},{1,7},{2,4},{3,5},{4,2},{5,3},{6,0},{7,1},{8,14},{9,15},{10,... | collective-permute-start | bytes 245768 | tf_op jit(solution)/shard_map/ppermute | solution.py:241
  67.7 8.9 %collective-permute-done.42.rest_2_ = f32[6,8,8,128]{3,2,1,0:T(8,128)S(1)} collective-permute-done((f32[6,8,8,128]{3,2,1,0:T(8,128)S(1)}, f32[6,8,8,128]{3,2,1,0:T(8,128)S(1)}, u32[]{:S(2)}, u32[]{:S(2)}) %collective-permute-start.42) | collective-permute-done | bytes 196640 | tf_op jit(solution)/shard_map/ppermute | solution.py:241
  76.6 0.5 collective-permute-start.22
  77.1 0.1 collective-permute-start.24
  77.2 0.4 collective-permute-start.26
  77.7 2.0 %shard_map.83 = f32[4,5,32,128]{3,2,1,0:T(8,128)} custom-call(s32[3]{0:T(128)S(1)} %pad_add_fusion.me, s32[4,1,64]{2,1,0:T(1,128)S(1)} %reshape.20.rest_4_.source, f32[6,8,8,128]{3,2,1,0:T(8,128)S(1)} %get-tuple-element.46.rest_0_, f32[6,8,8,128]{3,2,1,0:T(8,128)S(1)} %collective-permute-done.41.rest_1_, ...), custom_call_target="tpu_custom_call" | custom-call | tf_op jit(solution)/shard_map/pallas_call | solution.py:230
  79.7 1.7 %shard_map.80 = f32[640,128]{1,0:T(8,128)} custom-call(s32[3]{0:T(128)S(1)} %pad_add_fusion.me, f32[5,32,32]{2,1,0:T(8,128)S(1)} %bitcast.28, f32[2,5,16,128]{3,2,1,0:T(8,128)S(1)} %get-tuple-element.34.rest_0_, f32[2,5,16,128]{3,2,1,0:T(8,128)S(1)} %collective-permute-done.20.rest_1_, f32[2,5,16,128]{3,2,1,0:T(8,128)S(1)} %collective-permute-done.21.rest_2_, ...), custom_call_target="tpu_custom_call" | custom-call | tf_op jit(solution)/shard_map/pallas_call | solution.py:230
  (48 shorter events, 0.1 us)
Async XLA Ops:
  0.6 9.4 %copy-start.2 = (f32[1,5,32,32]{3,2,1,0:T(8,128)S(1)}, f32[1,5,32,32]{3,2,1,0:T(8,128)}, u32[]{:S(2)}) copy-start(f32[1,5,32,32]{3,2,1,0:T(8,128)} %param.9) | copy-start | bytes 61444
  0.6 28.9 %collective-permute-start.1 = (f32[4,5,32,128]{3,2,1,0:T(8,128)}, f32[4,5,32,128]{3,2,1,0:T(8,128)S(1)}, u32[]{:S(2)}, u32[]{:S(2)}) collective-permute-start(f32[4,5,32,128]{3,2,1,0:T(8,128)} %bitcast.24), channel_id=1, source_target_pairs={{0,16},{8,24},{16,0},{24,8},{1,17},{9,25},{17,1},{25,9},{2,18},{10... | collective-permute-start | bytes 983048 | tf_op jit(solution)/shard_map/ppermute | solution.py:241
  5.5 9.6 %collective-permute-start.3 = (s32[4,1,64]{2,1,0:T(1,128)S(1)}, s32[4,1,64]{2,1,0:T(1,128)S(1)}, u32[]{:S(2)}, u32[]{:S(2)}) collective-permute-start(s32[4,1,64]{2,1,0:T(1,128)S(1)} %reshape.20.rest_4_.source), channel_id=1, source_target_pairs={{0,8},{8,0},{16,24},{24,16},{1,9},{9,1},{17,25},{25,17},{2,10},{10... | collective-permute-start | bytes 3080 | tf_op jit(solution)/shard_map/ppermute | solution.py:241
  7.1 12.7 %collective-permute-start.4 = (s32[4,1,64]{2,1,0:T(1,128)S(1)}, s32[4,1,64]{2,1,0:T(1,128)S(1)}, u32[]{:S(2)}, u32[]{:S(2)}) collective-permute-start(s32[4,1,64]{2,1,0:T(1,128)S(1)} %reshape.20.rest_4_.source), channel_id=1, source_target_pairs={{0,16},{8,24},{16,0},{24,8},{1,17},{9,25},{17,1},{25,9},{2,18},{10... | collective-permute-start | bytes 3080 | tf_op jit(solution)/shard_map/ppermute | solution.py:241
  7.5 14.9 %collective-permute-start.5 = (s32[4,1,64]{2,1,0:T(1,128)S(1)}, s32[4,1,64]{2,1,0:T(1,128)S(1)}, u32[]{:S(2)}, u32[]{:S(2)}) collective-permute-start(s32[4,1,64]{2,1,0:T(1,128)S(1)} %reshape.20.rest_4_.source), channel_id=1, source_target_pairs={{0,24},{8,16},{16,8},{24,0},{1,25},{9,17},{17,9},{25,1},{2,26},{10... | collective-permute-start | bytes 3080 | tf_op jit(solution)/shard_map/ppermute | solution.py:241
  10.0 0.7 copy-start.4
  10.7 1.0 %copy-start = (f32[1,32,4,5,128]{4,2,3,1,0:T(4,128)S(1)}, f32[1,32,4,5,128]{4,2,3,1,0:T(4,128)}, u32[]{:S(2)}) copy-start(f32[1,32,4,5,128]{4,2,3,1,0:T(4,128)} %param.7) | copy-start | bytes 983044
  11.6 0.8 %copy-start.3 = (f32[1,4,32,128]{3,2,1,0:T(8,128)S(1)}, f32[1,4,32,128]{3,2,1,0:T(8,128)}, u32[]{:S(2)}) copy-start(f32[1,4,32,128]{3,2,1,0:T(8,128)} %param.8) | copy-start | bytes 196612
  12.5 12.7 %copy-start.1 = (f32[1,4,32,5,128]{4,2,3,1,0:T(8,128)S(1)}, f32[1,4,32,5,128]{4,2,3,1,0:T(8,128)}, u32[]{:S(2)}) copy-start(f32[1,4,32,5,128]{4,2,3,1,0:T(8,128)} %param.6) | copy-start | bytes 983044
  13.6 8.7 %collective-permute-start.28 = (f32[2,5,16,128]{3,2,1,0:T(8,128)S(1)}, f32[2,5,16,128]{3,2,1,0:T(8,128)S(1)}, u32[]{:S(2)}, u32[]{:S(2)}) collective-permute-start(f32[2,5,16,128]{3,2,1,0:T(8,128)S(1)} %get-tuple-element.39), channel_id=1, source_target_pairs={{0,2},{1,3},{2,0},{3,1},{4,6},{5,7},{6,4},{7,5},{8,10},{9,11},{10,... | collective-permute-start | bytes 245768 | tf_op jit(solution)/shard_map/ppermute | solution.py:241
  15.1 7.7 %collective-permute-start.30 = (f32[2,5,16,128]{3,2,1,0:T(8,128)S(1)}, f32[2,5,16,128]{3,2,1,0:T(8,128)S(1)}, u32[]{:S(2)}, u32[]{:S(2)}) collective-permute-start(f32[2,5,16,128]{3,2,1,0:T(8,128)S(1)} %get-tuple-element.40), channel_id=1, source_target_pairs={{0,4},{1,5},{2,6},{3,7},{4,0},{5,1},{6,2},{7,3},{8,12},{9,13},{10,... | collective-permute-start | bytes 245768 | tf_op jit(solution)/shard_map/ppermute | solution.py:241
  19.8 5.3 %collective-permute-start.32 = (f32[2,5,16,128]{3,2,1,0:T(8,128)S(1)}, f32[2,5,16,128]{3,2,1,0:T(8,128)S(1)}, u32[]{:S(2)}, u32[]{:S(2)}) collective-permute-start(f32[2,5,16,128]{3,2,1,0:T(8,128)S(1)} %get-tuple-element.41), channel_id=1, source_target_pairs={{0,6},{1,7},{2,4},{3,5},{4,2},{5,3},{6,0},{7,1},{8,14},{9,15},{10,... | collective-permute-start | bytes 245768 | tf_op jit(solution)/shard_map/ppermute | solution.py:241
  22.3 2.8 %collective-permute-start.27 = (f32[2,5,16,128]{3,2,1,0:T(8,128)S(1)}, f32[2,5,16,128]{3,2,1,0:T(8,128)S(1)}, u32[]{:S(2)}, u32[]{:S(2)}) collective-permute-start(f32[2,5,16,128]{3,2,1,0:T(8,128)S(1)} %get-tuple-element.38.rest_0_), channel_id=1, source_target_pairs={{0,1},{1,0},{2,3},{3,2},{4,5},{5,4},{6,7},{7,6},{8,9},{9,8},{10,11... | collective-permute-start | bytes 245768 | tf_op jit(solution)/shard_map/ppermute | solution.py:241
  22.3 3.7 %collective-permute-start.29 = (f32[2,5,16,128]{3,2,1,0:T(8,128)S(1)}, f32[2,5,16,128]{3,2,1,0:T(8,128)S(1)}, u32[]{:S(2)}, u32[]{:S(2)}) collective-permute-start(f32[2,5,16,128]{3,2,1,0:T(8,128)S(1)} %collective-permute-done.28.rest_2_), channel_id=1, source_target_pairs={{0,1},{1,0},{2,3},{3,2},{4,5},{5,4},{6,7},{7,6},{8,9},{9,8},{10,11... | collective-permute-start | bytes 245768 | tf_op jit(solution)/shard_map/ppermute | solution.py:241
  22.9 4.7 %collective-permute-start.31 = (f32[2,5,16,128]{3,2,1,0:T(8,128)S(1)}, f32[2,5,16,128]{3,2,1,0:T(8,128)S(1)}, u32[]{:S(2)}, u32[]{:S(2)}) collective-permute-start(f32[2,5,16,128]{3,2,1,0:T(8,128)S(1)} %collective-permute-done.30.rest_4_), channel_id=1, source_target_pairs={{0,1},{1,0},{2,3},{3,2},{4,5},{5,4},{6,7},{7,6},{8,9},{9,8},{10,11... | collective-permute-start | bytes 245768 | tf_op jit(solution)/shard_map/ppermute | solution.py:241
  25.2 3.8 %collective-permute-start.33 = (f32[2,5,16,128]{3,2,1,0:T(8,128)S(1)}, f32[2,5,16,128]{3,2,1,0:T(8,128)S(1)}, u32[]{:S(2)}, u32[]{:S(2)}) collective-permute-start(f32[2,5,16,128]{3,2,1,0:T(8,128)S(1)} %collective-permute-done.32.rest_6_), channel_id=1, source_target_pairs={{0,1},{1,0},{2,3},{3,2},{4,5},{5,4},{6,7},{7,6},{8,9},{9,8},{10,11... | collective-permute-start | bytes 245768 | tf_op jit(solution)/shard_map/ppermute | solution.py:241
  25.2 16.9 %collective-permute-start = (f32[4,5,32,128]{3,2,1,0:T(8,128)S(1)}, f32[4,5,32,128]{3,2,1,0:T(8,128)S(1)}, u32[]{:S(2)}, u32[]{:S(2)}) collective-permute-start(f32[4,5,32,128]{3,2,1,0:T(8,128)S(1)} %bitcast.25), channel_id=1, source_target_pairs={{0,8},{8,0},{16,24},{24,16},{1,9},{9,1},{17,25},{25,17},{2,10},{10... | collective-permute-start | bytes 983048 | tf_op jit(solution)/shard_map/ppermute | solution.py:241
  26.1 7.1 %collective-permute-start.9 = (f32[2,4,8,128]{3,2,1,0:T(8,128)S(1)}, f32[2,4,8,128]{3,2,1,0:T(8,128)S(1)}, u32[]{:S(2)}, u32[]{:S(2)}) collective-permute-start(f32[2,4,8,128]{3,2,1,0:T(8,128)S(1)} %get-tuple-element.28), channel_id=1, source_target_pairs={{0,4},{1,5},{2,6},{3,7},{4,0},{5,1},{6,2},{7,3},{8,12},{9,13},{10,... | collective-permute-start | bytes 98312 | tf_op jit(solution)/shard_map/ppermute | solution.py:241
  27.6 7.2 %collective-permute-start.11 = (f32[2,4,8,128]{3,2,1,0:T(8,128)S(1)}, f32[2,4,8,128]{3,2,1,0:T(8,128)S(1)}, u32[]{:S(2)}, u32[]{:S(2)}) collective-permute-start(f32[2,4,8,128]{3,2,1,0:T(8,128)S(1)} %get-tuple-element.29), channel_id=1, source_target_pairs={{0,6},{1,7},{2,4},{3,5},{4,2},{5,3},{6,0},{7,1},{8,14},{9,15},{10,... | collective-permute-start | bytes 98312 | tf_op jit(solution)/shard_map/ppermute | solution.py:241
  29.0 7.3 %collective-permute-start.7 = (f32[2,4,8,128]{3,2,1,0:T(8,128)S(1)}, f32[2,4,8,128]{3,2,1,0:T(8,128)S(1)}, u32[]{:S(2)}, u32[]{:S(2)}) collective-permute-start(f32[2,4,8,128]{3,2,1,0:T(8,128)S(1)} %get-tuple-element.27), channel_id=1, source_target_pairs={{0,2},{1,3},{2,0},{3,1},{4,6},{5,7},{6,4},{7,5},{8,10},{9,11},{10,... | collective-permute-start | bytes 98312 | tf_op jit(solution)/shard_map/ppermute | solution.py:241
  29.6 12.8 %collective-permute-start.2 = (f32[4,5,32,128]{3,2,1,0:T(8,128)S(1)}, f32[4,5,32,128]{3,2,1,0:T(8,128)S(1)}, u32[]{:S(2)}, u32[]{:S(2)}) collective-permute-start(f32[4,5,32,128]{3,2,1,0:T(8,128)S(1)} %collective-permute-done.1.rest_2_), channel_id=1, source_target_pairs={{0,8},{8,0},{16,24},{24,16},{1,9},{9,1},{17,25},{25,17},{2,10},{10... | collective-permute-start | bytes 983048 | tf_op jit(solution)/shard_map/ppermute | solution.py:241
  33.2 8.4 %collective-permute-start.35 = (f32[2,4,5,8,128]{4,3,2,1,0:T(8,128)S(1)}, f32[2,4,5,8,128]{4,3,2,1,0:T(8,128)S(1)}, u32[]{:S(2)}, u32[]{:S(2)}) collective-permute-start(f32[2,4,5,8,128]{4,3,2,1,0:T(8,128)S(1)} %get-tuple-element.43), channel_id=1, source_target_pairs={{0,2},{1,3},{2,0},{3,1},{4,6},{5,7},{6,4},{7,5},{8,10},{9,11},{10,... | collective-permute-start | bytes 491528 | tf_op jit(solution)/shard_map/ppermute | solution.py:241
  34.8 6.8 %collective-permute-start.37 = (f32[2,4,5,8,128]{4,3,2,1,0:T(8,128)S(1)}, f32[2,4,5,8,128]{4,3,2,1,0:T(8,128)S(1)}, u32[]{:S(2)}, u32[]{:S(2)}) collective-permute-start(f32[2,4,5,8,128]{4,3,2,1,0:T(8,128)S(1)} %get-tuple-element.44), channel_id=1, source_target_pairs={{0,4},{1,5},{2,6},{3,7},{4,0},{5,1},{6,2},{7,3},{8,12},{9,13},{10,... | collective-permute-start | bytes 491528 | tf_op jit(solution)/shard_map/ppermute | solution.py:241
  36.3 1.2 %collective-permute-start.6 = (f32[2,4,8,128]{3,2,1,0:T(8,128)S(1)}, f32[2,4,8,128]{3,2,1,0:T(8,128)S(1)}, u32[]{:S(2)}, u32[]{:S(2)}) collective-permute-start(f32[2,4,8,128]{3,2,1,0:T(8,128)S(1)} %get-tuple-element.26.rest_8_), channel_id=1, source_target_pairs={{0,1},{1,0},{2,3},{3,2},{4,5},{5,4},{6,7},{7,6},{8,9},{9,8},{10,11... | collective-permute-start | bytes 98312 | tf_op jit(solution)/shard_map/ppermute | solution.py:241
  37.5 1.2 %collective-permute-start.10 = (f32[2,4,8,128]{3,2,1,0:T(8,128)S(1)}, f32[2,4,8,128]{3,2,1,0:T(8,128)S(1)}, u32[]{:S(2)}, u32[]{:S(2)}) collective-permute-start(f32[2,4,8,128]{3,2,1,0:T(8,128)S(1)} %collective-permute-done.9.rest_12_), channel_id=1, source_target_pairs={{0,1},{1,0},{2,3},{3,2},{4,5},{5,4},{6,7},{7,6},{8,9},{9,8},{10,11... | collective-permute-start | bytes 98312 | tf_op jit(solution)/shard_map/ppermute | solution.py:241
  38.8 1.2 %collective-permute-start.12 = (f32[2,4,8,128]{3,2,1,0:T(8,128)S(1)}, f32[2,4,8,128]{3,2,1,0:T(8,128)S(1)}, u32[]{:S(2)}, u32[]{:S(2)}) collective-permute-start(f32[2,4,8,128]{3,2,1,0:T(8,128)S(1)} %collective-permute-done.11.rest_14_), channel_id=1, source_target_pairs={{0,1},{1,0},{2,3},{3,2},{4,5},{5,4},{6,7},{7,6},{8,9},{9,8},{10,11... | collective-permute-start | bytes 98312 | tf_op jit(solution)/shard_map/ppermute | solution.py:241
  40.0 1.2 %collective-permute-start.8 = (f32[2,4,8,128]{3,2,1,0:T(8,128)S(1)}, f32[2,4,8,128]{3,2,1,0:T(8,128)S(1)}, u32[]{:S(2)}, u32[]{:S(2)}) collective-permute-start(f32[2,4,8,128]{3,2,1,0:T(8,128)S(1)} %collective-permute-done.7.rest_10_), channel_id=1, source_target_pairs={{0,1},{1,0},{2,3},{3,2},{4,5},{5,4},{6,7},{7,6},{8,9},{9,8},{10,11... | collective-permute-start | bytes 98312 | tf_op jit(solution)/shard_map/ppermute | solution.py:241
  41.2 7.7 %collective-permute-start.39 = (f32[2,4,5,8,128]{4,3,2,1,0:T(8,128)S(1)}, f32[2,4,5,8,128]{4,3,2,1,0:T(8,128)S(1)}, u32[]{:S(2)}, u32[]{:S(2)}) collective-permute-start(f32[2,4,5,8,128]{4,3,2,1,0:T(8,128)S(1)} %get-tuple-element.45), channel_id=1, source_target_pairs={{0,6},{1,7},{2,4},{3,5},{4,2},{5,3},{6,0},{7,1},{8,14},{9,15},{10,... | collective-permute-start | bytes 491528 | tf_op jit(solution)/shard_map/ppermute | solution.py:241
  41.6 7.3 %collective-permute-start.34 = (f32[2,4,5,8,128]{4,3,2,1,0:T(8,128)S(1)}, f32[2,4,5,8,128]{4,3,2,1,0:T(8,128)S(1)}, u32[]{:S(2)}, u32[]{:S(2)}) collective-permute-start(f32[2,4,5,8,128]{4,3,2,1,0:T(8,128)S(1)} %get-tuple-element.42.rest_0_), channel_id=1, source_target_pairs={{0,1},{1,0},{2,3},{3,2},{4,5},{5,4},{6,7},{7,6},{8,9},{9,8},{10,11... | collective-permute-start | bytes 491528 | tf_op jit(solution)/shard_map/ppermute | solution.py:241
  41.6 7.9 %collective-permute-start.36 = (f32[2,4,5,8,128]{4,3,2,1,0:T(8,128)S(1)}, f32[2,4,5,8,128]{4,3,2,1,0:T(8,128)S(1)}, u32[]{:S(2)}, u32[]{:S(2)}) collective-permute-start(f32[2,4,5,8,128]{4,3,2,1,0:T(8,128)S(1)} %collective-permute-done.35.rest_2_), channel_id=1, source_target_pairs={{0,1},{1,0},{2,3},{3,2},{4,5},{5,4},{6,7},{7,6},{8,9},{9,8},{10,11... | collective-permute-start | bytes 491528 | tf_op jit(solution)/shard_map/ppermute | solution.py:241
  42.1 8.2 %collective-permute-start.38 = (f32[2,4,5,8,128]{4,3,2,1,0:T(8,128)S(1)}, f32[2,4,5,8,128]{4,3,2,1,0:T(8,128)S(1)}, u32[]{:S(2)}, u32[]{:S(2)}) collective-permute-start(f32[2,4,5,8,128]{4,3,2,1,0:T(8,128)S(1)} %collective-permute-done.37.rest_4_), channel_id=1, source_target_pairs={{0,1},{1,0},{2,3},{3,2},{4,5},{5,4},{6,7},{7,6},{8,9},{9,8},{10,11... | collective-permute-start | bytes 491528 | tf_op jit(solution)/shard_map/ppermute | solution.py:241
  43.7 7.2 %collective-permute-start.14 = (f32[2,4,5,8,128]{4,3,2,1,0:T(8,128)S(1)}, f32[2,4,5,8,128]{4,3,2,1,0:T(8,128)S(1)}, u32[]{:S(2)}, u32[]{:S(2)}) collective-permute-start(f32[2,4,5,8,128]{4,3,2,1,0:T(8,128)S(1)} %get-tuple-element.31), channel_id=1, source_target_pairs={{0,2},{1,3},{2,0},{3,1},{4,6},{5,7},{6,4},{7,5},{8,10},{9,11},{10,... | collective-permute-start | bytes 491528 | tf_op jit(solution)/shard_map/ppermute | solution.py:241
  48.9 2.0 %collective-permute-start.40 = (f32[2,4,5,8,128]{4,3,2,1,0:T(8,128)S(1)}, f32[2,4,5,8,128]{4,3,2,1,0:T(8,128)S(1)}, u32[]{:S(2)}, u32[]{:S(2)}) collective-permute-start(f32[2,4,5,8,128]{4,3,2,1,0:T(8,128)S(1)} %collective-permute-done.39.rest_6_), channel_id=1, source_target_pairs={{0,1},{1,0},{2,3},{3,2},{4,5},{5,4},{6,7},{7,6},{8,9},{9,8},{10,11... | collective-permute-start | bytes 491528 | tf_op jit(solution)/shard_map/ppermute | solution.py:241
  48.9 10.1 %collective-permute-start.16 = (f32[2,4,5,8,128]{4,3,2,1,0:T(8,128)S(1)}, f32[2,4,5,8,128]{4,3,2,1,0:T(8,128)S(1)}, u32[]{:S(2)}, u32[]{:S(2)}) collective-permute-start(f32[2,4,5,8,128]{4,3,2,1,0:T(8,128)S(1)} %get-tuple-element.32), channel_id=1, source_target_pairs={{0,4},{1,5},{2,6},{3,7},{4,0},{5,1},{6,2},{7,3},{8,12},{9,13},{10,... | collective-permute-start | bytes 491528 | tf_op jit(solution)/shard_map/ppermute | solution.py:241
  49.5 9.6 %collective-permute-start.18 = (f32[2,4,5,8,128]{4,3,2,1,0:T(8,128)S(1)}, f32[2,4,5,8,128]{4,3,2,1,0:T(8,128)S(1)}, u32[]{:S(2)}, u32[]{:S(2)}) collective-permute-start(f32[2,4,5,8,128]{4,3,2,1,0:T(8,128)S(1)} %get-tuple-element.33), channel_id=1, source_target_pairs={{0,6},{1,7},{2,4},{3,5},{4,2},{5,3},{6,0},{7,1},{8,14},{9,15},{10,... | collective-permute-start | bytes 491528 | tf_op jit(solution)/shard_map/ppermute | solution.py:241
  50.4 9.2 %collective-permute-start.13 = (f32[2,4,5,8,128]{4,3,2,1,0:T(8,128)S(1)}, f32[2,4,5,8,128]{4,3,2,1,0:T(8,128)S(1)}, u32[]{:S(2)}, u32[]{:S(2)}) collective-permute-start(f32[2,4,5,8,128]{4,3,2,1,0:T(8,128)S(1)} %get-tuple-element.30.rest_0_), channel_id=1, source_target_pairs={{0,1},{1,0},{2,3},{3,2},{4,5},{5,4},{6,7},{7,6},{8,9},{9,8},{10,11... | collective-permute-start | bytes 491528 | tf_op jit(solution)/shard_map/ppermute | solution.py:241
  50.9 10.8 %collective-permute-start.15 = (f32[2,4,5,8,128]{4,3,2,1,0:T(8,128)S(1)}, f32[2,4,5,8,128]{4,3,2,1,0:T(8,128)S(1)}, u32[]{:S(2)}, u32[]{:S(2)}) collective-permute-start(f32[2,4,5,8,128]{4,3,2,1,0:T(8,128)S(1)} %collective-permute-done.14.rest_2_), channel_id=1, source_target_pairs={{0,1},{1,0},{2,3},{3,2},{4,5},{5,4},{6,7},{7,6},{8,9},{9,8},{10,11... | collective-permute-start | bytes 491528 | tf_op jit(solution)/shard_map/ppermute | solution.py:241
  51.6 13.2 %collective-permute-start.41 = (f32[6,8,8,128]{3,2,1,0:T(8,128)S(1)}, f32[6,8,8,128]{3,2,1,0:T(8,128)S(1)}, u32[]{:S(2)}, u32[]{:S(2)}) collective-permute-start(f32[6,8,8,128]{3,2,1,0:T(8,128)S(1)} %get-tuple-element.47), channel_id=1, source_target_pairs={{0,8},{8,0},{16,24},{24,16},{1,9},{9,1},{17,25},{25,17},{2,10},{10... | collective-permute-start | bytes 589832 | tf_op jit(solution)/shard_map/ppermute | solution.py:241
  59.0 4.1 %collective-permute-start.17 = (f32[2,4,5,8,128]{4,3,2,1,0:T(8,128)S(1)}, f32[2,4,5,8,128]{4,3,2,1,0:T(8,128)S(1)}, u32[]{:S(2)}, u32[]{:S(2)}) collective-permute-start(f32[2,4,5,8,128]{4,3,2,1,0:T(8,128)S(1)} %collective-permute-done.16.rest_4_), channel_id=1, source_target_pairs={{0,1},{1,0},{2,3},{3,2},{4,5},{5,4},{6,7},{7,6},{8,9},{9,8},{10,11... | collective-permute-start | bytes 491528 | tf_op jit(solution)/shard_map/ppermute | solution.py:241
  59.0 4.1 %collective-permute-start.19 = (f32[2,4,5,8,128]{4,3,2,1,0:T(8,128)S(1)}, f32[2,4,5,8,128]{4,3,2,1,0:T(8,128)S(1)}, u32[]{:S(2)}, u32[]{:S(2)}) collective-permute-start(f32[2,4,5,8,128]{4,3,2,1,0:T(8,128)S(1)} %collective-permute-done.18.rest_6_), channel_id=1, source_target_pairs={{0,1},{1,0},{2,3},{3,2},{4,5},{5,4},{6,7},{7,6},{8,9},{9,8},{10,11... | collective-permute-start | bytes 491528 | tf_op jit(solution)/shard_map/ppermute | solution.py:241
  59.5 17.1 %collective-permute-start.42 = (f32[6,8,8,128]{3,2,1,0:T(8,128)S(1)}, f32[6,8,8,128]{3,2,1,0:T(8,128)S(1)}, u32[]{:S(2)}, u32[]{:S(2)}) collective-permute-start(f32[6,8,8,128]{3,2,1,0:T(8,128)S(1)} %get-tuple-element.48), channel_id=1, source_target_pairs={{0,16},{8,24},{16,0},{24,8},{1,17},{9,25},{17,1},{25,9},{2,18},{10... | collective-permute-start | bytes 589832 | tf_op jit(solution)/shard_map/ppermute | solution.py:241
  61.7 16.0 %collective-permute-start.43 = (f32[6,8,8,128]{3,2,1,0:T(8,128)S(1)}, f32[6,8,8,128]{3,2,1,0:T(8,128)S(1)}, u32[]{:S(2)}, u32[]{:S(2)}) collective-permute-start(f32[6,8,8,128]{3,2,1,0:T(8,128)S(1)} %get-tuple-element.49), channel_id=1, source_target_pairs={{0,24},{8,16},{16,8},{24,0},{1,25},{9,17},{17,9},{25,1},{2,26},{10... | collective-permute-start | bytes 589832 | tf_op jit(solution)/shard_map/ppermute | solution.py:241
  64.2 12.5 %collective-permute-start.21 = (f32[2,5,16,128]{3,2,1,0:T(8,128)S(1)}, f32[2,5,16,128]{3,2,1,0:T(8,128)S(1)}, u32[]{:S(2)}, u32[]{:S(2)}) collective-permute-start(f32[2,5,16,128]{3,2,1,0:T(8,128)S(1)} %get-tuple-element.35), channel_id=1, source_target_pairs={{0,2},{1,3},{2,0},{3,1},{4,6},{5,7},{6,4},{7,5},{8,10},{9,11},{10,... | collective-permute-start | bytes 245768 | tf_op jit(solution)/shard_map/ppermute | solution.py:241
  64.2 12.9 %collective-permute-start.23 = (f32[2,5,16,128]{3,2,1,0:T(8,128)S(1)}, f32[2,5,16,128]{3,2,1,0:T(8,128)S(1)}, u32[]{:S(2)}, u32[]{:S(2)}) collective-permute-start(f32[2,5,16,128]{3,2,1,0:T(8,128)S(1)} %get-tuple-element.36), channel_id=1, source_target_pairs={{0,4},{1,5},{2,6},{3,7},{4,0},{5,1},{6,2},{7,3},{8,12},{9,13},{10,... | collective-permute-start | bytes 245768 | tf_op jit(solution)/shard_map/ppermute | solution.py:241
  64.8 12.4 %collective-permute-start.25 = (f32[2,5,16,128]{3,2,1,0:T(8,128)S(1)}, f32[2,5,16,128]{3,2,1,0:T(8,128)S(1)}, u32[]{:S(2)}, u32[]{:S(2)}) collective-permute-start(f32[2,5,16,128]{3,2,1,0:T(8,128)S(1)} %get-tuple-element.37), channel_id=1, source_target_pairs={{0,6},{1,7},{2,4},{3,5},{4,2},{5,3},{6,0},{7,1},{8,14},{9,15},{10,... | collective-permute-start | bytes 245768 | tf_op jit(solution)/shard_map/ppermute | solution.py:241
  76.6 3.0 %collective-permute-start.20 = (f32[2,5,16,128]{3,2,1,0:T(8,128)S(1)}, f32[2,5,16,128]{3,2,1,0:T(8,128)S(1)}, u32[]{:S(2)}, u32[]{:S(2)}) collective-permute-start(f32[2,5,16,128]{3,2,1,0:T(8,128)S(1)} %get-tuple-element.34.rest_0_), channel_id=1, source_target_pairs={{0,1},{1,0},{2,3},{3,2},{4,5},{5,4},{6,7},{7,6},{8,9},{9,8},{10,11... | collective-permute-start | bytes 245768 | tf_op jit(solution)/shard_map/ppermute | solution.py:241
  76.6 3.0 %collective-permute-start.22 = (f32[2,5,16,128]{3,2,1,0:T(8,128)S(1)}, f32[2,5,16,128]{3,2,1,0:T(8,128)S(1)}, u32[]{:S(2)}, u32[]{:S(2)}) collective-permute-start(f32[2,5,16,128]{3,2,1,0:T(8,128)S(1)} %collective-permute-done.21.rest_2_), channel_id=1, source_target_pairs={{0,1},{1,0},{2,3},{3,2},{4,5},{5,4},{6,7},{7,6},{8,9},{9,8},{10,11... | collective-permute-start | bytes 245768 | tf_op jit(solution)/shard_map/ppermute | solution.py:241
  77.1 2.5 %collective-permute-start.24 = (f32[2,5,16,128]{3,2,1,0:T(8,128)S(1)}, f32[2,5,16,128]{3,2,1,0:T(8,128)S(1)}, u32[]{:S(2)}, u32[]{:S(2)}) collective-permute-start(f32[2,5,16,128]{3,2,1,0:T(8,128)S(1)} %collective-permute-done.23.rest_4_), channel_id=1, source_target_pairs={{0,1},{1,0},{2,3},{3,2},{4,5},{5,4},{6,7},{7,6},{8,9},{9,8},{10,11... | collective-permute-start | bytes 245768 | tf_op jit(solution)/shard_map/ppermute | solution.py:241
  77.2 2.5 %collective-permute-start.26 = (f32[2,5,16,128]{3,2,1,0:T(8,128)S(1)}, f32[2,5,16,128]{3,2,1,0:T(8,128)S(1)}, u32[]{:S(2)}, u32[]{:S(2)}) collective-permute-start(f32[2,5,16,128]{3,2,1,0:T(8,128)S(1)} %collective-permute-done.25.rest_6_), channel_id=1, source_target_pairs={{0,1},{1,0},{2,3},{3,2},{4,5},{5,4},{6,7},{7,6},{8,9},{9,8},{10,11... | collective-permute-start | bytes 245768 | tf_op jit(solution)/shard_map/ppermute | solution.py:241

commit v2 on v0

v2 whole, which is shorter than its diff:
```python
import functools

import jax
import jax.numpy as jnp
from jax import lax
from jax.experimental import pallas as pl
from jax.experimental.pallas import tpu as pltpu
from jax.sharding import PartitionSpec as P

LANES = 128
F32 = jnp.float32
EXACT = functools.partial(lax.dot_general, precision=lax.Precision.HIGHEST, preferred_element_type=F32)
SHORT = functools.partial(lax.dot_general, preferred_element_type=F32)


def two_parts(values):
    high = values.astype(jnp.bfloat16)
    return high, (values - high.astype(F32)).astype(jnp.bfloat16)


def pick(table, values, contract):
    dims = ((contract, (0,)), ((), ()))
    high, low = two_parts(values)
    return SHORT(table, low, dims) + SHORT(table, high, dims)


def product(left, right, contract):
    dims = ((contract, (0,)), ((), ()))
    left_high, left_low = two_parts(left)
    right_high, right_low = two_parts(right)
    return (
        SHORT(left_low, right_high, dims)
        + SHORT(left_high, right_low, dims)
        + SHORT(left_high, right_high, dims)
    )


def hot(rows, wanted):
    return jnp.where(rows == wanted, 1.0, 0.0).astype(jnp.bfloat16)


def iota(shape, axis):
    return lax.broadcasted_iota(jnp.int32, shape, axis)


def xor(a, b):
    return jnp.bitwise_xor(a, b)


def pack_kernel(dims, me, state, source, out):
    lats, slabs, chips, cap, lev_dev, here, fields = dims
    total = state.shape[0]
    out[:total, :] = state[...]
    slots = slabs * cap
    spread = jnp.where(iota((cap, slots), 1) % cap == iota((cap, slots), 0), 1.0, 0.0)
    wide = EXACT(source[...].reshape(lats * slabs, cap).astype(F32), spread, (((1,), (0,)), ((), ())))
    mine = iota((slabs, slots), 1) // cap == iota((slabs, slots), 0)
    out[total:, :] = jnp.zeros((out.shape[0] - total, LANES), F32)
    for g in range(lats):
        row = jnp.where(mine, wide[g * slabs : (g + 1) * slabs], 0.0)
        out[total + g : total + g + 1, :slots] = jnp.sum(row, axis=0, keepdims=True)


def start_kernel(dims, me, cot, inverse, cot_pair, *rest):
    lats, slabs, chips, cap, lev_dev, here, fields = dims
    out, back = rest[:chips], rest[-1]
    chip, core = me[1], me[2]
    levels = slabs * lev_dev
    step = fields * here
    span = 2 * lev_dev * 2 * here
    for f in range(fields):
        own = [cot[pl.ds(f * here + b, levels, stride=step), :] for b in range(here)]
        pair = [cot_pair[pl.ds(f * here + b, levels, stride=step), :] for b in range(here)]
        own, pair = jnp.concatenate(own, axis=1), jnp.concatenate(pair, axis=1)
        wide = jnp.concatenate(
            [jnp.where(core == 0, own, pair), jnp.where(core == 0, pair, own)], axis=1
        )
        res = product(inverse[f], wide, (0,))
        for b in range(2 * here):
            back[f, pl.ds(b, levels, stride=2 * here), :] = res[:, b * LANES : (b + 1) * LANES]
    for k in range(chips):
        first = pl.multiple_of(xor(chip, k) * span, span)
        for f in range(fields):
            out[k][f] = back[f, pl.ds(first, span), :].reshape(2, span // 2, LANES)


def by_column_owner(dest, lev_dev, chips, wide):
    total = dest.shape[1]
    at = iota((total, total), 1)
    span = lev_dev * wide
    chip = at // span
    level = (at - chip * span) // wide
    block = at - chip * span - level * wide
    order = jnp.where(iota((total, total), 0) == (level * chips + chip) * wide + block, 1.0, 0.0)
    return EXACT(dest.astype(F32), order, (((1,), (0,)), ((), ()))).astype(jnp.int32)


def slot_table(dims, core, dest, by_chip):
    lats, slabs, chips, cap, lev_dev, here, fields = dims
    shape = (chips * lats * cap, dest.shape[1])
    at = iota(shape, 0)
    if by_chip:
        chip = at // (lats * cap)
        lat = at // cap - chip * lats
    else:
        lat = at // (chips * cap)
        chip = at // cap - lat * chips
    slot = at - at // cap * cap
    return hot(lat * (slabs * cap) + (chip * 2 + core) * cap + slot, dest)


def back_kernel(dims, me, dest, dest_pair, weight, weight_pair, *rest):
    lats, slabs, chips, cap, lev_dev, here, fields = dims
    got, out, dest_out = rest[:chips], rest[-chips - 3 : -3], rest[-3]
    rows, slots = rest[-2:]
    chip, core = me[1], me[2]
    wide = 2 * here
    span = lev_dev * wide
    both = by_column_owner(jnp.concatenate([dest[...], dest_pair[...]], axis=0), lev_dev, chips, wide)
    dest_out[...] = both
    for x, w in enumerate((weight, weight_pair)):
        r = xor(core, x)
        for k in range(chips):
            first = pl.multiple_of(xor(chip, k) * span, span)
            for f in range(fields):
                rows[x, pl.ds(first, span), f * LANES : (f + 1) * LANES] = got[k][f, r]
        for c in range(chips):
            for l in range(lev_dev):
                at = l * chips * wide + c * wide
                rows[x, c * span + l * wide : c * span + (l + 1) * wide, fields * LANES :] = w[at : at + wide]
        res = pick(slot_table(dims, core, both[x : x + 1], True), rows[x], (1,))
        for c in range(chips):
            for g in range(lats):
                at = (c * lats + g) * cap
                for f in range(fields + 1):
                    slots[c, g, f] = res[at : at + cap, f * LANES : (f + 1) * LANES]
        for k in range(chips):
            out[k][x] = slots[xor(chip, k)]


def sort_kernel(groups, dims, me, *rest):
    lats, slabs, chips, cap, lev_dev, here, fields = dims
    got, outs = rest[:chips], rest[-len(groups) :]
    lat, chip, core = me[0], me[1], me[2]
    for out, j in zip(outs, groups):
        other = xor(lat, j)
        for k in range(chips):
            for x in range(2):
                src = xor(chip, k) * 2 + xor(core, x)
                for f in range(fields + 1):
                    out[f, src] = got[k][x, other, f]


def add_kernel(dims, me, packed, *rest):
    lats, slabs, chips, cap, lev_dev, here, fields = dims
    got, out = rest[:lats], rest[-1]
    blocks = slabs * here
    row_total = lev_dev * blocks
    slots = slabs * cap
    lat = me[0]
    row = iota((row_total, slots), 0)
    tables, values = [], []
    for j in range(lats):
        at = fields * row_total + xor(lat, j)
        low = packed[pl.ds(at, 1), :][:, :slots].astype(jnp.int32)
        scale = jnp.concatenate([got[j][fields].reshape(slots, LANES)] * fields, axis=1)
        value = jnp.concatenate([got[j][f].reshape(slots, LANES) for f in range(fields)], axis=1)
        values += [(1.0 - scale) * value, scale * value]
        tables += [hot(row, low), hot(row, low + blocks)]
    total = pick(jnp.concatenate(tables, axis=1), jnp.concatenate(values, axis=0), (1,))
    for l in range(lev_dev):
        for f in range(fields):
            out[l, f] = total[l * blocks : (l + 1) * blocks, f * LANES : (f + 1) * LANES]


def hold_kernel(dims, me, array, *rest):
    out, sem = rest[-2:]
    copy = pltpu.make_async_copy(array, out, sem)
    copy.start()
    copy.wait()


def mix_kernel(dims, me, *rest):
    lats, slabs, chips, cap, lev_dev, here, fields = dims
    got, packed = rest[:chips], rest[chips : chips + lats]
    out, weight, mixed = rest[-chips - 2 : -2], rest[-2], rest[-1]
    lat, chip, core = me[0], me[1], me[2]
    blocks = slabs * here
    row_total = lev_dev * blocks
    slots = slabs * cap
    for k in range(chips):
        for x in range(2):
            src = xor(chip, k) * 2 + xor(core, x)
            for g in range(lats):
                weight[g, src] = got[k][x, g, fields]
    row = iota((row_total, slots), 0)
    for j in range(lats):
        sender = xor(lat, j)
        low = packed[j][pl.ds(fields * row_total + lat, 1), :][:, :slots].astype(jnp.int32)
        values = jnp.concatenate(
            [
                jnp.concatenate(
                    [packed[j][(l * fields + f) * blocks : (l * fields + f + 1) * blocks] for l in range(lev_dev)],
                    axis=0,
                )
                for f in range(fields)
            ],
            axis=1,
        )
        table = jnp.concatenate([hot(row, low), hot(row, low + blocks)], axis=1)
        both = pick(table, values, (0,))
        scale = jnp.concatenate([weight[sender].reshape(slots, LANES)] * fields, axis=1)
        res = (1.0 - scale) * both[:slots] + scale * both[slots:]
        for s in range(slabs):
            for f in range(fields):
                mixed[s, f] = res[s * cap : (s + 1) * cap, f * LANES : (f + 1) * LANES]
        for k in range(chips):
            for x in range(2):
                out[k][x, sender] = mixed[xor(chip, k) * 2 + xor(core, x)]


def arrive_kernel(dims, me, dest, *rest):
    lats, slabs, chips, cap, lev_dev, here, fields = dims
    got, out = rest[:chips], rest[-chips - 2 : -2]
    rows, moved = rest[-2:]
    chip, core = me[1], me[2]
    span = lev_dev * 2 * here
    for x in range(2):
        for k in range(chips):
            for g in range(lats):
                for f in range(fields):
                    rows[f, g * chips + xor(chip, k)] = got[k][x, g, f]
        values = jnp.concatenate(
            [rows[f].reshape(lats * chips * cap, LANES) for f in range(fields)], axis=1
        )
        res = pick(slot_table(dims, core, dest[x : x + 1, :], False), values, (0,))
        for c in range(chips):
            for f in range(fields):
                moved[c, f] = res[c * span : (c + 1) * span, f * LANES : (f + 1) * LANES]
        for k in range(chips):
            for f in range(fields):
                out[k][f, xor(core, x)] = moved[xor(chip, k), f]


def diffuse_kernel(dims, me, inverse, *rest):
    lats, slabs, chips, cap, lev_dev, here, fields = dims
    got, own, pair, rows = rest[:chips], rest[-3], rest[-2], rest[-1]
    chip, core = me[1], me[2]
    wide = 2 * here
    span = 2 * lev_dev * wide
    levels = slabs * lev_dev
    for k in range(chips):
        first = pl.multiple_of(xor(chip, k) * span, span)
        for f in range(fields):
            rows[f, pl.ds(first, span), :] = got[k][f].reshape(span, LANES)
    for f in range(fields):
        values = jnp.concatenate([rows[f, pl.ds(b, levels, stride=wide), :] for b in range(wide)], axis=1)
        res = product(inverse[f], values, (1,))
        first, second = res[:, : here * LANES], res[:, here * LANES :]
        mine, other = jnp.where(core == 0, first, second), jnp.where(core == 0, second, first)
        for b in range(here):
            at = pl.ds(f * here + b, levels, stride=fields * here)
            own[at, :] = mine[:, b * LANES : (b + 1) * LANES]
            pair[at, :] = other[:, b * LANES : (b + 1) * LANES]


def call(kernel, dims, args, outs, scratch=(), after=(), outside=()):
    inside = pl.BlockSpec(memory_space=pltpu.VMEM)
    anywhere = pl.BlockSpec(memory_space=pl.ANY)
    specs = [pl.BlockSpec(memory_space=pltpu.SMEM)]
    specs += [anywhere if i in outside else inside for i in range(1, len(args))]
    return pl.pallas_call(
        functools.partial(kernel, dims),
        out_shape=[shape if hasattr(shape, "dtype") else jax.ShapeDtypeStruct(shape, F32) for shape in outs],
        in_specs=specs + [anywhere] * len(after),
        out_specs=[inside] * len(outs),
        scratch_shapes=[pltpu.VMEM(shape, F32) if isinstance(shape, tuple) else shape for shape in scratch],
        compiler_params=pltpu.CompilerParams(vmem_limit_bytes=48 * 1024 * 1024),
    )(*args, *after)


def swap(array, axis, bit, count):
    return lax.ppermute(array, axis, [(i, i ^ bit) for i in range(count)])


def body(lats, slabs, field_state, cotangent, vertical_weight, diffusion_inverse, source_row, dest_slot):
    _, lev_dev, blocks, fields, width = field_state.shape
    cap = source_row.shape[-1]
    chips = slabs // 2
    here = blocks // slabs
    levels = slabs * lev_dev
    row_total = lev_dev * blocks
    span = lev_dev * 2 * here
    dims = (lats, slabs, chips, cap, lev_dev, here, fields)
    lat, slab = lax.axis_index("lat"), lax.axis_index("slab")
    me = jnp.stack([lat, slab // 2, slab % 2]).astype(jnp.int32)

    def pair(array):
        return swap(array, "slab", 1, slabs)

    def over_chips(messages):
        return [m if k == 0 else swap(m, "slab", 2 * k, slabs) for k, m in enumerate(messages)]

    state = field_state[0].transpose(0, 2, 1, 3).reshape(row_total * fields, width)
    cot = cotangent[0].transpose(0, 2, 1, 3).reshape(levels * fields * here, width)
    weights = vertical_weight.reshape(row_total, width)
    inverse = diffusion_inverse[0]
    dest = dest_slot[0]

    (packed,) = call(
        pack_kernel,
        dims,
        (me, state, source_row[0, 0]),
        [(row_total * fields + -(-lats // 8) * 8, width)],
    )
    near, far = swap(packed, "lat", 1, lats), swap(packed, "lat", 2, lats)
    first = call(
        start_kernel,
        dims,
        (me, cot, inverse, pair(cot)),
        [(fields, 2, span, width)] * chips,
        [(fields, levels * 2 * here, width)],
    )
    *slot_back, dests = call(
        back_kernel,
        dims,
        (me, dest, pair(dest), weights, pair(weights), *over_chips(first)),
        [(2, lats, fields + 1, cap, width)] * chips + [jax.ShapeDtypeStruct((2, row_total), jnp.int32)],
        [(2, row_total, (fields + 1) * width), (chips, lats, fields + 1, cap, width)],
    )
    slot_back = over_chips(slot_back)
    (far,) = call(
        hold_kernel, dims, (me, far), [packed.shape], [pltpu.SemaphoreType.DMA(())], after=[dests, near]
    )
    states = [packed, near]
    for j in range(2, lats):
        if j % 2 == 0:
            states.append(far if j == 2 else swap(packed, "lat", j, lats))
        else:
            states.append(swap(states[j - 1], "lat", 1, lats))
    soon = [j for j in range(lats) if j == 2]
    late = [j for j in range(lats) if j != 2]
    message = (fields + 1, slabs, cap, width)
    sorted_soon = call(functools.partial(sort_kernel, soon), dims, (me, *slot_back), [message] * len(soon))
    mixed = call(
        mix_kernel,
        dims,
        (me, *slot_back, *states),
        [(2, lats, fields, cap, width)] * chips,
        [(lats, slabs, cap, width), (slabs, fields, cap, width)],
        after=sorted_soon,
    )
    sorted_late = call(
        functools.partial(sort_kernel, late), dims, (me, *slot_back), [message] * len(late), after=mixed[:1]
    )
    returned = [None] * lats
    for j, sorted_back in zip(soon + late, [*sorted_soon, *sorted_late]):
        returned[j] = sorted_back if j == 0 else swap(sorted_back, "lat", j, lats)
    moved = call(
        arrive_kernel,
        dims,
        (me, dests, *over_chips(mixed)),
        [(fields, 2, span, width)] * chips,
        [(fields, lats * chips, cap, width), (chips, fields, span, width)],
        after=returned[2:3],
    )
    tangent, tangent_pair = call(
        diffuse_kernel,
        dims,
        (me, inverse, *over_chips(moved)),
        [cot.shape, cot.shape],
        [(fields, levels * 2 * here, width)],
        after=returned[1:2] + returned[3:],
    )
    (adjoint,) = call(
        add_kernel,
        dims,
        (me, packed, *returned),
        [(lev_dev, fields, blocks, width)],
        after=[tangent_pair],
    )
    tangent = tangent + pair(tangent_pair)
    tangent_out = tangent.reshape(1, levels, fields, here, width).transpose(0, 1, 3, 2, 4)
    adjoint_out = adjoint.transpose(0, 2, 1, 3)[None]
    return tangent_out, adjoint_out


def solution(mesh):
    placed = (
        P("lat", "slab", None, None, None),
        P("lat", None, "slab", None, None),
        P("lat", "slab", None, None),
        P("lat", None, None, None),
        P("lat", "slab", None, None, None),
        P("lat", "slab", None),
    )
    return jax.shard_map(
        functools.partial(body, mesh.shape["lat"], mesh.shape["slab"]),
        mesh=mesh,
        in_specs=placed,
        out_specs=(P("lat", None, "slab", None, None), P("lat", "slab", None, None, None)),
        check_vma=False,
    )
```

time: 144 us -> 65.7 us (0.46)
  waiting for transfers between devices: 96.7 us -> 24.5 us
  local copies, waits for them, and re-layouts: 13.2 us -> 2.28 us
  Pallas kernels: 0 us -> 9.68 us
  matrix products: 7.04 us -> 0 us
  starting transfers between devices: 24.3 us -> 27.4 us
    all_to_all x6 -> x0, waiting for transfers between devices: 96.7 us -> none  [the longest x1 29.6 us: body(): lax.all_to_all(slot_back.reshape(lower_idx.shape + (2, fields, width)), '...]
    ppermute x0 -> x22, starting transfers between devices: none -> 27.4 us  [swap(): return lax.ppermute(array, axis, [(i, i ^ bit) for i in range(count)])]
    ppermute x0 -> x22, waiting for transfers between devices: none -> 24.5 us  [swap(): return lax.ppermute(array, axis, [(i, i ^ bit) for i in range(count)])]
    all_to_all x6 -> x0, starting transfers between devices: 24.3 us -> none  [the longest x1 5.17 us: body(): back = lax.all_to_all(back, 'slab', split_axis=1, concat_axis=2, tiled=True)]
    pallas_call x0 -> x10, Pallas kernels: none -> 9.68 us  [call(): pl.pallas_call(functools.partial(kernel, dims), out_shape=[shape if hasat...]
    dot_general x6 -> x0, matrix products: 7.04 us -> none  [the longest x2 2.68 us: select(): jnp.dot(table, values, precision=lax.Precision.HIGHEST, preferred_element...]
    all_to_all x6 -> x0, local copies, waits for them, and re-layouts: 5.13 us -> none  [the longest x1 2.49 us: body(): lax.all_to_all(slot_back.reshape(lower_idx.shape + (2, fields, width)), '...]
    unnamed x15 -> x12, local copies, waits for them, and re-layouts: 4.4 us -> 2.28 us
  transfers between devices with their start and end apart: 6 -> 22, of which waited for: 6 -> 8; matrix products, arithmetic and copies ran while one was open for 11% -> 0% of each run, Pallas kernels for 0% -> 12%
where the time goes in v2:
time: 65.7 us; the launch traced here: 65.4 us
  starting transfers between devices  27.4 us (42%)
  waiting for transfers between devices  24.5 us (37%)
  Pallas kernels  9.68 us (15%)
  local copies, waits for them, and re-layouts  2.28 us (3%)
  other arithmetic  0.84 us (1%)
  between operations  0.76 us (1%)
    ppermute x22, starting transfers between devices, swap(): return lax.ppermute(array, axis, [(i, i ^ bit) for i in range(count)])  27.4 us
    ppermute x22, waiting for transfers between devices, swap(): return lax.ppermute(array, axis, [(i, i ^ bit) for i in range(count)])  24.5 us
    pallas_call x10, Pallas kernels, call(): pl.pallas_call(functools.partial(kernel, dims), out_shape=[shape if hasat...  9.68 us
    unnamed x12, local copies, waits for them, and re-layouts  2.28 us
  transfers between devices with their start and end apart: 22, of which 8 were waited for; matrix products, arithmetic and copies ran while one was open for 0% of the time, Pallas kernels for 12%

profile of v2, /device:TPU:0, one launch (start us, length us, event | category | flops | bytes accessed | tf_op | source)
XLA Modules:
  0.0 65.4 jit_solution(17601054289676792885)
XLA Ops:
  0.6 0.5 collective-permute-start.2
  1.1 0.0 copy-start.4
  1.1 0.1 pad_add_fusion.me
  1.2 0.6 copy-done.4
  1.9 0.0 copy-start.1
  1.9 1.0 %copy-done.1 = f32[1,4,32,5,128]{4,2,3,1,0:T(8,128)S(1)} copy-done((f32[1,4,32,5,128]{4,2,3,1,0:T(8,128)S(1)}, f32[1,4,32,5,128]{4,2,3,1,0:T(8,128)}, u32[]{:S(2)}) %copy-start.1) | copy-done | bytes 327704
  2.8 0.7 %shard_map.79.rest_4_.packed = f32[648,128]{1,0:T(8,128)S(1)} custom-call(s32[3]{0:T(128)S(1)} %pad_add_fusion.me, f32[640,128]{1,0:T(8,128)S(1)} %bitcast.25, s32[4,8,8]{2,1,0:T(8,128)S(1)} %bitcast.30), custom_call_target="tpu_custom_call" | custom-call | tf_op jit(solution)/shard_map/pallas_call | solution.py:272
  3.6 3.7 %collective-permute-start.10 = (f32[648,128]{1,0:T(8,128)S(1)}, f32[648,128]{1,0:T(8,128)S(1)}, u32[]{:S(2)}, u32[]{:S(2)}) collective-permute-start(f32[648,128]{1,0:T(8,128)S(1)} %shard_map.79.rest_4_.packed), channel_id=1, source_target_pairs={{0,16},{8,24},{16,0},{24,8},{1,17},{9,25},{17,1},{25,9},{2,18},{10... | collective-permute-start | bytes 995336 | tf_op jit(solution)/shard_map/ppermute | solution.py:283
  7.2 1.6 %collective-permute-start.9 = (f32[648,128]{1,0:T(8,128)S(1)}, f32[648,128]{1,0:T(8,128)S(1)}, u32[]{:S(2)}, u32[]{:S(2)}) collective-permute-start(f32[648,128]{1,0:T(8,128)S(1)} %shard_map.79.rest_4_.packed), channel_id=1, source_target_pairs={{0,8},{8,0},{16,24},{24,16},{1,9},{9,1},{17,25},{25,17},{2,10},{10... | collective-permute-start | bytes 995336 | tf_op jit(solution)/shard_map/ppermute | solution.py:283
  8.8 0.0 copy-done.3
  8.8 0.0 collective-permute-start.1
  8.8 0.7 copy-done.5
  9.5 0.0 collective-permute-start
  9.5 0.0 collective-permute-done.2.cot_pair
  9.5 0.0 copy-done
  9.5 0.0 copy-done.2
  9.5 1.0 %shard_map.77 = (f32[5,2,32,128]{3,2,1,0:T(8,128)S(1)}, f32[5,2,32,128]{3,2,1,0:T(8,128)S(1)}, f32[5,2,32,128]{3,2,1,0:T(8,128)S(1)}, f32[5,2,32,128]{3,2,1,0:T(8,128)S(1)}) custom-call(s32[3]{0:T(128)S(1)} %pad_add_fusion.me, f32[640,128]{1,0:T(8,128)S(1)} %bitcast.27, f32[5,32,32]{2,1,0:T(8,128)S(1)} %bitcast.23, ...), custom_call_target="tpu_custom_call" | custom-call | tf_op jit(solution)/shard_map/pallas_call | solution.py:272
  10.5 1.6 %collective-permute-start.3 = (f32[5,2,32,128]{3,2,1,0:T(8,128)S(1)}, f32[5,2,32,128]{3,2,1,0:T(8,128)S(1)}, u32[]{:S(2)}, u32[]{:S(2)}) collective-permute-start(f32[5,2,32,128]{3,2,1,0:T(8,128)S(1)} %get-tuple-element.25), channel_id=1, source_target_pairs={{0,2},{1,3},{2,0},{3,1},{4,6},{5,7},{6,4},{7,5},{8,10},{9,11},{10,... | collective-permute-start | bytes 491528 | tf_op jit(solution)/shard_map/ppermute | solution.py:283
  12.1 0.0 collective-permute-done.dest_pair
  12.1 1.5 %collective-permute-start.4 = (f32[5,2,32,128]{3,2,1,0:T(8,128)S(1)}, f32[5,2,32,128]{3,2,1,0:T(8,128)S(1)}, u32[]{:S(2)}, u32[]{:S(2)}) collective-permute-start(f32[5,2,32,128]{3,2,1,0:T(8,128)S(1)} %get-tuple-element.26), channel_id=1, source_target_pairs={{0,4},{1,5},{2,6},{3,7},{4,0},{5,1},{6,2},{7,3},{8,12},{9,13},{10,... | collective-permute-start | bytes 491528 | tf_op jit(solution)/shard_map/ppermute | solution.py:283
  13.6 0.0 collective-permute-done.1.weight_pair
  13.6 0.5 collective-permute-start.5
  14.1 3.5 %collective-permute-done.3.rest_1_ = f32[5,2,32,128]{3,2,1,0:T(8,128)S(1)} collective-permute-done((f32[5,2,32,128]{3,2,1,0:T(8,128)S(1)}, f32[5,2,32,128]{3,2,1,0:T(8,128)S(1)}, u32[]{:S(2)}, u32[]{:S(2)}) %collective-permute-start.3) | collective-permute-done | bytes 163872 | tf_op jit(solution)/shard_map/ppermute | solution.py:283
  17.6 4.3 %collective-permute-done.4.rest_2_ = f32[5,2,32,128]{3,2,1,0:T(8,128)S(1)} collective-permute-done((f32[5,2,32,128]{3,2,1,0:T(8,128)S(1)}, f32[5,2,32,128]{3,2,1,0:T(8,128)S(1)}, u32[]{:S(2)}, u32[]{:S(2)}) %collective-permute-start.4) | collective-permute-done | bytes 163872 | tf_op jit(solution)/shard_map/ppermute | solution.py:283
  21.9 0.0 collective-permute-done.5.rest_3_
  21.9 1.2 %shard_map.78 = (f32[2,4,6,8,128]{4,3,2,1,0:T(8,128)S(1)}, f32[2,4,6,8,128]{4,3,2,1,0:T(8,128)S(1)}, f32[2,4,6,8,128]{4,3,2,1,0:T(8,128)S(1)}, f32[2,4,6,8,128]{4,3,2,1,0:T(8,128)S(1)}, s32[2,128]{1,0:T(2,128)S(1)}) custom-call(s32[3]{0:T(128)S(1)} %pad_add_fusion.me, s32[1,128]{1,0:T(1,128)S(1)} %bitcast.32, s32[1,128]{1,0:T(1,128)S(1)} %collective-permute-done.dest_pair, ...), custom_call_target="tpu_custom_call" | custom-call | tf_op jit(solution)/shard_map/pallas_call | solution.py:272
  23.2 0.0 collective-permute-done.10.array
  23.2 0.0 collective-permute-done.9.rest_1_.rest_5_
  23.2 0.7 %shard_map.80.rest_6_ = f32[648,128]{1,0:T(8,128)S(1)} custom-call(s32[3]{0:T(128)S(1)} %pad_add_fusion.me, f32[648,128]{1,0:T(8,128)S(1)} %collective-permute-done.10.array, s32[2,128]{1,0:T(2,128)S(1)} %get-tuple-element.28.rest_0_.dest, f32[648,128]{1,0:T(8,128)S(1)} %collective-permute-done.9.rest_1_.rest_5_), custom_call_target="tpu_custom_call" | custom-call | tf_op jit(solution)/shard_map/pallas_call | solution.py:272
  23.9 1.5 %collective-permute-start.11 = (f32[648,128]{1,0:T(8,128)S(1)}, f32[648,128]{1,0:T(8,128)S(1)}, u32[]{:S(2)}, u32[]{:S(2)}) collective-permute-start(f32[648,128]{1,0:T(8,128)S(1)} %shard_map.80.rest_6_), channel_id=1, source_target_pairs={{0,8},{8,0},{16,24},{24,16},{1,9},{9,1},{17,25},{25,17},{2,10},{10... | collective-permute-start | bytes 995336 | tf_op jit(solution)/shard_map/ppermute | solution.py:283
  25.3 1.5 %collective-permute-start.6 = (f32[2,4,6,8,128]{4,3,2,1,0:T(8,128)S(1)}, f32[2,4,6,8,128]{4,3,2,1,0:T(8,128)S(1)}, u32[]{:S(2)}, u32[]{:S(2)}) collective-permute-start(f32[2,4,6,8,128]{4,3,2,1,0:T(8,128)S(1)} %get-tuple-element.30), channel_id=1, source_target_pairs={{0,2},{1,3},{2,0},{3,1},{4,6},{5,7},{6,4},{7,5},{8,10},{9,11},{10,... | collective-permute-start | bytes 589832 | tf_op jit(solution)/shard_map/ppermute | solution.py:283
  26.8 1.5 %collective-permute-start.7 = (f32[2,4,6,8,128]{4,3,2,1,0:T(8,128)S(1)}, f32[2,4,6,8,128]{4,3,2,1,0:T(8,128)S(1)}, u32[]{:S(2)}, u32[]{:S(2)}) collective-permute-start(f32[2,4,6,8,128]{4,3,2,1,0:T(8,128)S(1)} %get-tuple-element.31), channel_id=1, source_target_pairs={{0,4},{1,5},{2,6},{3,7},{4,0},{5,1},{6,2},{7,3},{8,12},{9,13},{10,... | collective-permute-start | bytes 589832 | tf_op jit(solution)/shard_map/ppermute | solution.py:283
  28.3 0.5 collective-permute-start.8
  28.8 4.3 %collective-permute-done.6.rest_1_ = f32[2,4,6,8,128]{4,3,2,1,0:T(8,128)S(1)} collective-permute-done((f32[2,4,6,8,128]{4,3,2,1,0:T(8,128)S(1)}, f32[2,4,6,8,128]{4,3,2,1,0:T(8,128)S(1)}, u32[]{:S(2)}, u32[]{:S(2)}) %collective-permute-start.6) | collective-permute-done | bytes 196640 | tf_op jit(solution)/shard_map/ppermute | solution.py:283
  33.1 3.8 %collective-permute-done.7.rest_2_ = f32[2,4,6,8,128]{4,3,2,1,0:T(8,128)S(1)} collective-permute-done((f32[2,4,6,8,128]{4,3,2,1,0:T(8,128)S(1)}, f32[2,4,6,8,128]{4,3,2,1,0:T(8,128)S(1)}, u32[]{:S(2)}, u32[]{:S(2)}) %collective-permute-start.7) | collective-permute-done | bytes 196640 | tf_op jit(solution)/shard_map/ppermute | solution.py:283
  37.0 0.0 collective-permute-done.8.rest_3_
  37.0 0.6 shard_map.81.rest_8_
  37.5 2.8 %collective-permute-start.15 = (f32[6,8,8,128]{3,2,1,0:T(8,128)S(1)}, f32[6,8,8,128]{3,2,1,0:T(8,128)S(1)}, u32[]{:S(2)}, u32[]{:S(2)}) collective-permute-start(f32[6,8,8,128]{3,2,1,0:T(8,128)S(1)} %shard_map.81.rest_8_), channel_id=1, source_target_pairs={{0,16},{8,24},{16,0},{24,8},{1,17},{9,25},{17,1},{25,9},{2,18},{10... | collective-permute-start | bytes 589832 | tf_op jit(solution)/shard_map/ppermute | solution.py:283
  40.3 0.0 collective-permute-done.11.rest_7_
  40.3 1.2 %shard_map.82 = (f32[2,4,5,8,128]{4,3,2,1,0:T(8,128)S(1)}, f32[2,4,5,8,128]{4,3,2,1,0:T(8,128)S(1)}, f32[2,4,5,8,128]{4,3,2,1,0:T(8,128)S(1)}, f32[2,4,5,8,128]{4,3,2,1,0:T(8,128)S(1)}) custom-call(s32[3]{0:T(128)S(1)} %pad_add_fusion.me, f32[2,4,6,8,128]{4,3,2,1,0:T(8,128)S(1)} %get-tuple-element.29.rest_0_, ...), custom_call_target="tpu_custom_call" | custom-call | tf_op jit(solution)/shard_map/pallas_call | solution.py:272
  41.5 1.3 %collective-permute-start.12 = (f32[2,4,5,8,128]{4,3,2,1,0:T(8,128)S(1)}, f32[2,4,5,8,128]{4,3,2,1,0:T(8,128)S(1)}, u32[]{:S(2)}, u32[]{:S(2)}) collective-permute-start(f32[2,4,5,8,128]{4,3,2,1,0:T(8,128)S(1)} %get-tuple-element.34), channel_id=1, source_target_pairs={{0,2},{1,3},{2,0},{3,1},{4,6},{5,7},{6,4},{7,5},{8,10},{9,11},{10,... | collective-permute-start | bytes 491528 | tf_op jit(solution)/shard_map/ppermute | solution.py:283
  42.8 0.8 %collective-permute-start.13 = (f32[2,4,5,8,128]{4,3,2,1,0:T(8,128)S(1)}, f32[2,4,5,8,128]{4,3,2,1,0:T(8,128)S(1)}, u32[]{:S(2)}, u32[]{:S(2)}) collective-permute-start(f32[2,4,5,8,128]{4,3,2,1,0:T(8,128)S(1)} %get-tuple-element.35), channel_id=1, source_target_pairs={{0,4},{1,5},{2,6},{3,7},{4,0},{5,1},{6,2},{7,3},{8,12},{9,13},{10,... | collective-permute-start | bytes 491528 | tf_op jit(solution)/shard_map/ppermute | solution.py:283
  43.6 1.4 %collective-permute-start.14 = (f32[2,4,5,8,128]{4,3,2,1,0:T(8,128)S(1)}, f32[2,4,5,8,128]{4,3,2,1,0:T(8,128)S(1)}, u32[]{:S(2)}, u32[]{:S(2)}) collective-permute-start(f32[2,4,5,8,128]{4,3,2,1,0:T(8,128)S(1)} %get-tuple-element.36), channel_id=1, source_target_pairs={{0,6},{1,7},{2,4},{3,5},{4,2},{5,3},{6,0},{7,1},{8,14},{9,15},{10,... | collective-permute-start | bytes 491528 | tf_op jit(solution)/shard_map/ppermute | solution.py:283
  45.0 0.6 shard_map.84
  45.6 0.4 collective-permute-start.19
  46.1 2.3 %collective-permute-done.15.rest_4_.rest_2_ = f32[6,8,8,128]{3,2,1,0:T(8,128)S(1)} collective-permute-done((f32[6,8,8,128]{3,2,1,0:T(8,128)S(1)}, f32[6,8,8,128]{3,2,1,0:T(8,128)S(1)}, u32[]{:S(2)}, u32[]{:S(2)}) %collective-permute-start.15) | collective-permute-done | bytes 196640 | tf_op jit(solution)/shard_map/ppermute | solution.py:283
  48.4 2.8 %collective-permute-start.20 = (f32[6,8,8,128]{3,2,1,0:T(8,128)S(1)}, f32[6,8,8,128]{3,2,1,0:T(8,128)S(1)}, u32[]{:S(2)}, u32[]{:S(2)}) collective-permute-start(f32[6,8,8,128]{3,2,1,0:T(8,128)S(1)} %get-tuple-element.42), channel_id=1, source_target_pairs={{0,24},{8,16},{16,8},{24,0},{1,25},{9,17},{17,9},{25,1},{2,26},{10... | collective-permute-start | bytes 589832 | tf_op jit(solution)/shard_map/ppermute | solution.py:283
  51.1 0.0 collective-permute-done.12.rest_1_
  51.1 0.0 collective-permute-done.13.rest_2_
  51.1 0.0 collective-permute-done.14.rest_3_
  51.1 1.0 %shard_map.83 = (f32[5,2,32,128]{3,2,1,0:T(8,128)S(1)}, f32[5,2,32,128]{3,2,1,0:T(8,128)S(1)}, f32[5,2,32,128]{3,2,1,0:T(8,128)S(1)}, f32[5,2,32,128]{3,2,1,0:T(8,128)S(1)}) custom-call(s32[3]{0:T(128)S(1)} %pad_add_fusion.me, s32[2,128]{1,0:T(2,128)S(1)} %get-tuple-element.28.rest_0_.dest, f32[2,4,5,8,128]{4,3,2,1,0:T(8,128)S(1)} %get-tuple-element.33.rest_0_.rest_4_, ...), custom_call_target="tpu_custom_call" | custom-call | tf_op jit(solution)/shard_map/pallas_call | solution.py:272
  52.1 1.5 %collective-permute-start.16 = (f32[5,2,32,128]{3,2,1,0:T(8,128)S(1)}, f32[5,2,32,128]{3,2,1,0:T(8,128)S(1)}, u32[]{:S(2)}, u32[]{:S(2)}) collective-permute-start(f32[5,2,32,128]{3,2,1,0:T(8,128)S(1)} %get-tuple-element.38), channel_id=1, source_target_pairs={{0,2},{1,3},{2,0},{3,1},{4,6},{5,7},{6,4},{7,5},{8,10},{9,11},{10,... | collective-permute-start | bytes 491528 | tf_op jit(solution)/shard_map/ppermute | solution.py:283
  53.7 0.6 collective-permute-start.17
  54.2 1.5 %collective-permute-start.18 = (f32[5,2,32,128]{3,2,1,0:T(8,128)S(1)}, f32[5,2,32,128]{3,2,1,0:T(8,128)S(1)}, u32[]{:S(2)}, u32[]{:S(2)}) collective-permute-start(f32[5,2,32,128]{3,2,1,0:T(8,128)S(1)} %get-tuple-element.40), channel_id=1, source_target_pairs={{0,6},{1,7},{2,4},{3,5},{4,2},{5,3},{6,0},{7,1},{8,14},{9,15},{10,... | collective-permute-start | bytes 491528 | tf_op jit(solution)/shard_map/ppermute | solution.py:283
  55.7 0.0 collective-permute-done.19.rest_4_.rest_1_
  55.7 1.2 %collective-permute-done.20.rest_5_.rest_3_ = f32[6,8,8,128]{3,2,1,0:T(8,128)S(1)} collective-permute-done((f32[6,8,8,128]{3,2,1,0:T(8,128)S(1)}, f32[6,8,8,128]{3,2,1,0:T(8,128)S(1)}, u32[]{:S(2)}, u32[]{:S(2)}) %collective-permute-start.20) | collective-permute-done | bytes 196640 | tf_op jit(solution)/shard_map/ppermute | solution.py:283
  56.9 2.1 %collective-permute-done.16.rest_1_ = f32[5,2,32,128]{3,2,1,0:T(8,128)S(1)} collective-permute-done((f32[5,2,32,128]{3,2,1,0:T(8,128)S(1)}, f32[5,2,32,128]{3,2,1,0:T(8,128)S(1)}, u32[]{:S(2)}, u32[]{:S(2)}) %collective-permute-start.16) | collective-permute-done | bytes 163872 | tf_op jit(solution)/shard_map/ppermute | solution.py:283
  59.1 2.8 %collective-permute-done.17.rest_2_ = f32[5,2,32,128]{3,2,1,0:T(8,128)S(1)} collective-permute-done((f32[5,2,32,128]{3,2,1,0:T(8,128)S(1)}, f32[5,2,32,128]{3,2,1,0:T(8,128)S(1)}, u32[]{:S(2)}, u32[]{:S(2)}) %collective-permute-start.17) | collective-permute-done | bytes 163872 | tf_op jit(solution)/shard_map/ppermute | solution.py:283
  61.8 0.0 collective-permute-done.18.rest_3_
  61.8 1.0 %shard_map.85 = (f32[640,128]{1,0:T(8,128)S(1)}, f32[640,128]{1,0:T(8,128)S(1)}) custom-call(s32[3]{0:T(128)S(1)} %pad_add_fusion.me, f32[5,32,32]{2,1,0:T(8,128)S(1)} %bitcast.24, f32[5,2,32,128]{3,2,1,0:T(8,128)S(1)} %get-tuple-element.37.rest_0_, f32[5,2,32,128]{3,2,1,0:T(8,128)S(1)} %collective-permute-done.16.rest_1_, ...), custom_call_target="tpu_custom_call" | custom-call | tf_op jit(solution)/shard_map/pallas_call | solution.py:272
  62.9 0.1 collective-permute-start.21
  62.9 1.7 %shard_map.86 = f32[4,5,32,128]{3,2,1,0:T(8,128)} custom-call(s32[3]{0:T(128)S(1)} %pad_add_fusion.me, f32[648,128]{1,0:T(8,128)S(1)} %shard_map.79.rest_4_.packed, f32[6,8,8,128]{3,2,1,0:T(8,128)S(1)} %get-tuple-element.45.rest_0_, f32[6,8,8,128]{3,2,1,0:T(8,128)S(1)} %collective-permute-done.19.rest_4_.rest_1_, ...), custom_call_target="tpu_custom_call" | custom-call | tf_op jit(solution)/shard_map/pallas_call | solution.py:272
  64.7 0.0 collective-permute-done.21
  64.7 0.8 %add.9 = f32[640,128]{1,0:T(8,128)} add(f32[640,128]{1,0:T(8,128)S(1)} %get-tuple-element.43, f32[640,128]{1,0:T(8,128)S(1)} %collective-permute-done.21) | non-fusion elementwise | flops 81920 | bytes 983040 | tf_op jit(solution)/shard_map/add | solution.py:382
  (4 shorter events, 0.0 us)
Async XLA Ops:
  0.6 8.8 %collective-permute-start.2 = (f32[640,128]{1,0:T(8,128)}, f32[640,128]{1,0:T(8,128)S(1)}, u32[]{:S(2)}, u32[]{:S(2)}) collective-permute-start(f32[640,128]{1,0:T(8,128)} %bitcast.26), channel_id=1, source_target_pairs={{0,1},{1,0},{2,3},{3,2},{4,5},{5,4},{6,7},{7,6},{8,9},{9,8},{10,11... | collective-permute-start | bytes 983048 | tf_op jit(solution)/shard_map/ppermute | solution.py:283
  1.1 0.7 %copy-start.4 = (s32[1,1,4,8,8]{4,3,2,1,0:T(8,128)S(1)}, s32[1,1,4,8,8]{4,3,2,1,0:T(8,128)}, u32[]{:S(2)}) copy-start(s32[1,1,4,8,8]{4,3,2,1,0:T(8,128)} %param.10) | copy-start | bytes 3076
  1.9 1.0 %copy-start.1 = (f32[1,4,32,5,128]{4,2,3,1,0:T(8,128)S(1)}, f32[1,4,32,5,128]{4,2,3,1,0:T(8,128)}, u32[]{:S(2)}) copy-start(f32[1,4,32,5,128]{4,2,3,1,0:T(8,128)} %param.6) | copy-start | bytes 983044
  2.8 6.0 %copy-start.3 = (f32[1,4,32,128]{3,2,1,0:T(8,128)S(1)}, f32[1,4,32,128]{3,2,1,0:T(8,128)}, u32[]{:S(2)}) copy-start(f32[1,4,32,128]{3,2,1,0:T(8,128)} %param.8) | copy-start | bytes 196612
  2.8 6.6 %copy-start = (f32[1,5,32,32]{3,2,1,0:T(8,128)S(1)}, f32[1,5,32,32]{3,2,1,0:T(8,128)}, u32[]{:S(2)}) copy-start(f32[1,5,32,32]{3,2,1,0:T(8,128)} %param.9) | copy-start | bytes 61444
  2.8 6.6 %copy-start.2 = (f32[1,32,4,5,128]{4,2,3,1,0:T(4,128)S(1)}, f32[1,32,4,5,128]{4,2,3,1,0:T(4,128)}, u32[]{:S(2)}) copy-start(f32[1,32,4,5,128]{4,2,3,1,0:T(4,128)} %param.7) | copy-start | bytes 983044
  3.6 19.6 %collective-permute-start.10 = (f32[648,128]{1,0:T(8,128)S(1)}, f32[648,128]{1,0:T(8,128)S(1)}, u32[]{:S(2)}, u32[]{:S(2)}) collective-permute-start(f32[648,128]{1,0:T(8,128)S(1)} %shard_map.79.rest_4_.packed), channel_id=1, source_target_pairs={{0,16},{8,24},{16,0},{24,8},{1,17},{9,25},{17,1},{25,9},{2,18},{10... | collective-permute-start | bytes 995336 | tf_op jit(solution)/shard_map/ppermute | solution.py:283
  7.2 15.9 %collective-permute-start.9 = (f32[648,128]{1,0:T(8,128)S(1)}, f32[648,128]{1,0:T(8,128)S(1)}, u32[]{:S(2)}, u32[]{:S(2)}) collective-permute-start(f32[648,128]{1,0:T(8,128)S(1)} %shard_map.79.rest_4_.packed), channel_id=1, source_target_pairs={{0,8},{8,0},{16,24},{24,16},{1,9},{9,1},{17,25},{25,17},{2,10},{10... | collective-permute-start | bytes 995336 | tf_op jit(solution)/shard_map/ppermute | solution.py:283
  8.8 0.7 %copy-start.5 = (s32[1,1,128]{2,1,0:T(1,128)S(1)}, s32[1,1,128]{2,1,0:T(1,128)}, u32[]{:S(2)}) copy-start(s32[1,1,128]{2,1,0:T(1,128)} %param.11) | copy-start | bytes 1540
  8.8 4.8 %collective-permute-start.1 = (f32[128,128]{1,0:T(8,128)S(1)}, f32[128,128]{1,0:T(8,128)S(1)}, u32[]{:S(2)}, u32[]{:S(2)}) collective-permute-start(f32[128,128]{1,0:T(8,128)S(1)} %bitcast.28), channel_id=1, source_target_pairs={{0,1},{1,0},{2,3},{3,2},{4,5},{5,4},{6,7},{7,6},{8,9},{9,8},{10,11... | collective-permute-start | bytes 196616 | tf_op jit(solution)/shard_map/ppermute | solution.py:283
  9.5 2.6 %collective-permute-start = (s32[1,128]{1,0:T(1,128)S(1)}, s32[1,128]{1,0:T(1,128)S(1)}, u32[]{:S(2)}, u32[]{:S(2)}) collective-permute-start(s32[1,128]{1,0:T(1,128)S(1)} %bitcast.31), channel_id=1, source_target_pairs={{0,1},{1,0},{2,3},{3,2},{4,5},{5,4},{6,7},{7,6},{8,9},{9,8},{10,11... | collective-permute-start | bytes 1544 | tf_op jit(solution)/shard_map/ppermute | solution.py:283
  10.5 7.1 %collective-permute-start.3 = (f32[5,2,32,128]{3,2,1,0:T(8,128)S(1)}, f32[5,2,32,128]{3,2,1,0:T(8,128)S(1)}, u32[]{:S(2)}, u32[]{:S(2)}) collective-permute-start(f32[5,2,32,128]{3,2,1,0:T(8,128)S(1)} %get-tuple-element.25), channel_id=1, source_target_pairs={{0,2},{1,3},{2,0},{3,1},{4,6},{5,7},{6,4},{7,5},{8,10},{9,11},{10,... | collective-permute-start | bytes 491528 | tf_op jit(solution)/shard_map/ppermute | solution.py:283
  12.1 9.8 %collective-permute-start.4 = (f32[5,2,32,128]{3,2,1,0:T(8,128)S(1)}, f32[5,2,32,128]{3,2,1,0:T(8,128)S(1)}, u32[]{:S(2)}, u32[]{:S(2)}) collective-permute-start(f32[5,2,32,128]{3,2,1,0:T(8,128)S(1)} %get-tuple-element.26), channel_id=1, source_target_pairs={{0,4},{1,5},{2,6},{3,7},{4,0},{5,1},{6,2},{7,3},{8,12},{9,13},{10,... | collective-permute-start | bytes 491528 | tf_op jit(solution)/shard_map/ppermute | solution.py:283
  13.6 8.3 %collective-permute-start.5 = (f32[5,2,32,128]{3,2,1,0:T(8,128)S(1)}, f32[5,2,32,128]{3,2,1,0:T(8,128)S(1)}, u32[]{:S(2)}, u32[]{:S(2)}) collective-permute-start(f32[5,2,32,128]{3,2,1,0:T(8,128)S(1)} %get-tuple-element.27), channel_id=1, source_target_pairs={{0,6},{1,7},{2,4},{3,5},{4,2},{5,3},{6,0},{7,1},{8,14},{9,15},{10,... | collective-permute-start | bytes 491528 | tf_op jit(solution)/shard_map/ppermute | solution.py:283
  23.9 16.4 %collective-permute-start.11 = (f32[648,128]{1,0:T(8,128)S(1)}, f32[648,128]{1,0:T(8,128)S(1)}, u32[]{:S(2)}, u32[]{:S(2)}) collective-permute-start(f32[648,128]{1,0:T(8,128)S(1)} %shard_map.80.rest_6_), channel_id=1, source_target_pairs={{0,8},{8,0},{16,24},{24,16},{1,9},{9,1},{17,25},{25,17},{2,10},{10... | collective-permute-start | bytes 995336 | tf_op jit(solution)/shard_map/ppermute | solution.py:283
  25.3 7.8 %collective-permute-start.6 = (f32[2,4,6,8,128]{4,3,2,1,0:T(8,128)S(1)}, f32[2,4,6,8,128]{4,3,2,1,0:T(8,128)S(1)}, u32[]{:S(2)}, u32[]{:S(2)}) collective-permute-start(f32[2,4,6,8,128]{4,3,2,1,0:T(8,128)S(1)} %get-tuple-element.30), channel_id=1, source_target_pairs={{0,2},{1,3},{2,0},{3,1},{4,6},{5,7},{6,4},{7,5},{8,10},{9,11},{10,... | collective-permute-start | bytes 589832 | tf_op jit(solution)/shard_map/ppermute | solution.py:283
  26.8 10.2 %collective-permute-start.7 = (f32[2,4,6,8,128]{4,3,2,1,0:T(8,128)S(1)}, f32[2,4,6,8,128]{4,3,2,1,0:T(8,128)S(1)}, u32[]{:S(2)}, u32[]{:S(2)}) collective-permute-start(f32[2,4,6,8,128]{4,3,2,1,0:T(8,128)S(1)} %get-tuple-element.31), channel_id=1, source_target_pairs={{0,4},{1,5},{2,6},{3,7},{4,0},{5,1},{6,2},{7,3},{8,12},{9,13},{10,... | collective-permute-start | bytes 589832 | tf_op jit(solution)/shard_map/ppermute | solution.py:283
  28.3 8.6 %collective-permute-start.8 = (f32[2,4,6,8,128]{4,3,2,1,0:T(8,128)S(1)}, f32[2,4,6,8,128]{4,3,2,1,0:T(8,128)S(1)}, u32[]{:S(2)}, u32[]{:S(2)}) collective-permute-start(f32[2,4,6,8,128]{4,3,2,1,0:T(8,128)S(1)} %get-tuple-element.32), channel_id=1, source_target_pairs={{0,6},{1,7},{2,4},{3,5},{4,2},{5,3},{6,0},{7,1},{8,14},{9,15},{10,... | collective-permute-start | bytes 589832 | tf_op jit(solution)/shard_map/ppermute | solution.py:283
  37.5 10.8 %collective-permute-start.15 = (f32[6,8,8,128]{3,2,1,0:T(8,128)S(1)}, f32[6,8,8,128]{3,2,1,0:T(8,128)S(1)}, u32[]{:S(2)}, u32[]{:S(2)}) collective-permute-start(f32[6,8,8,128]{3,2,1,0:T(8,128)S(1)} %shard_map.81.rest_8_), channel_id=1, source_target_pairs={{0,16},{8,24},{16,0},{24,8},{1,17},{9,25},{17,1},{25,9},{2,18},{10... | collective-permute-start | bytes 589832 | tf_op jit(solution)/shard_map/ppermute | solution.py:283
  41.5 9.6 %collective-permute-start.12 = (f32[2,4,5,8,128]{4,3,2,1,0:T(8,128)S(1)}, f32[2,4,5,8,128]{4,3,2,1,0:T(8,128)S(1)}, u32[]{:S(2)}, u32[]{:S(2)}) collective-permute-start(f32[2,4,5,8,128]{4,3,2,1,0:T(8,128)S(1)} %get-tuple-element.34), channel_id=1, source_target_pairs={{0,2},{1,3},{2,0},{3,1},{4,6},{5,7},{6,4},{7,5},{8,10},{9,11},{10,... | collective-permute-start | bytes 491528 | tf_op jit(solution)/shard_map/ppermute | solution.py:283
  42.8 8.4 %collective-permute-start.13 = (f32[2,4,5,8,128]{4,3,2,1,0:T(8,128)S(1)}, f32[2,4,5,8,128]{4,3,2,1,0:T(8,128)S(1)}, u32[]{:S(2)}, u32[]{:S(2)}) collective-permute-start(f32[2,4,5,8,128]{4,3,2,1,0:T(8,128)S(1)} %get-tuple-element.35), channel_id=1, source_target_pairs={{0,4},{1,5},{2,6},{3,7},{4,0},{5,1},{6,2},{7,3},{8,12},{9,13},{10,... | collective-permute-start | bytes 491528 | tf_op jit(solution)/shard_map/ppermute | solution.py:283
  43.6 7.5 %collective-permute-start.14 = (f32[2,4,5,8,128]{4,3,2,1,0:T(8,128)S(1)}, f32[2,4,5,8,128]{4,3,2,1,0:T(8,128)S(1)}, u32[]{:S(2)}, u32[]{:S(2)}) collective-permute-start(f32[2,4,5,8,128]{4,3,2,1,0:T(8,128)S(1)} %get-tuple-element.36), channel_id=1, source_target_pairs={{0,6},{1,7},{2,4},{3,5},{4,2},{5,3},{6,0},{7,1},{8,14},{9,15},{10,... | collective-permute-start | bytes 491528 | tf_op jit(solution)/shard_map/ppermute | solution.py:283
  45.6 10.1 %collective-permute-start.19 = (f32[6,8,8,128]{3,2,1,0:T(8,128)S(1)}, f32[6,8,8,128]{3,2,1,0:T(8,128)S(1)}, u32[]{:S(2)}, u32[]{:S(2)}) collective-permute-start(f32[6,8,8,128]{3,2,1,0:T(8,128)S(1)} %get-tuple-element.41), channel_id=1, source_target_pairs={{0,8},{8,0},{16,24},{24,16},{1,9},{9,1},{17,25},{25,17},{2,10},{10... | collective-permute-start | bytes 589832 | tf_op jit(solution)/shard_map/ppermute | solution.py:283
  48.4 8.6 %collective-permute-start.20 = (f32[6,8,8,128]{3,2,1,0:T(8,128)S(1)}, f32[6,8,8,128]{3,2,1,0:T(8,128)S(1)}, u32[]{:S(2)}, u32[]{:S(2)}) collective-permute-start(f32[6,8,8,128]{3,2,1,0:T(8,128)S(1)} %get-tuple-element.42), channel_id=1, source_target_pairs={{0,24},{8,16},{16,8},{24,0},{1,25},{9,17},{17,9},{25,1},{2,26},{10... | collective-permute-start | bytes 589832 | tf_op jit(solution)/shard_map/ppermute | solution.py:283
  52.1 6.9 %collective-permute-start.16 = (f32[5,2,32,128]{3,2,1,0:T(8,128)S(1)}, f32[5,2,32,128]{3,2,1,0:T(8,128)S(1)}, u32[]{:S(2)}, u32[]{:S(2)}) collective-permute-start(f32[5,2,32,128]{3,2,1,0:T(8,128)S(1)} %get-tuple-element.38), channel_id=1, source_target_pairs={{0,2},{1,3},{2,0},{3,1},{4,6},{5,7},{6,4},{7,5},{8,10},{9,11},{10,... | collective-permute-start | bytes 491528 | tf_op jit(solution)/shard_map/ppermute | solution.py:283
  53.7 8.2 %collective-permute-start.17 = (f32[5,2,32,128]{3,2,1,0:T(8,128)S(1)}, f32[5,2,32,128]{3,2,1,0:T(8,128)S(1)}, u32[]{:S(2)}, u32[]{:S(2)}) collective-permute-start(f32[5,2,32,128]{3,2,1,0:T(8,128)S(1)} %get-tuple-element.39), channel_id=1, source_target_pairs={{0,4},{1,5},{2,6},{3,7},{4,0},{5,1},{6,2},{7,3},{8,12},{9,13},{10,... | collective-permute-start | bytes 491528 | tf_op jit(solution)/shard_map/ppermute | solution.py:283
  54.2 7.6 %collective-permute-start.18 = (f32[5,2,32,128]{3,2,1,0:T(8,128)S(1)}, f32[5,2,32,128]{3,2,1,0:T(8,128)S(1)}, u32[]{:S(2)}, u32[]{:S(2)}) collective-permute-start(f32[5,2,32,128]{3,2,1,0:T(8,128)S(1)} %get-tuple-element.40), channel_id=1, source_target_pairs={{0,6},{1,7},{2,4},{3,5},{4,2},{5,3},{6,0},{7,1},{8,14},{9,15},{10,... | collective-permute-start | bytes 491528 | tf_op jit(solution)/shard_map/ppermute | solution.py:283
  62.9 1.8 %collective-permute-start.21 = (f32[640,128]{1,0:T(8,128)S(1)}, f32[640,128]{1,0:T(8,128)S(1)}, u32[]{:S(2)}, u32[]{:S(2)}) collective-permute-start(f32[640,128]{1,0:T(8,128)S(1)} %get-tuple-element.44.rest_4_), channel_id=1, source_target_pairs={{0,1},{1,0},{2,3},{3,2},{4,5},{5,4},{6,7},{7,6},{8,9},{9,8},{10,11... | collective-permute-start | bytes 983048 | tf_op jit(solution)/shard_map/ppermute | solution.py:283

commit v3 on v2

v3 whole, which is shorter than its diff:
```python
import functools

import jax
import jax.numpy as jnp
from jax import lax
from jax.experimental import pallas as pl
from jax.experimental.pallas import tpu as pltpu
from jax.sharding import PartitionSpec as P

LANES = 128
F32 = jnp.float32
EXACT = functools.partial(lax.dot_general, precision=lax.Precision.HIGHEST, preferred_element_type=F32)
SHORT = functools.partial(lax.dot_general, preferred_element_type=F32)


def two_parts(values):
    high = values.astype(jnp.bfloat16)
    return high, (values - high.astype(F32)).astype(jnp.bfloat16)


def pick(table, values, contract):
    dims = ((contract, (0,)), ((), ()))
    high, low = two_parts(values)
    return SHORT(table, low, dims) + SHORT(table, high, dims)


def product(left, right, contract):
    dims = ((contract, (0,)), ((), ()))
    left_high, left_low = two_parts(left)
    right_high, right_low = two_parts(right)
    return (
        SHORT(left_low, right_high, dims)
        + SHORT(left_high, right_low, dims)
        + SHORT(left_high, right_high, dims)
    )


def hot(rows, wanted):
    return jnp.where(rows == wanted, 1.0, 0.0).astype(jnp.bfloat16)


def iota(shape, axis):
    return lax.broadcasted_iota(jnp.int32, shape, axis)


def xor(a, b):
    return jnp.bitwise_xor(a, b)


def pack_kernel(dims, state, source_in, dest_in, cot_in, weight_in, inverse_in, *rest):
    lats, slabs, chips, cap, lev_dev, here, fields = dims
    out, mine, cot, weight, inverse, source, dest, sems = rest
    total = state.shape[0]
    copies = [
        pltpu.make_async_copy(src, dst, sems.at[i])
        for i, (src, dst) in enumerate(
            (
                (source_in, source),
                (dest_in, dest),
                (state, out.at[pl.ds(0, total)]),
                (cot_in, cot),
                (weight_in, weight),
                (inverse_in, inverse),
            )
        )
    ]
    for copy in copies:
        copy.start()
    copies[0].wait()
    copies[1].wait()
    numbers = source[...].reshape(lats * slabs, cap).astype(F32)
    slots = slabs * cap
    row = iota((slabs, slots), 0)
    at = iota((slabs, slots), 1)
    core = at // (chips * cap)
    chosen = row == (at // cap - core * chips) * 2 + core
    spread = jnp.where(iota((cap, slots), 1) % cap == iota((cap, slots), 0), 1.0, 0.0)
    wide = EXACT(numbers, spread, (((1,), (0,)), ((), ())))
    out[total:, :] = jnp.zeros((out.shape[0] - total, LANES), F32)
    for g in range(lats):
        lanes = jnp.where(chosen, wide[g * slabs : (g + 1) * slabs], 0.0)
        out[total + g : total + g + 1, :slots] = jnp.sum(lanes, axis=0, keepdims=True)
    slots = lats * chips * cap
    row = iota((lats * slabs, slots), 0)
    at = iota((lats * slabs, slots), 1)
    spread = jnp.where(iota((cap, slots), 1) % cap == iota((cap, slots), 0), 1.0, 0.0)
    wide = EXACT(numbers, spread, (((1,), (0,)), ((), ())))
    mine[...] = jnp.zeros(mine.shape, F32)
    for core in range(2):
        lanes = jnp.where(row == at // cap * 2 + core, wide, 0.0)
        mine[core : core + 1, :slots] = jnp.sum(lanes, axis=0, keepdims=True)
    mine[2:3, : dest.shape[1]] = dest[...].astype(F32)
    for copy in copies[2:]:
        copy.wait()


def start_kernel(dims, me, cot, inverse, cot_pair, weight, mine, *rest):
    lats, slabs, chips, cap, lev_dev, here, fields = dims
    out, back, held = rest[:chips], rest[-2], rest[-1]
    chip, core = me[1], me[2]
    levels = slabs * lev_dev
    step = fields * here
    span = lev_dev * 2 * here
    per = lats * cap
    for f in range(fields):
        own = [cot[pl.ds(f * here + b, levels, stride=step), :] for b in range(here)]
        pair = [cot_pair[pl.ds(f * here + b, levels, stride=step), :] for b in range(here)]
        own, pair = jnp.concatenate(own, axis=1), jnp.concatenate(pair, axis=1)
        wide = jnp.concatenate(
            [jnp.where(core == 0, own, pair), jnp.where(core == 0, pair, own)], axis=1
        )
        res = product(inverse[f], wide, (0,))
        for b in range(2 * here):
            back[f, pl.ds(b, levels, stride=2 * here), :] = res[:, b * LANES : (b + 1) * LANES]
    dest = mine[2:3, : weight.shape[0]].astype(jnp.int32)
    for x in range(2):
        res = pick(slot_table(dims, x, dest, True), weight[...], (1,))
        for c in range(chips):
            held[c, x] = res[c * per : (c + 1) * per]
    for k in range(chips):
        to = xor(chip, k)
        first = pl.multiple_of((to * 2 + core) * span, span)
        for f in range(fields):
            out[k][f * span : (f + 1) * span] = back[f, pl.ds(first, span), :]
        for x in range(2):
            at = fields * span + x * per
            out[k][at : at + per] = held[to, x]


def by_column_owner(dest, lev_dev, chips, wide):
    total = dest.shape[1]
    at = iota((total, total), 1)
    span = lev_dev * wide
    chip = at // span
    level = (at - chip * span) // wide
    block = at - chip * span - level * wide
    order = jnp.where(iota((total, total), 0) == (level * chips + chip) * wide + block, 1.0, 0.0)
    return EXACT(dest.astype(F32), order, (((1,), (0,)), ((), ()))).astype(jnp.int32)


def slot_table(dims, core, dest, by_chip):
    lats, slabs, chips, cap, lev_dev, here, fields = dims
    at = iota((lats * chips * cap, dest.shape[1]), 0)
    if by_chip:
        chip = at // (lats * cap)
        lat = at // cap - chip * lats
    else:
        lat = at // (chips * cap)
        chip = at // cap - lat * chips
    slot = at - at // cap * cap
    return hot(lat * (slabs * cap) + (chip * 2 + core) * cap + slot, dest)


def back_kernel(dims, me, mine, weight, *rest):
    lats, slabs, chips, cap, lev_dev, here, fields = dims
    got, out, other = rest[:chips], rest[-chips - 3 : -3], rest[-3]
    rows, slots = rest[-2:]
    chip, core = me[1], me[2]
    wide = 2 * here
    span = lev_dev * wide
    per = lats * cap
    order = by_column_owner(mine[2:3, : weight.shape[0]], lev_dev, chips, wide)
    for k in range(chips):
        first = pl.multiple_of(xor(chip, k) * span, span)
        for f in range(fields):
            rows[pl.ds(first, span), f * LANES : (f + 1) * LANES] = got[k][f * span : (f + 1) * span]
        other[xor(chip, k)] = got[k][pl.ds(pl.multiple_of(fields * span + (1 - core) * per, 8), per), :]
    for c in range(chips):
        for l in range(lev_dev):
            at = l * chips * wide + c * wide
            rows[c * span + l * wide : c * span + (l + 1) * wide, fields * LANES :] = weight[at : at + wide]
    tables = [slot_table(dims, core, order, False) for core in range(2)]
    res = pick(jnp.concatenate(tables, axis=0), rows[...], (1,))
    for core in range(2):
        for g in range(lats):
            for c in range(chips):
                at = ((core * lats + g) * chips + c) * cap
                for f in range(fields + 1):
                    slots[c, core, g, f] = res[at : at + cap, f * LANES : (f + 1) * LANES]
    for k in range(chips):
        out[k][...] = slots[xor(chip, k)]


def sort_kernel(groups, dims, me, *rest):
    lats, slabs, chips, cap, lev_dev, here, fields = dims
    got, outs = rest[:chips], rest[-len(groups) :]
    lat, chip, core = me[0], me[1], me[2]
    for k in range(chips):
        src = xor(chip, k)
        for out, j in zip(outs, groups):
            for x in range(2):
                for f in range(fields + 1):
                    out[f, x, src] = got[k][x, xor(lat, j), f]


def add_kernel(dims, me, mine, mine_pair, *rest):
    lats, slabs, chips, cap, lev_dev, here, fields = dims
    got, outs, rows = rest[:lats], rest[-3:-1], rest[-1]
    blocks = slabs * here
    row_total = lev_dev * blocks
    slots = lats * chips * cap
    lat, core = me[0], me[2]
    row = iota((row_total, slots), 0)
    for x, (source, out) in enumerate(zip((mine, mine_pair), outs)):
        for j in range(lats):
            for f in range(fields + 1):
                rows[f, xor(lat, j)] = got[j][f, xor(core, x)]
        low = source[pl.ds(core, 1), :slots].astype(jnp.int32)
        scale = jnp.concatenate([rows[fields].reshape(slots, LANES)] * fields, axis=1)
        value = jnp.concatenate([rows[f].reshape(slots, LANES) for f in range(fields)], axis=1)
        values = jnp.concatenate([(1.0 - scale) * value, scale * value], axis=0)
        table = jnp.concatenate([hot(row, low), hot(row, low + blocks)], axis=1)
        total = pick(table, values, (1,))
        for l in range(lev_dev):
            for f in range(fields):
                out[l, f] = total[l * blocks : (l + 1) * blocks, f * LANES : (f + 1) * LANES]


def hold_kernel(dims, me, array, mine, mine_pair, *rest):
    lats, slabs, chips, cap, lev_dev, here, fields = dims
    out, second, dests, sems = rest[-4:]
    cut = out.shape[0]
    copies = [
        pltpu.make_async_copy(array.at[pl.ds(0, cut)], out, sems.at[0]),
        pltpu.make_async_copy(array.at[pl.ds(cut, second.shape[0])], second, sems.at[1]),
    ]
    for copy in copies:
        copy.start()
    total = dests.shape[1]
    both = jnp.concatenate([mine[2:3, :total], mine_pair[2:3, :total]], axis=0)
    dests[...] = by_column_owner(both, lev_dev, chips, 2 * here)
    for copy in copies:
        copy.wait()


def mix_kernel(dims, me, weight_pair, *rest):
    lats, slabs, chips, cap, lev_dev, here, fields = dims
    got, packed, at = rest[:chips], [], chips
    for j in range(lats):
        count = 2 if forwarded(j) else 1
        packed.append(rest[at : at + count])
        at += count
    out, weight, mixed = rest[-chips - 2 : -2], rest[-2], rest[-1]
    lat, chip, core = me[0], me[1], me[2]
    blocks = slabs * here
    row_total = lev_dev * blocks
    slots = slabs * cap
    for g in range(lats):
        for k in range(chips):
            at = pl.multiple_of(fields * lev_dev * 2 * here + core * lats * cap, 8) + g * cap
            weight[g, core, xor(chip, k)] = got[k][pl.ds(at, cap), :]
            weight[g, 1 - core, k] = weight_pair[k, g * cap : (g + 1) * cap]
    row = iota((row_total, slots), 0)
    for j in range(lats):
        sender = xor(lat, j)
        tail = fields * row_total - sum(part.shape[0] for part in packed[j][:-1])
        low = packed[j][-1][pl.ds(tail + lat, 1), :][:, :slots].astype(jnp.int32)

        def level_rows(l, f, parts=packed[j]):
            at = (l * fields + f) * blocks
            if at >= parts[0].shape[0]:
                return parts[1][at - parts[0].shape[0] : at - parts[0].shape[0] + blocks]
            return parts[0][at : at + blocks]

        values = jnp.concatenate(
            [
                jnp.concatenate([level_rows(l, f) for l in range(lev_dev)], axis=0)
                for f in range(fields)
            ],
            axis=1,
        )
        table = jnp.concatenate([hot(row, low), hot(row, low + blocks)], axis=1)
        both = pick(table, values, (0,))
        scale = jnp.concatenate([weight[sender].reshape(slots, LANES)] * fields, axis=1)
        res = (1.0 - scale) * both[:slots] + scale * both[slots:]
        for r in range(2):
            for c in range(chips):
                at = (r * chips + c) * cap
                for f in range(fields):
                    mixed[r, c, f] = res[at : at + cap, f * LANES : (f + 1) * LANES]
        for k in range(chips):
            for x in range(2):
                out[k][x, sender] = mixed[xor(core, x), xor(chip, k)]


def arrive_kernel(dims, me, dest, *rest):
    lats, slabs, chips, cap, lev_dev, here, fields = dims
    got, out = rest[:chips], rest[-chips - 2 : -2]
    rows, moved = rest[-2:]
    chip, core = me[1], me[2]
    span = lev_dev * 2 * here
    for x in range(2):
        for k in range(chips):
            for g in range(lats):
                for f in range(fields):
                    rows[f, g * chips + xor(chip, k)] = got[k][x, g, f]
        values = jnp.concatenate(
            [rows[f].reshape(lats * chips * cap, LANES) for f in range(fields)], axis=1
        )
        res = pick(slot_table(dims, core, dest[x : x + 1, :], False), values, (0,))
        for c in range(chips):
            for f in range(fields):
                moved[c, f] = res[c * span : (c + 1) * span, f * LANES : (f + 1) * LANES]
        for k in range(chips):
            for f in range(fields):
                out[k][f, xor(core, x)] = moved[xor(chip, k), f]


def diffuse_kernel(dims, me, inverse, *rest):
    lats, slabs, chips, cap, lev_dev, here, fields = dims
    got, own, pair, rows = rest[:chips], rest[-3], rest[-2], rest[-1]
    chip, core = me[1], me[2]
    wide = 2 * here
    span = 2 * lev_dev * wide
    levels = slabs * lev_dev
    for k in range(chips):
        first = pl.multiple_of(xor(chip, k) * span, span)
        for f in range(fields):
            rows[f, pl.ds(first, span), :] = got[k][f].reshape(span, LANES)
    for f in range(fields):
        values = jnp.concatenate([rows[f, pl.ds(b, levels, stride=wide), :] for b in range(wide)], axis=1)
        res = product(inverse[f], values, (1,))
        first, second = res[:, : here * LANES], res[:, here * LANES :]
        mine, other = jnp.where(core == 0, first, second), jnp.where(core == 0, second, first)
        for b in range(here):
            at = pl.ds(f * here + b, levels, stride=fields * here)
            own[at, :] = mine[:, b * LANES : (b + 1) * LANES]
            pair[at, :] = other[:, b * LANES : (b + 1) * LANES]


def call(kernel, dims, args, outs, scratch=(), after=(), outside=False, limit=48):
    inside = pl.BlockSpec(memory_space=pltpu.VMEM)
    anywhere = pl.BlockSpec(memory_space=pl.ANY)
    if outside:
        specs = [anywhere] * len(args)
    else:
        specs = [pl.BlockSpec(memory_space=pltpu.SMEM)] + [inside] * (len(args) - 1)
    return pl.pallas_call(
        functools.partial(kernel, dims),
        out_shape=[shape if hasattr(shape, "dtype") else jax.ShapeDtypeStruct(shape, F32) for shape in outs],
        in_specs=specs + [anywhere] * len(after),
        out_specs=[inside] * len(outs),
        scratch_shapes=[pltpu.VMEM(shape, F32) if isinstance(shape, tuple) else shape for shape in scratch],
        compiler_params=pltpu.CompilerParams(vmem_limit_bytes=limit * 1024 * 1024),
    )(*args, *after)


def forwarded(j):
    return j % 2 == 1 and j > 1


def swap(array, axis, bit, count):
    return lax.ppermute(array, axis, [(i, i ^ bit) for i in range(count)])


def body(lats, slabs, field_state, cotangent, vertical_weight, diffusion_inverse, source_row, dest_slot):
    _, lev_dev, blocks, fields, width = field_state.shape
    cap = source_row.shape[-1]
    chips = slabs // 2
    here = blocks // slabs
    levels = slabs * lev_dev
    row_total = lev_dev * blocks
    span = lev_dev * 2 * here
    dims = (lats, slabs, chips, cap, lev_dev, here, fields)
    lat, slab = lax.axis_index("lat"), lax.axis_index("slab")
    me = jnp.stack([lat, slab // 2, slab % 2]).astype(jnp.int32)

    def pair(array):
        return swap(array, "slab", 1, slabs)

    def over_chips(messages):
        got = list(messages)
        for k in reversed(range(1, chips)):
            got[k] = swap(messages[k], "slab", 2 * k, slabs)
        return got

    state = field_state[0].transpose(0, 2, 1, 3).reshape(row_total * fields, width)
    cot = cotangent[0].transpose(0, 2, 1, 3).reshape(levels * fields * here, width)
    weights = vertical_weight.reshape(row_total, width)
    inverse = diffusion_inverse[0]
    dest = dest_slot[0]

    packed, mine, cot_here, weights_here, inverse_here = call(
        pack_kernel,
        dims,
        [
            pltpu.with_memory_space_constraint(array, pltpu.HBM)
            for array in (state, source_row[0, 0], dest, cot, weights, inverse)
        ],
        [
            (row_total * fields + -(-lats // 8) * 8, width),
            (8, max(row_total, lats * chips * cap)),
            cot.shape,
            weights.shape,
            inverse.shape,
        ],
        [
            pltpu.VMEM((lats, slabs, cap), jnp.int32),
            pltpu.VMEM(dest.shape, jnp.int32),
            pltpu.SemaphoreType.DMA((6,)),
        ],
        outside=True,
        limit=48,
    )
    mine_pair = pair(mine)
    near, far = swap(packed, "lat", 1, lats), swap(packed, "lat", 2, lats)
    first = over_chips(
        call(
            start_kernel,
            dims,
            (me, cot_here, inverse_here, pair(cot), weights_here, mine),
            [(fields * span + 2 * lats * cap, width)] * chips,
            [(fields, levels * 2 * here, width), (chips, 2, lats * cap, width)],
        )
    )
    *slot_back, weight_other = call(
        back_kernel,
        dims,
        (me, mine, weights_here, *first),
        [(2, lats, fields + 1, cap, width)] * chips + [(chips, lats * cap, width)],
        [(row_total, (fields + 1) * width), (chips, 2, lats, fields + 1, cap, width)],
        after=[mine_pair],
    )
    cut = row_total * fields // 2
    first_half, second_half, dests = call(
        hold_kernel,
        dims,
        (me, far, mine, mine_pair),
        [(cut, width), (packed.shape[0] - cut, width), jax.ShapeDtypeStruct((2, row_total), jnp.int32)],
        [pltpu.SemaphoreType.DMA((2,))],
        after=[slot_back[0], near],
    )
    slot_back = over_chips(slot_back)
    states = []
    for j in range(lats):
        if forwarded(j):
            halves = (first_half, second_half) if j == 3 else (states[-1][:cut], states[-1][cut:])
            states += [swap(half, "lat", 1, lats) for half in halves]
        else:
            states.append({0: packed, 1: near, 2: far}[j] if j < 3 else swap(packed, "lat", j, lats))
    mixed = call(
        mix_kernel,
        dims,
        (me, pair(weight_other), *first, *states),
        [(2, lats, fields, cap, width)] * chips,
        [(lats, 2, chips, cap, width), (2, chips, fields, cap, width)],
    )
    soon = [j for j in range(lats) if j == 2]
    late = [j for j in range(lats) if j not in (1, 2)]
    message = (fields + 1, 2, chips, cap, width)
    sorted_soon = call(functools.partial(sort_kernel, soon), dims, (me, *slot_back), [message] * len(soon))
    sorted_late = call(
        functools.partial(sort_kernel, late), dims, (me, *slot_back), [message] * len(late), after=mixed[:1]
    )
    returned = [None] * lats
    for j, sorted_back in zip(soon + late, [*sorted_soon, *sorted_late]):
        returned[j] = sorted_back if j == 0 else swap(sorted_back, "lat", j, lats)
    moved = call(
        arrive_kernel,
        dims,
        (me, dests, *over_chips(mixed)),
        [(fields, 2, span, width)] * chips,
        [(fields, lats * chips, cap, width), (chips, fields, span, width)],
        after=returned[2:3],
    )
    (sorted_last,) = call(
        functools.partial(sort_kernel, [1]), dims, (me, *slot_back), [message], after=moved[:1]
    )
    returned[1] = swap(sorted_last, "lat", 1, lats)
    tangent, tangent_pair = call(
        diffuse_kernel,
        dims,
        (me, inverse_here, *over_chips(moved)),
        [cot.shape, cot.shape],
        [(fields, levels * 2 * here, width)],
        after=returned[3:4],
    )
    adjoint, adjoint_pair = call(
        add_kernel,
        dims,
        (me, mine, mine_pair, *returned),
        [(lev_dev, fields, blocks, width)] * 2,
        [(fields + 1, lats, chips, cap, width)],
        after=[tangent_pair],
    )
    adjoint = adjoint + pair(adjoint_pair)
    tangent = tangent + pair(tangent_pair)
    tangent_out = tangent.reshape(1, levels, fields, here, width).transpose(0, 1, 3, 2, 4)
    adjoint_out = adjoint.transpose(0, 2, 1, 3)[None]
    return tangent_out, adjoint_out


def solution(mesh):
    placed = (
        P("lat", "slab", None, None, None),
        P("lat", None, "slab", None, None),
        P("lat", "slab", None, None),
        P("lat", None, None, None),
        P("lat", "slab", None, None, None),
        P("lat", "slab", None),
    )
    return jax.shard_map(
        functools.partial(body, mesh.shape["lat"], mesh.shape["slab"]),
        mesh=mesh,
        in_specs=placed,
        out_specs=(P("lat", None, "slab", None, None), P("lat", "slab", None, None, None)),
        check_vma=False,
    )
```

time: 65.7 us -> 62.3 us (0.948)
  the two profiles are of different devices: /device:TPU:0 before, /device:TPU:17 now
where the time goes in v3:
time: 62.3 us; the launch traced here: 62.1 us
  starting transfers between devices  26.8 us (43%)
  waiting for transfers between devices  22.4 us (36%)
  Pallas kernels  10.6 us (17%)
  other arithmetic  1.61 us (3%)
  between operations  0.76 us (1%)
    ppermute x24, starting transfers between devices, swap(): return lax.ppermute(array, axis, [(i, i ^ bit) for i in range(count)])  26.8 us
    ppermute x24, waiting for transfers between devices, swap(): return lax.ppermute(array, axis, [(i, i ^ bit) for i in range(count)])  22.4 us
    pallas_call x11, Pallas kernels, call(): pl.pallas_call(functools.partial(kernel, dims), out_shape=[shape if hasat...  10.6 us
  transfers between devices with their start and end apart: 24, of which 13 were waited for; matrix products, arithmetic and copies ran while one was open for 1% of the time, Pallas kernels for 17%

profile of v3, /device:TPU:17, one launch (start us, length us, event | category | flops | bytes accessed | tf_op | source)
XLA Modules:
  0.0 62.1 jit_solution(2183099895478427316)
XLA Ops:
  0.6 0.7 %collective-permute-start.2 = (f32[640,128]{1,0:T(8,128)}, f32[640,128]{1,0:T(8,128)S(1)}, u32[]{:S(2)}, u32[]{:S(2)}) collective-permute-start(f32[640,128]{1,0:T(8,128)} %bitcast.25), channel_id=1, source_target_pairs={{0,1},{1,0},{2,3},{3,2},{4,5},{5,4},{6,7},{7,6},{8,9},{9,8},{10,11... | collective-permute-start | bytes 983048 | tf_op jit(solution)/shard_map/ppermute | solution.py:353
  1.4 1.2 %shard_map.77 = (f32[648,128]{1,0:T(8,128)S(1)}, f32[8,128]{1,0:T(8,128)S(1)}, f32[640,128]{1,0:T(8,128)S(1)}, f32[128,128]{1,0:T(8,128)S(1)}, f32[5,32,32]{2,1,0:T(8,128)S(1)}) custom-call(f32[640,128]{1,0:T(8,128)} %bitcast.24, s32[4,8,8]{2,1,0:T(8,128)} %bitcast.30, s32[1,128]{1,0:T(1,128)} %bitcast.31, f32[640,128]{1,0:T(8,128)} %bitcast.26, ...), custom_call_target="tpu_custom_call" | custom-call | tf_op jit(solution)/shard_map/pallas_call | solution.py:338
  2.6 0.1 collective-permute-start
  2.6 1.4 %collective-permute-start.6 = (f32[648,128]{1,0:T(8,128)S(1)}, f32[648,128]{1,0:T(8,128)S(1)}, u32[]{:S(2)}, u32[]{:S(2)}) collective-permute-start(f32[648,128]{1,0:T(8,128)S(1)} %get-tuple-element.34.rest_4_), channel_id=1, source_target_pairs={{0,8},{8,0},{16,24},{24,16},{1,9},{9,1},{17,25},{25,17},{2,10},{10... | collective-permute-start | bytes 995336 | tf_op jit(solution)/shard_map/ppermute | solution.py:353
  4.0 0.6 collective-permute-start.1
  4.6 0.1 pad_add_fusion.me
  4.6 0.0 collective-permute-done.2.cot_pair
  4.6 1.0 %shard_map.78 = (f32[224,128]{1,0:T(8,128)S(1)}, f32[224,128]{1,0:T(8,128)S(1)}, f32[224,128]{1,0:T(8,128)S(1)}, f32[224,128]{1,0:T(8,128)S(1)}) custom-call(s32[3]{0:T(128)S(1)} %pad_add_fusion.me, f32[640,128]{1,0:T(8,128)S(1)} %get-tuple-element.37.cot, f32[5,32,32]{2,1,0:T(8,128)S(1)} %get-tuple-element.33.inverse, ...), custom_call_target="tpu_custom_call" | custom-call | tf_op jit(solution)/shard_map/pallas_call | solution.py:338
  5.7 1.3 %collective-permute-start.3 = (f32[224,128]{1,0:T(8,128)S(1)}, f32[224,128]{1,0:T(8,128)S(1)}, u32[]{:S(2)}, u32[]{:S(2)}) collective-permute-start(f32[224,128]{1,0:T(8,128)S(1)} %get-tuple-element.39), channel_id=1, source_target_pairs={{0,2},{1,3},{2,0},{3,1},{4,6},{5,7},{6,4},{7,5},{8,10},{9,11},{10,... | collective-permute-start | bytes 344072 | tf_op jit(solution)/shard_map/ppermute | solution.py:353
  7.0 1.2 %collective-permute-start.4 = (f32[224,128]{1,0:T(8,128)S(1)}, f32[224,128]{1,0:T(8,128)S(1)}, u32[]{:S(2)}, u32[]{:S(2)}) collective-permute-start(f32[224,128]{1,0:T(8,128)S(1)} %get-tuple-element.40), channel_id=1, source_target_pairs={{0,4},{1,5},{2,6},{3,7},{4,0},{5,1},{6,2},{7,3},{8,12},{9,13},{10,... | collective-permute-start | bytes 344072 | tf_op jit(solution)/shard_map/ppermute | solution.py:353
  8.2 0.0 collective-permute-done.1.rest_4_.mine_pair
  8.2 0.2 collective-permute-start.5
  8.4 2.1 %collective-permute-done.3.rest_1_ = f32[224,128]{1,0:T(8,128)S(1)} collective-permute-done((f32[224,128]{1,0:T(8,128)S(1)}, f32[224,128]{1,0:T(8,128)S(1)}, u32[]{:S(2)}, u32[]{:S(2)}) %collective-permute-start.3) | collective-permute-done | bytes 114720 | tf_op jit(solution)/shard_map/ppermute | solution.py:353
  10.5 2.3 %collective-permute-done.4.rest_2_ = f32[224,128]{1,0:T(8,128)S(1)} collective-permute-done((f32[224,128]{1,0:T(8,128)S(1)}, f32[224,128]{1,0:T(8,128)S(1)}, u32[]{:S(2)}, u32[]{:S(2)}) %collective-permute-start.4) | collective-permute-done | bytes 114720 | tf_op jit(solution)/shard_map/ppermute | solution.py:353
  12.8 0.6 collective-permute-done.5.rest_3_
  13.4 1.2 %shard_map.79 = (f32[2,4,6,8,128]{4,3,2,1,0:T(8,128)S(1)}, f32[2,4,6,8,128]{4,3,2,1,0:T(8,128)S(1)}, f32[2,4,6,8,128]{4,3,2,1,0:T(8,128)S(1)}, f32[2,4,6,8,128]{4,3,2,1,0:T(8,128)S(1)}, f32[4,32,128]{2,1,0:T(8,128)S(1)}) custom-call(s32[3]{0:T(128)S(1)} %pad_add_fusion.me, f32[8,128]{1,0:T(8,128)S(1)} %get-tuple-element.35.mine, ...), custom_call_target="tpu_custom_call" | custom-call | tf_op jit(solution)/shard_map/pallas_call | solution.py:338
  14.7 1.8 %collective-permute-start.13 = (f32[2,4,6,8,128]{4,3,2,1,0:T(8,128)S(1)}, f32[2,4,6,8,128]{4,3,2,1,0:T(8,128)S(1)}, u32[]{:S(2)}, u32[]{:S(2)}) collective-permute-start(f32[2,4,6,8,128]{4,3,2,1,0:T(8,128)S(1)} %get-tuple-element.51), channel_id=1, source_target_pairs={{0,2},{1,3},{2,0},{3,1},{4,6},{5,7},{6,4},{7,5},{8,10},{9,11},{10,... | collective-permute-start | bytes 589832 | tf_op jit(solution)/shard_map/ppermute | solution.py:353
  16.5 0.3 collective-permute-start.14
  16.7 1.0 %collective-permute-start.15 = (f32[2,4,6,8,128]{4,3,2,1,0:T(8,128)S(1)}, f32[2,4,6,8,128]{4,3,2,1,0:T(8,128)S(1)}, u32[]{:S(2)}, u32[]{:S(2)}) collective-permute-start(f32[2,4,6,8,128]{4,3,2,1,0:T(8,128)S(1)} %get-tuple-element.53), channel_id=1, source_target_pairs={{0,6},{1,7},{2,4},{3,5},{4,2},{5,3},{6,0},{7,1},{8,14},{9,15},{10,... | collective-permute-start | bytes 589832 | tf_op jit(solution)/shard_map/ppermute | solution.py:353
  17.7 0.0 collective-permute-done.array.rest_6_
  17.7 1.4 %collective-permute-done.6.rest_1_.rest_5_ = f32[648,128]{1,0:T(8,128)S(1)} collective-permute-done((f32[648,128]{1,0:T(8,128)S(1)}, f32[648,128]{1,0:T(8,128)S(1)}, u32[]{:S(2)}, u32[]{:S(2)}) %collective-permute-start.6) | collective-permute-done | bytes 331808 | tf_op jit(solution)/shard_map/ppermute | solution.py:353
  19.1 1.2 %shard_map.80 = (f32[320,128]{1,0:T(8,128)S(1)}, f32[328,128]{1,0:T(8,128)S(1)}, s32[2,128]{1,0:T(2,128)S(1)}) custom-call(s32[3]{0:T(128)S(1)} %pad_add_fusion.me, f32[648,128]{1,0:T(8,128)S(1)} %collective-permute-done.array.rest_6_, f32[8,128]{1,0:T(8,128)S(1)} %get-tuple-element.35.mine, f32[8,128]{1,0:T(8,128)S(1)} %collective-permute-done.1.rest_4_.mine_pair, ...), custom_call_target="tpu_custom_call" | custom-call | tf_op jit(solution)/shard_map/pallas_call | solution.py:338
  20.3 2.6 %collective-permute-start.9 = (f32[328,128]{1,0:T(8,128)S(1)}, f32[328,128]{1,0:T(8,128)S(1)}, u32[]{:S(2)}, u32[]{:S(2)}) collective-permute-start(f32[328,128]{1,0:T(8,128)S(1)} %get-tuple-element.46), channel_id=1, source_target_pairs={{0,8},{8,0},{16,24},{24,16},{1,9},{9,1},{17,25},{25,17},{2,10},{10... | collective-permute-start | bytes 503816 | tf_op jit(solution)/shard_map/ppermute | solution.py:353
  22.9 0.1 collective-permute-start.8
  22.9 0.0 collective-permute-done.13.rest_1_
  22.9 1.0 %collective-permute-start.7 = (f32[4,32,128]{2,1,0:T(8,128)S(1)}, f32[4,32,128]{2,1,0:T(8,128)S(1)}, u32[]{:S(2)}, u32[]{:S(2)}) collective-permute-start(f32[4,32,128]{2,1,0:T(8,128)S(1)} %get-tuple-element.44), channel_id=1, source_target_pairs={{0,1},{1,0},{2,3},{3,2},{4,5},{5,4},{6,7},{7,6},{8,9},{9,8},{10,11... | collective-permute-start | bytes 196616 | tf_op jit(solution)/shard_map/ppermute | solution.py:353
  23.9 0.0 collective-permute-done.14.rest_2_
  23.9 1.7 %collective-permute-done.15.rest_3_ = f32[2,4,6,8,128]{4,3,2,1,0:T(8,128)S(1)} collective-permute-done((f32[2,4,6,8,128]{4,3,2,1,0:T(8,128)S(1)}, f32[2,4,6,8,128]{4,3,2,1,0:T(8,128)S(1)}, u32[]{:S(2)}, u32[]{:S(2)}) %collective-permute-start.15) | collective-permute-done | bytes 196640 | tf_op jit(solution)/shard_map/ppermute | solution.py:353
  25.7 0.6 shard_map.82
  26.2 2.4 %collective-permute-start.16 = (f32[6,2,4,8,128]{4,3,2,1,0:T(8,128)S(1)}, f32[6,2,4,8,128]{4,3,2,1,0:T(8,128)S(1)}, u32[]{:S(2)}, u32[]{:S(2)}) collective-permute-start(f32[6,2,4,8,128]{4,3,2,1,0:T(8,128)S(1)} %shard_map.82), channel_id=1, source_target_pairs={{0,16},{8,24},{16,0},{24,8},{1,17},{9,25},{17,1},{25,9},{2,18},{10... | collective-permute-start | bytes 589832 | tf_op jit(solution)/shard_map/ppermute | solution.py:353
  28.6 0.0 collective-permute-done.7.weight_pair
  28.6 3.2 %collective-permute-done.8.rest_7_ = f32[320,128]{1,0:T(8,128)S(1)} collective-permute-done((f32[320,128]{1,0:T(8,128)S(1)}, f32[320,128]{1,0:T(8,128)S(1)}, u32[]{:S(2)}, u32[]{:S(2)}) %collective-permute-start.8) | collective-permute-done | bytes 163872 | tf_op jit(solution)/shard_map/ppermute | solution.py:353
  31.8 0.0 collective-permute-done.9.rest_8_
  31.8 1.2 %shard_map.81 = (f32[2,4,5,8,128]{4,3,2,1,0:T(8,128)S(1)}, f32[2,4,5,8,128]{4,3,2,1,0:T(8,128)S(1)}, f32[2,4,5,8,128]{4,3,2,1,0:T(8,128)S(1)}, f32[2,4,5,8,128]{4,3,2,1,0:T(8,128)S(1)}) custom-call(s32[3]{0:T(128)S(1)} %pad_add_fusion.me, f32[4,32,128]{2,1,0:T(8,128)S(1)} %collective-permute-done.7.weight_pair, f32[224,128]{1,0:T(8,128)S(1)} %get-tuple-element.38.rest_0_, ...), custom_call_target="tpu_custom_call" | custom-call | tf_op jit(solution)/shard_map/pallas_call | solution.py:338
  33.0 1.9 %collective-permute-start.10 = (f32[2,4,5,8,128]{4,3,2,1,0:T(8,128)S(1)}, f32[2,4,5,8,128]{4,3,2,1,0:T(8,128)S(1)}, u32[]{:S(2)}, u32[]{:S(2)}) collective-permute-start(f32[2,4,5,8,128]{4,3,2,1,0:T(8,128)S(1)} %get-tuple-element.48), channel_id=1, source_target_pairs={{0,2},{1,3},{2,0},{3,1},{4,6},{5,7},{6,4},{7,5},{8,10},{9,11},{10,... | collective-permute-start | bytes 491528 | tf_op jit(solution)/shard_map/ppermute | solution.py:353
  34.9 1.2 %collective-permute-start.11 = (f32[2,4,5,8,128]{4,3,2,1,0:T(8,128)S(1)}, f32[2,4,5,8,128]{4,3,2,1,0:T(8,128)S(1)}, u32[]{:S(2)}, u32[]{:S(2)}) collective-permute-start(f32[2,4,5,8,128]{4,3,2,1,0:T(8,128)S(1)} %get-tuple-element.49), channel_id=1, source_target_pairs={{0,4},{1,5},{2,6},{3,7},{4,0},{5,1},{6,2},{7,3},{8,12},{9,13},{10,... | collective-permute-start | bytes 491528 | tf_op jit(solution)/shard_map/ppermute | solution.py:353
  36.1 0.0 collective-permute-start.12
  36.2 0.6 shard_map.84
  36.8 0.1 collective-permute-start.20
  36.8 1.3 %collective-permute-done.10.rest_1_ = f32[2,4,5,8,128]{4,3,2,1,0:T(8,128)S(1)} collective-permute-done((f32[2,4,5,8,128]{4,3,2,1,0:T(8,128)S(1)}, f32[2,4,5,8,128]{4,3,2,1,0:T(8,128)S(1)}, u32[]{:S(2)}, u32[]{:S(2)}) %collective-permute-start.10) | collective-permute-done | bytes 163872 | tf_op jit(solution)/shard_map/ppermute | solution.py:353
  38.1 1.2 %collective-permute-done.11.rest_2_ = f32[2,4,5,8,128]{4,3,2,1,0:T(8,128)S(1)} collective-permute-done((f32[2,4,5,8,128]{4,3,2,1,0:T(8,128)S(1)}, f32[2,4,5,8,128]{4,3,2,1,0:T(8,128)S(1)}, u32[]{:S(2)}, u32[]{:S(2)}) %collective-permute-start.11) | collective-permute-done | bytes 163872 | tf_op jit(solution)/shard_map/ppermute | solution.py:353
  39.4 3.7 %collective-permute-done.12.rest_3_ = f32[2,4,5,8,128]{4,3,2,1,0:T(8,128)S(1)} collective-permute-done((f32[2,4,5,8,128]{4,3,2,1,0:T(8,128)S(1)}, f32[2,4,5,8,128]{4,3,2,1,0:T(8,128)S(1)}, u32[]{:S(2)}, u32[]{:S(2)}) %collective-permute-start.12) | collective-permute-done | bytes 163872 | tf_op jit(solution)/shard_map/ppermute | solution.py:353
  43.1 0.0 collective-permute-done.16.rest_4_.rest_2_
  43.1 1.0 %shard_map.83 = (f32[5,2,32,128]{3,2,1,0:T(8,128)S(1)}, f32[5,2,32,128]{3,2,1,0:T(8,128)S(1)}, f32[5,2,32,128]{3,2,1,0:T(8,128)S(1)}, f32[5,2,32,128]{3,2,1,0:T(8,128)S(1)}) custom-call(s32[3]{0:T(128)S(1)} %pad_add_fusion.me, s32[2,128]{1,0:T(2,128)S(1)} %get-tuple-element.43.dest, f32[2,4,5,8,128]{4,3,2,1,0:T(8,128)S(1)} %get-tuple-element.47.rest_0_.rest_4_, ...), custom_call_target="tpu_custom_call" | custom-call | tf_op jit(solution)/shard_map/pallas_call | solution.py:338
  44.1 0.6 shard_map.86
  44.7 2.3 %collective-permute-start.22 = (f32[6,2,4,8,128]{4,3,2,1,0:T(8,128)S(1)}, f32[6,2,4,8,128]{4,3,2,1,0:T(8,128)S(1)}, u32[]{:S(2)}, u32[]{:S(2)}) collective-permute-start(f32[6,2,4,8,128]{4,3,2,1,0:T(8,128)S(1)} %shard_map.86), channel_id=1, source_target_pairs={{0,8},{8,0},{16,24},{24,16},{1,9},{9,1},{17,25},{25,17},{2,10},{10... | collective-permute-start | bytes 589832 | tf_op jit(solution)/shard_map/ppermute | solution.py:353
  47.0 0.4 collective-permute-start.17
  47.3 0.2 collective-permute-start.18
  47.6 2.1 %collective-permute-start.19 = (f32[5,2,32,128]{3,2,1,0:T(8,128)S(1)}, f32[5,2,32,128]{3,2,1,0:T(8,128)S(1)}, u32[]{:S(2)}, u32[]{:S(2)}) collective-permute-start(f32[5,2,32,128]{3,2,1,0:T(8,128)S(1)} %get-tuple-element.57), channel_id=1, source_target_pairs={{0,6},{1,7},{2,4},{3,5},{4,2},{5,3},{6,0},{7,1},{8,14},{9,15},{10,... | collective-permute-start | bytes 491528 | tf_op jit(solution)/shard_map/ppermute | solution.py:353
  49.6 0.0 collective-permute-done.20.rest_4_.rest_3_
  49.6 1.8 %collective-permute-done.17.rest_1_ = f32[5,2,32,128]{3,2,1,0:T(8,128)S(1)} collective-permute-done((f32[5,2,32,128]{3,2,1,0:T(8,128)S(1)}, f32[5,2,32,128]{3,2,1,0:T(8,128)S(1)}, u32[]{:S(2)}, u32[]{:S(2)}) %collective-permute-start.17) | collective-permute-done | bytes 163872 | tf_op jit(solution)/shard_map/ppermute | solution.py:353
  51.4 2.1 %collective-permute-done.18.rest_2_ = f32[5,2,32,128]{3,2,1,0:T(8,128)S(1)} collective-permute-done((f32[5,2,32,128]{3,2,1,0:T(8,128)S(1)}, f32[5,2,32,128]{3,2,1,0:T(8,128)S(1)}, u32[]{:S(2)}, u32[]{:S(2)}) %collective-permute-start.18) | collective-permute-done | bytes 163872 | tf_op jit(solution)/shard_map/ppermute | solution.py:353
  53.6 0.0 collective-permute-done.19.rest_3_
  53.6 1.0 %shard_map.85 = (f32[640,128]{1,0:T(8,128)S(1)}, f32[640,128]{1,0:T(8,128)S(1)}) custom-call(s32[3]{0:T(128)S(1)} %pad_add_fusion.me, f32[5,32,32]{2,1,0:T(8,128)S(1)} %get-tuple-element.33.inverse, f32[5,2,32,128]{3,2,1,0:T(8,128)S(1)} %get-tuple-element.54.rest_0_.rest_4_, f32[5,2,32,128]{3,2,1,0:T(8,128)S(1)} %collective-permute-done.17.rest_1_, ...), custom_call_target="tpu_custom_call" | custom-call | tf_op jit(solution)/shard_map/pallas_call | solution.py:338
  54.6 4.0 %collective-permute-start.21 = (f32[640,128]{1,0:T(8,128)S(1)}, f32[640,128]{1,0:T(8,128)S(1)}, u32[]{:S(2)}, u32[]{:S(2)}) collective-permute-start(f32[640,128]{1,0:T(8,128)S(1)} %get-tuple-element.60.rest_4_), channel_id=1, source_target_pairs={{0,1},{1,0},{2,3},{3,2},{4,5},{5,4},{6,7},{7,6},{8,9},{9,8},{10,11... | collective-permute-start | bytes 983048 | tf_op jit(solution)/shard_map/ppermute | solution.py:353
  58.5 0.0 collective-permute-done.22.rest_1_
  58.5 1.0 %shard_map.87 = (f32[4,5,32,128]{3,2,1,0:T(8,128)S(1)}, f32[4,5,32,128]{3,2,1,0:T(8,128)S(1)}) custom-call(s32[3]{0:T(128)S(1)} %pad_add_fusion.me, f32[8,128]{1,0:T(8,128)S(1)} %get-tuple-element.35.mine, f32[8,128]{1,0:T(8,128)S(1)} %collective-permute-done.1.rest_4_.mine_pair, f32[6,2,4,8,128]{4,3,2,1,0:T(8,128)S(1)} %get-tuple-element.61.rest_0_, ...), custom_call_target="tpu_custom_call" | custom-call | tf_op jit(solution)/shard_map/pallas_call | solution.py:338
  59.6 0.1 collective-permute-start.23
  59.7 0.1 collective-permute-done.21
  59.8 0.8 %add.12 = f32[640,128]{1,0:T(8,128)} add(f32[640,128]{1,0:T(8,128)S(1)} %get-tuple-element.59, f32[640,128]{1,0:T(8,128)S(1)} %collective-permute-done.21) | non-fusion elementwise | flops 81920 | bytes 983040 | tf_op jit(solution)/shard_map/add | solution.py:487
  60.6 0.7 %collective-permute-done.23 = f32[4,5,32,128]{3,2,1,0:T(8,128)S(1)} collective-permute-done((f32[4,5,32,128]{3,2,1,0:T(8,128)S(1)}, f32[4,5,32,128]{3,2,1,0:T(8,128)S(1)}, u32[]{:S(2)}, u32[]{:S(2)}) %collective-permute-start.23) | collective-permute-done | bytes 327712 | tf_op jit(solution)/shard_map/ppermute | solution.py:353
  61.3 0.8 %add_bitcast_fusion = f32[1,4,32,5,128]{4,2,3,1,0:T(8,128)} fusion(f32[4,5,32,128]{3,2,1,0:T(8,128)S(1)} %get-tuple-element.62, f32[4,5,32,128]{3,2,1,0:T(8,128)S(1)} %collective-permute-done.23), kind=kLoop, calls=%fused_computation | loop fusion | flops 81920 | bytes 983040 | tf_op jit(solution)/shard_map/broadcast_in_dim | solution.py:489
Async XLA Ops:
  0.6 4.0 %collective-permute-start.2 = (f32[640,128]{1,0:T(8,128)}, f32[640,128]{1,0:T(8,128)S(1)}, u32[]{:S(2)}, u32[]{:S(2)}) collective-permute-start(f32[640,128]{1,0:T(8,128)} %bitcast.25), channel_id=1, source_target_pairs={{0,1},{1,0},{2,3},{3,2},{4,5},{5,4},{6,7},{7,6},{8,9},{9,8},{10,11... | collective-permute-start | bytes 983048 | tf_op jit(solution)/shard_map/ppermute | solution.py:353
  2.6 15.2 %collective-permute-start = (f32[648,128]{1,0:T(8,128)S(1)}, f32[648,128]{1,0:T(8,128)S(1)}, u32[]{:S(2)}, u32[]{:S(2)}) collective-permute-start(f32[648,128]{1,0:T(8,128)S(1)} %get-tuple-element.34.rest_4_), channel_id=1, source_target_pairs={{0,16},{8,24},{16,0},{24,8},{1,17},{9,25},{17,1},{25,9},{2,18},{10... | collective-permute-start | bytes 995336 | tf_op jit(solution)/shard_map/ppermute | solution.py:353
  2.6 16.4 %collective-permute-start.6 = (f32[648,128]{1,0:T(8,128)S(1)}, f32[648,128]{1,0:T(8,128)S(1)}, u32[]{:S(2)}, u32[]{:S(2)}) collective-permute-start(f32[648,128]{1,0:T(8,128)S(1)} %get-tuple-element.34.rest_4_), channel_id=1, source_target_pairs={{0,8},{8,0},{16,24},{24,16},{1,9},{9,1},{17,25},{25,17},{2,10},{10... | collective-permute-start | bytes 995336 | tf_op jit(solution)/shard_map/ppermute | solution.py:353
  4.0 4.2 %collective-permute-start.1 = (f32[8,128]{1,0:T(8,128)S(1)}, f32[8,128]{1,0:T(8,128)S(1)}, u32[]{:S(2)}, u32[]{:S(2)}) collective-permute-start(f32[8,128]{1,0:T(8,128)S(1)} %get-tuple-element.35.mine), channel_id=1, source_target_pairs={{0,1},{1,0},{2,3},{3,2},{4,5},{5,4},{6,7},{7,6},{8,9},{9,8},{10,11... | collective-permute-start | bytes 12296 | tf_op jit(solution)/shard_map/ppermute | solution.py:353
  5.7 4.8 %collective-permute-start.3 = (f32[224,128]{1,0:T(8,128)S(1)}, f32[224,128]{1,0:T(8,128)S(1)}, u32[]{:S(2)}, u32[]{:S(2)}) collective-permute-start(f32[224,128]{1,0:T(8,128)S(1)} %get-tuple-element.39), channel_id=1, source_target_pairs={{0,2},{1,3},{2,0},{3,1},{4,6},{5,7},{6,4},{7,5},{8,10},{9,11},{10,... | collective-permute-start | bytes 344072 | tf_op jit(solution)/shard_map/ppermute | solution.py:353
  7.0 5.8 %collective-permute-start.4 = (f32[224,128]{1,0:T(8,128)S(1)}, f32[224,128]{1,0:T(8,128)S(1)}, u32[]{:S(2)}, u32[]{:S(2)}) collective-permute-start(f32[224,128]{1,0:T(8,128)S(1)} %get-tuple-element.40), channel_id=1, source_target_pairs={{0,4},{1,5},{2,6},{3,7},{4,0},{5,1},{6,2},{7,3},{8,12},{9,13},{10,... | collective-permute-start | bytes 344072 | tf_op jit(solution)/shard_map/ppermute | solution.py:353
  8.2 5.2 %collective-permute-start.5 = (f32[224,128]{1,0:T(8,128)S(1)}, f32[224,128]{1,0:T(8,128)S(1)}, u32[]{:S(2)}, u32[]{:S(2)}) collective-permute-start(f32[224,128]{1,0:T(8,128)S(1)} %get-tuple-element.41), channel_id=1, source_target_pairs={{0,6},{1,7},{2,4},{3,5},{4,2},{5,3},{6,0},{7,1},{8,14},{9,15},{10,... | collective-permute-start | bytes 344072 | tf_op jit(solution)/shard_map/ppermute | solution.py:353
  14.7 8.3 %collective-permute-start.13 = (f32[2,4,6,8,128]{4,3,2,1,0:T(8,128)S(1)}, f32[2,4,6,8,128]{4,3,2,1,0:T(8,128)S(1)}, u32[]{:S(2)}, u32[]{:S(2)}) collective-permute-start(f32[2,4,6,8,128]{4,3,2,1,0:T(8,128)S(1)} %get-tuple-element.51), channel_id=1, source_target_pairs={{0,2},{1,3},{2,0},{3,1},{4,6},{5,7},{6,4},{7,5},{8,10},{9,11},{10,... | collective-permute-start | bytes 589832 | tf_op jit(solution)/shard_map/ppermute | solution.py:353
  16.5 7.4 %collective-permute-start.14 = (f32[2,4,6,8,128]{4,3,2,1,0:T(8,128)S(1)}, f32[2,4,6,8,128]{4,3,2,1,0:T(8,128)S(1)}, u32[]{:S(2)}, u32[]{:S(2)}) collective-permute-start(f32[2,4,6,8,128]{4,3,2,1,0:T(8,128)S(1)} %get-tuple-element.52), channel_id=1, source_target_pairs={{0,4},{1,5},{2,6},{3,7},{4,0},{5,1},{6,2},{7,3},{8,12},{9,13},{10,... | collective-permute-start | bytes 589832 | tf_op jit(solution)/shard_map/ppermute | solution.py:353
  16.7 8.9 %collective-permute-start.15 = (f32[2,4,6,8,128]{4,3,2,1,0:T(8,128)S(1)}, f32[2,4,6,8,128]{4,3,2,1,0:T(8,128)S(1)}, u32[]{:S(2)}, u32[]{:S(2)}) collective-permute-start(f32[2,4,6,8,128]{4,3,2,1,0:T(8,128)S(1)} %get-tuple-element.53), channel_id=1, source_target_pairs={{0,6},{1,7},{2,4},{3,5},{4,2},{5,3},{6,0},{7,1},{8,14},{9,15},{10,... | collective-permute-start | bytes 589832 | tf_op jit(solution)/shard_map/ppermute | solution.py:353
  20.3 11.5 %collective-permute-start.9 = (f32[328,128]{1,0:T(8,128)S(1)}, f32[328,128]{1,0:T(8,128)S(1)}, u32[]{:S(2)}, u32[]{:S(2)}) collective-permute-start(f32[328,128]{1,0:T(8,128)S(1)} %get-tuple-element.46), channel_id=1, source_target_pairs={{0,8},{8,0},{16,24},{24,16},{1,9},{9,1},{17,25},{25,17},{2,10},{10... | collective-permute-start | bytes 503816 | tf_op jit(solution)/shard_map/ppermute | solution.py:353
  22.9 8.9 %collective-permute-start.8 = (f32[320,128]{1,0:T(8,128)S(1)}, f32[320,128]{1,0:T(8,128)S(1)}, u32[]{:S(2)}, u32[]{:S(2)}) collective-permute-start(f32[320,128]{1,0:T(8,128)S(1)} %get-tuple-element.45), channel_id=1, source_target_pairs={{0,8},{8,0},{16,24},{24,16},{1,9},{9,1},{17,25},{25,17},{2,10},{10... | collective-permute-start | bytes 491528 | tf_op jit(solution)/shard_map/ppermute | solution.py:353
  22.9 5.7 %collective-permute-start.7 = (f32[4,32,128]{2,1,0:T(8,128)S(1)}, f32[4,32,128]{2,1,0:T(8,128)S(1)}, u32[]{:S(2)}, u32[]{:S(2)}) collective-permute-start(f32[4,32,128]{2,1,0:T(8,128)S(1)} %get-tuple-element.44), channel_id=1, source_target_pairs={{0,1},{1,0},{2,3},{3,2},{4,5},{5,4},{6,7},{7,6},{8,9},{9,8},{10,11... | collective-permute-start | bytes 196616 | tf_op jit(solution)/shard_map/ppermute | solution.py:353
  26.2 16.9 %collective-permute-start.16 = (f32[6,2,4,8,128]{4,3,2,1,0:T(8,128)S(1)}, f32[6,2,4,8,128]{4,3,2,1,0:T(8,128)S(1)}, u32[]{:S(2)}, u32[]{:S(2)}) collective-permute-start(f32[6,2,4,8,128]{4,3,2,1,0:T(8,128)S(1)} %shard_map.82), channel_id=1, source_target_pairs={{0,16},{8,24},{16,0},{24,8},{1,17},{9,25},{17,1},{25,9},{2,18},{10... | collective-permute-start | bytes 589832 | tf_op jit(solution)/shard_map/ppermute | solution.py:353
  33.0 5.2 %collective-permute-start.10 = (f32[2,4,5,8,128]{4,3,2,1,0:T(8,128)S(1)}, f32[2,4,5,8,128]{4,3,2,1,0:T(8,128)S(1)}, u32[]{:S(2)}, u32[]{:S(2)}) collective-permute-start(f32[2,4,5,8,128]{4,3,2,1,0:T(8,128)S(1)} %get-tuple-element.48), channel_id=1, source_target_pairs={{0,2},{1,3},{2,0},{3,1},{4,6},{5,7},{6,4},{7,5},{8,10},{9,11},{10,... | collective-permute-start | bytes 491528 | tf_op jit(solution)/shard_map/ppermute | solution.py:353
  34.9 4.5 %collective-permute-start.11 = (f32[2,4,5,8,128]{4,3,2,1,0:T(8,128)S(1)}, f32[2,4,5,8,128]{4,3,2,1,0:T(8,128)S(1)}, u32[]{:S(2)}, u32[]{:S(2)}) collective-permute-start(f32[2,4,5,8,128]{4,3,2,1,0:T(8,128)S(1)} %get-tuple-element.49), channel_id=1, source_target_pairs={{0,4},{1,5},{2,6},{3,7},{4,0},{5,1},{6,2},{7,3},{8,12},{9,13},{10,... | collective-permute-start | bytes 491528 | tf_op jit(solution)/shard_map/ppermute | solution.py:353
  36.1 7.0 %collective-permute-start.12 = (f32[2,4,5,8,128]{4,3,2,1,0:T(8,128)S(1)}, f32[2,4,5,8,128]{4,3,2,1,0:T(8,128)S(1)}, u32[]{:S(2)}, u32[]{:S(2)}) collective-permute-start(f32[2,4,5,8,128]{4,3,2,1,0:T(8,128)S(1)} %get-tuple-element.50), channel_id=1, source_target_pairs={{0,6},{1,7},{2,4},{3,5},{4,2},{5,3},{6,0},{7,1},{8,14},{9,15},{10,... | collective-permute-start | bytes 491528 | tf_op jit(solution)/shard_map/ppermute | solution.py:353
  36.8 12.8 %collective-permute-start.20 = (f32[6,2,4,8,128]{4,3,2,1,0:T(8,128)S(1)}, f32[6,2,4,8,128]{4,3,2,1,0:T(8,128)S(1)}, u32[]{:S(2)}, u32[]{:S(2)}) collective-permute-start(f32[6,2,4,8,128]{4,3,2,1,0:T(8,128)S(1)} %get-tuple-element.58), channel_id=1, source_target_pairs={{0,24},{8,16},{16,8},{24,0},{1,25},{9,17},{17,9},{25,1},{2,26},{10... | collective-permute-start | bytes 589832 | tf_op jit(solution)/shard_map/ppermute | solution.py:353
  44.7 13.8 %collective-permute-start.22 = (f32[6,2,4,8,128]{4,3,2,1,0:T(8,128)S(1)}, f32[6,2,4,8,128]{4,3,2,1,0:T(8,128)S(1)}, u32[]{:S(2)}, u32[]{:S(2)}) collective-permute-start(f32[6,2,4,8,128]{4,3,2,1,0:T(8,128)S(1)} %shard_map.86), channel_id=1, source_target_pairs={{0,8},{8,0},{16,24},{24,16},{1,9},{9,1},{17,25},{25,17},{2,10},{10... | collective-permute-start | bytes 589832 | tf_op jit(solution)/shard_map/ppermute | solution.py:353
  47.0 4.5 %collective-permute-start.17 = (f32[5,2,32,128]{3,2,1,0:T(8,128)S(1)}, f32[5,2,32,128]{3,2,1,0:T(8,128)S(1)}, u32[]{:S(2)}, u32[]{:S(2)}) collective-permute-start(f32[5,2,32,128]{3,2,1,0:T(8,128)S(1)} %get-tuple-element.55), channel_id=1, source_target_pairs={{0,2},{1,3},{2,0},{3,1},{4,6},{5,7},{6,4},{7,5},{8,10},{9,11},{10,... | collective-permute-start | bytes 491528 | tf_op jit(solution)/shard_map/ppermute | solution.py:353
  47.3 6.2 %collective-permute-start.18 = (f32[5,2,32,128]{3,2,1,0:T(8,128)S(1)}, f32[5,2,32,128]{3,2,1,0:T(8,128)S(1)}, u32[]{:S(2)}, u32[]{:S(2)}) collective-permute-start(f32[5,2,32,128]{3,2,1,0:T(8,128)S(1)} %get-tuple-element.56), channel_id=1, source_target_pairs={{0,4},{1,5},{2,6},{3,7},{4,0},{5,1},{6,2},{7,3},{8,12},{9,13},{10,... | collective-permute-start | bytes 491528 | tf_op jit(solution)/shard_map/ppermute | solution.py:353
  47.6 6.0 %collective-permute-start.19 = (f32[5,2,32,128]{3,2,1,0:T(8,128)S(1)}, f32[5,2,32,128]{3,2,1,0:T(8,128)S(1)}, u32[]{:S(2)}, u32[]{:S(2)}) collective-permute-start(f32[5,2,32,128]{3,2,1,0:T(8,128)S(1)} %get-tuple-element.57), channel_id=1, source_target_pairs={{0,6},{1,7},{2,4},{3,5},{4,2},{5,3},{6,0},{7,1},{8,14},{9,15},{10,... | collective-permute-start | bytes 491528 | tf_op jit(solution)/shard_map/ppermute | solution.py:353
  54.6 5.2 %collective-permute-start.21 = (f32[640,128]{1,0:T(8,128)S(1)}, f32[640,128]{1,0:T(8,128)S(1)}, u32[]{:S(2)}, u32[]{:S(2)}) collective-permute-start(f32[640,128]{1,0:T(8,128)S(1)} %get-tuple-element.60.rest_4_), channel_id=1, source_target_pairs={{0,1},{1,0},{2,3},{3,2},{4,5},{5,4},{6,7},{7,6},{8,9},{9,8},{10,11... | collective-permute-start | bytes 983048 | tf_op jit(solution)/shard_map/ppermute | solution.py:353
  59.6 1.7 %collective-permute-start.23 = (f32[4,5,32,128]{3,2,1,0:T(8,128)S(1)}, f32[4,5,32,128]{3,2,1,0:T(8,128)S(1)}, u32[]{:S(2)}, u32[]{:S(2)}) collective-permute-start(f32[4,5,32,128]{3,2,1,0:T(8,128)S(1)} %get-tuple-element.63), channel_id=1, source_target_pairs={{0,1},{1,0},{2,3},{3,2},{4,5},{5,4},{6,7},{7,6},{8,9},{9,8},{10,11... | collective-permute-start | bytes 983048 | tf_op jit(solution)/shard_map/ppermute | solution.py:353

commit v4 on v3

--- a/solution.py
+++ b/solution.py
@@ -19,20 +19,16 @@
 
 
 def pick(table, values, contract):
-    dims = ((contract, (0,)), ((), ()))
-    high, low = two_parts(values)
-    return SHORT(table, low, dims) + SHORT(table, high, dims)
+    table = jnp.concatenate([table, table], axis=contract[0])
+    return SHORT(table, jnp.concatenate(two_parts(values), axis=0), ((contract, (0,)), ((), ())))
 
 
 def product(left, right, contract):
-    dims = ((contract, (0,)), ((), ()))
     left_high, left_low = two_parts(left)
     right_high, right_low = two_parts(right)
-    return (
-        SHORT(left_low, right_high, dims)
-        + SHORT(left_high, right_low, dims)
-        + SHORT(left_high, right_high, dims)
-    )
+    left = jnp.concatenate([left_high, left_low, left_high], axis=contract[0])
+    right = jnp.concatenate([right_high, right_high, right_low], axis=0)
+    return SHORT(left, right, ((contract, (0,)), ((), ())))
 
 
 def hot(rows, wanted):
@@ -49,8 +45,9 @@
 
 def pack_kernel(dims, state, source_in, dest_in, cot_in, weight_in, inverse_in, *rest):
     lats, slabs, chips, cap, lev_dev, here, fields = dims
-    out, mine, cot, weight, inverse, source, dest, sems = rest
+    out, second_half, mine, cot, weight, inverse, source, dest, sems = rest
     total = state.shape[0]
+    cut = out.shape[0] - second_half.shape[0]
     copies = [
         pltpu.make_async_copy(src, dst, sems.at[i])
         for i, (src, dst) in enumerate(
@@ -58,6 +55,7 @@
                 (source_in, source),
                 (dest_in, dest),
                 (state, out.at[pl.ds(0, total)]),
+                (state.at[pl.ds(cut, total - cut)], second_half.at[pl.ds(0, total - cut)]),
                 (cot_in, cot),
                 (weight_in, weight),
                 (inverse_in, inverse),
@@ -80,6 +78,7 @@
     for g in range(lats):
         lanes = jnp.where(chosen, wide[g * slabs : (g + 1) * slabs], 0.0)
         out[total + g : total + g + 1, :slots] = jnp.sum(lanes, axis=0, keepdims=True)
+    second_half[total - cut :, :] = out[total:, :]
     slots = lats * chips * cap
     row = iota((lats * slabs, slots), 0)
     at = iota((lats * slabs, slots), 1)
@@ -218,19 +217,13 @@
 
 def hold_kernel(dims, me, array, mine, mine_pair, *rest):
     lats, slabs, chips, cap, lev_dev, here, fields = dims
-    out, second, dests, sems = rest[-4:]
-    cut = out.shape[0]
-    copies = [
-        pltpu.make_async_copy(array.at[pl.ds(0, cut)], out, sems.at[0]),
-        pltpu.make_async_copy(array.at[pl.ds(cut, second.shape[0])], second, sems.at[1]),
-    ]
-    for copy in copies:
-        copy.start()
+    out, dests, sem = rest[-3:]
+    copy = pltpu.make_async_copy(array.at[pl.ds(0, out.shape[0])], out, sem)
+    copy.start()
     total = dests.shape[1]
     both = jnp.concatenate([mine[2:3, :total], mine_pair[2:3, :total]], axis=0)
     dests[...] = by_column_owner(both, lev_dev, chips, 2 * here)
-    for copy in copies:
-        copy.wait()
+    copy.wait()
 
 
 def mix_kernel(dims, me, weight_pair, *rest):
@@ -380,7 +373,8 @@
     inverse = diffusion_inverse[0]
     dest = dest_slot[0]
 
-    packed, mine, cot_here, weights_here, inverse_here = call(
+    cut = row_total * fields // 2
+    packed, second_half, mine, cot_here, weights_here, inverse_here = call(
         pack_kernel,
         dims,
         [
@@ -389,6 +383,7 @@
         ],
         [
             (row_total * fields + -(-lats // 8) * 8, width),
+            (row_total * fields + -(-lats // 8) * 8 - cut, width),
             (8, max(row_total, lats * chips * cap)),
             cot.shape,
             weights.shape,
@@ -397,7 +392,7 @@
         [
             pltpu.VMEM((lats, slabs, cap), jnp.int32),
             pltpu.VMEM(dest.shape, jnp.int32),
-            pltpu.SemaphoreType.DMA((6,)),
+            pltpu.SemaphoreType.DMA((7,)),
         ],
         outside=True,
         limit=48,
@@ -421,34 +416,35 @@
         [(row_total, (fields + 1) * width), (chips, 2, lats, fields + 1, cap, width)],
         after=[mine_pair],
     )
-    cut = row_total * fields // 2
-    first_half, second_half, dests = call(
+    opposite = swap(second_half, "lat", 3, lats)
+    first_half, dests = call(
         hold_kernel,
         dims,
         (me, far, mine, mine_pair),
-        [(cut, width), (packed.shape[0] - cut, width), jax.ShapeDtypeStruct((2, row_total), jnp.int32)],
-        [pltpu.SemaphoreType.DMA((2,))],
+        [(cut, width), jax.ShapeDtypeStruct((2, row_total), jnp.int32)],
+        [pltpu.SemaphoreType.DMA(())],
         after=[slot_back[0], near],
     )
     slot_back = over_chips(slot_back)
     states = []
     for j in range(lats):
         if forwarded(j):
-            halves = (first_half, second_half) if j == 3 else (states[-1][:cut], states[-1][cut:])
-            states += [swap(half, "lat", 1, lats) for half in halves]
+            states.append(swap(first_half if j == 3 else states[-1][:cut], "lat", 1, lats))
+            states.append(opposite if j == 3 else swap(second_half, "lat", j, lats))
         else:
             states.append({0: packed, 1: near, 2: far}[j] if j < 3 else swap(packed, "lat", j, lats))
+    soon = [j for j in range(lats) if j == 2]
+    late = [j for j in range(lats) if j != 2]
+    message = (fields + 1, 2, chips, cap, width)
+    sorted_soon = call(functools.partial(sort_kernel, soon), dims, (me, *slot_back), [message] * len(soon))
     mixed = call(
         mix_kernel,
         dims,
         (me, pair(weight_other), *first, *states),
         [(2, lats, fields, cap, width)] * chips,
         [(lats, 2, chips, cap, width), (2, chips, fields, cap, width)],
-    )
-    soon = [j for j in range(lats) if j == 2]
-    late = [j for j in range(lats) if j not in (1, 2)]
-    message = (fields + 1, 2, chips, cap, width)
-    sorted_soon = call(functools.partial(sort_kernel, soon), dims, (me, *slot_back), [message] * len(soon))
+        after=sorted_soon,
+    )
     sorted_late = call(
         functools.partial(sort_kernel, late), dims, (me, *slot_back), [message] * len(late), after=mixed[:1]
     )
@@ -463,25 +459,22 @@
         [(fields, lats * chips, cap, width), (chips, fields, span, width)],
         after=returned[2:3],
     )
-    (sorted_last,) = call(
-        functools.partial(sort_kernel, [1]), dims, (me, *slot_back), [message], after=moved[:1]
-    )
-    returned[1] = swap(sorted_last, "lat", 1, lats)
-    tangent, tangent_pair = call(
-        diffuse_kernel,
-        dims,
-        (me, inverse_here, *over_chips(moved)),
-        [cot.shape, cot.shape],
-        [(fields, levels * 2 * here, width)],
-        after=returned[3:4],
-    )
+    moved = over_chips(moved)
     adjoint, adjoint_pair = call(
         add_kernel,
         dims,
         (me, mine, mine_pair, *returned),
         [(lev_dev, fields, blocks, width)] * 2,
         [(fields + 1, lats, chips, cap, width)],
-        after=[tangent_pair],
+        after=moved[1:2],
+    )
+    tangent, tangent_pair = call(
+        diffuse_kernel,
+        dims,
+        (me, inverse_here, *moved),
+        [cot.shape, cot.shape],
+        [(fields, levels * 2 * here, width)],
+        after=[adjoint_pair],
     )
     adjoint = adjoint + pair(adjoint_pair)
     tangent = tangent + pair(tangent_pair)

time: 62.3 us -> 59.4 us (0.953)
  the two profiles are of different devices: /device:TPU:17 before, /device:TPU:0 now
where the time goes in v4:
time: 59.4 us; the launch traced here: 59.2 us
  starting transfers between devices  25.3 us (43%)
  waiting for transfers between devices  22.2 us (37%)
  Pallas kernels  9.33 us (16%)
  other arithmetic  1.6 us (3%)
  between operations  0.74 us (1%)
    ppermute x24, starting transfers between devices, swap(): return lax.ppermute(array, axis, [(i, i ^ bit) for i in range(count)])  25.3 us
    ppermute x24, waiting for transfers between devices, swap(): return lax.ppermute(array, axis, [(i, i ^ bit) for i in range(count)])  22.2 us
    pallas_call x10, Pallas kernels, call(): pl.pallas_call(functools.partial(kernel, dims), out_shape=[shape if hasat...  9.33 us
  transfers between devices with their start and end apart: 24, of which 11 were waited for; matrix products, arithmetic and copies ran while one was open for 1% of the time, Pallas kernels for 14%

profile of v4, /device:TPU:0, one launch (start us, length us, event | category | flops | bytes accessed | tf_op | source)
XLA Modules:
  0.0 59.2 jit_solution(10303067937084216900)
XLA Ops:
  0.6 0.5 collective-permute-start.2
  1.1 1.3 %shard_map.77 = (f32[648,128]{1,0:T(8,128)S(1)}, f32[328,128]{1,0:T(8,128)S(1)}, f32[8,128]{1,0:T(8,128)S(1)}, f32[640,128]{1,0:T(8,128)S(1)}, f32[128,128]{1,0:T(8,128)S(1)}, /*index=5*/f32[5,32,32]{2,1,0:T(8,128)S(1)}) custom-call(f32[640,128]{1,0:T(8,128)} %bitcast.24, s32[4,8,8]{2,1,0:T(8,128)} %bitcast.30, s32[1,128]{1,0:T(1,128)} %bitcast.31, ...), custom_call_target="tpu_custom_call" | custom-call | tf_op jit(solution)/shard_map/pallas_call | solution.py:331
  2.4 2.7 %collective-permute-start.6 = (f32[648,128]{1,0:T(8,128)S(1)}, f32[648,128]{1,0:T(8,128)S(1)}, u32[]{:S(2)}, u32[]{:S(2)}) collective-permute-start(f32[648,128]{1,0:T(8,128)S(1)} %get-tuple-element.35.rest_4_), channel_id=1, source_target_pairs={{0,8},{8,0},{16,24},{24,16},{1,9},{9,1},{17,25},{25,17},{2,10},{10... | collective-permute-start | bytes 995336 | tf_op jit(solution)/shard_map/ppermute | solution.py:346
  5.1 2.6 %collective-permute-start = (f32[648,128]{1,0:T(8,128)S(1)}, f32[648,128]{1,0:T(8,128)S(1)}, u32[]{:S(2)}, u32[]{:S(2)}) collective-permute-start(f32[648,128]{1,0:T(8,128)S(1)} %get-tuple-element.35.rest_4_), channel_id=1, source_target_pairs={{0,16},{8,24},{16,0},{24,8},{1,17},{9,25},{17,1},{25,9},{2,18},{10... | collective-permute-start | bytes 995336 | tf_op jit(solution)/shard_map/ppermute | solution.py:346
  7.7 0.0 collective-permute-start.1
  7.7 0.1 pad_add_fusion.me
  7.8 0.0 collective-permute-done.2.cot_pair
  7.8 0.9 %shard_map.78 = (f32[224,128]{1,0:T(8,128)S(1)}, f32[224,128]{1,0:T(8,128)S(1)}, f32[224,128]{1,0:T(8,128)S(1)}, f32[224,128]{1,0:T(8,128)S(1)}) custom-call(s32[3]{0:T(128)S(1)} %pad_add_fusion.me, f32[640,128]{1,0:T(8,128)S(1)} %get-tuple-element.38.cot, f32[5,32,32]{2,1,0:T(8,128)S(1)} %get-tuple-element.34.inverse, ...), custom_call_target="tpu_custom_call" | custom-call | tf_op jit(solution)/shard_map/pallas_call | solution.py:331
  8.7 1.6 %collective-permute-start.3 = (f32[224,128]{1,0:T(8,128)S(1)}, f32[224,128]{1,0:T(8,128)S(1)}, u32[]{:S(2)}, u32[]{:S(2)}) collective-permute-start(f32[224,128]{1,0:T(8,128)S(1)} %get-tuple-element.40), channel_id=1, source_target_pairs={{0,2},{1,3},{2,0},{3,1},{4,6},{5,7},{6,4},{7,5},{8,10},{9,11},{10,... | collective-permute-start | bytes 344072 | tf_op jit(solution)/shard_map/ppermute | solution.py:346
  10.3 1.5 %collective-permute-start.4 = (f32[224,128]{1,0:T(8,128)S(1)}, f32[224,128]{1,0:T(8,128)S(1)}, u32[]{:S(2)}, u32[]{:S(2)}) collective-permute-start(f32[224,128]{1,0:T(8,128)S(1)} %get-tuple-element.41), channel_id=1, source_target_pairs={{0,4},{1,5},{2,6},{3,7},{4,0},{5,1},{6,2},{7,3},{8,12},{9,13},{10,... | collective-permute-start | bytes 344072 | tf_op jit(solution)/shard_map/ppermute | solution.py:346
  11.8 0.0 collective-permute-done.1.rest_4_.mine_pair
  11.8 0.5 collective-permute-start.5
  12.3 2.1 %collective-permute-done.3.rest_1_ = f32[224,128]{1,0:T(8,128)S(1)} collective-permute-done((f32[224,128]{1,0:T(8,128)S(1)}, f32[224,128]{1,0:T(8,128)S(1)}, u32[]{:S(2)}, u32[]{:S(2)}) %collective-permute-start.3) | collective-permute-done | bytes 114720 | tf_op jit(solution)/shard_map/ppermute | solution.py:346
  14.3 3.7 %collective-permute-done.4.rest_2_ = f32[224,128]{1,0:T(8,128)S(1)} collective-permute-done((f32[224,128]{1,0:T(8,128)S(1)}, f32[224,128]{1,0:T(8,128)S(1)}, u32[]{:S(2)}, u32[]{:S(2)}) %collective-permute-start.4) | collective-permute-done | bytes 114720 | tf_op jit(solution)/shard_map/ppermute | solution.py:346
  18.0 0.0 collective-permute-done.5.rest_3_
  18.0 1.1 %shard_map.79 = (f32[2,4,6,8,128]{4,3,2,1,0:T(8,128)S(1)}, f32[2,4,6,8,128]{4,3,2,1,0:T(8,128)S(1)}, f32[2,4,6,8,128]{4,3,2,1,0:T(8,128)S(1)}, f32[2,4,6,8,128]{4,3,2,1,0:T(8,128)S(1)}, f32[4,32,128]{2,1,0:T(8,128)S(1)}) custom-call(s32[3]{0:T(128)S(1)} %pad_add_fusion.me, f32[8,128]{1,0:T(8,128)S(1)} %get-tuple-element.36.mine, ...), custom_call_target="tpu_custom_call" | custom-call | tf_op jit(solution)/shard_map/pallas_call | solution.py:331
  19.1 1.3 %collective-permute-start.10 = (f32[2,4,6,8,128]{4,3,2,1,0:T(8,128)S(1)}, f32[2,4,6,8,128]{4,3,2,1,0:T(8,128)S(1)}, u32[]{:S(2)}, u32[]{:S(2)}) collective-permute-start(f32[2,4,6,8,128]{4,3,2,1,0:T(8,128)S(1)} %get-tuple-element.48), channel_id=1, source_target_pairs={{0,2},{1,3},{2,0},{3,1},{4,6},{5,7},{6,4},{7,5},{8,10},{9,11},{10,... | collective-permute-start | bytes 589832 | tf_op jit(solution)/shard_map/ppermute | solution.py:346
  20.4 0.8 %collective-permute-start.11 = (f32[2,4,6,8,128]{4,3,2,1,0:T(8,128)S(1)}, f32[2,4,6,8,128]{4,3,2,1,0:T(8,128)S(1)}, u32[]{:S(2)}, u32[]{:S(2)}) collective-permute-start(f32[2,4,6,8,128]{4,3,2,1,0:T(8,128)S(1)} %get-tuple-element.49), channel_id=1, source_target_pairs={{0,4},{1,5},{2,6},{3,7},{4,0},{5,1},{6,2},{7,3},{8,12},{9,13},{10,... | collective-permute-start | bytes 589832 | tf_op jit(solution)/shard_map/ppermute | solution.py:346
  21.2 1.4 %collective-permute-start.12 = (f32[2,4,6,8,128]{4,3,2,1,0:T(8,128)S(1)}, f32[2,4,6,8,128]{4,3,2,1,0:T(8,128)S(1)}, u32[]{:S(2)}, u32[]{:S(2)}) collective-permute-start(f32[2,4,6,8,128]{4,3,2,1,0:T(8,128)S(1)} %get-tuple-element.50), channel_id=1, source_target_pairs={{0,6},{1,7},{2,4},{3,5},{4,2},{5,3},{6,0},{7,1},{8,14},{9,15},{10,... | collective-permute-start | bytes 589832 | tf_op jit(solution)/shard_map/ppermute | solution.py:346
  22.6 0.0 collective-permute-done.6.rest_1_.rest_5_
  22.6 0.5 collective-permute-start.9
  23.2 0.0 collective-permute-done.array.rest_6_
  23.2 0.9 %shard_map.80 = (f32[320,128]{1,0:T(8,128)S(1)}, s32[2,128]{1,0:T(2,128)S(1)}) custom-call(s32[3]{0:T(128)S(1)} %pad_add_fusion.me, f32[648,128]{1,0:T(8,128)S(1)} %collective-permute-done.array.rest_6_, f32[8,128]{1,0:T(8,128)S(1)} %get-tuple-element.36.mine, f32[8,128]{1,0:T(8,128)S(1)} %collective-permute-done.1.rest_4_.mine_pair, ...), custom_call_target="tpu_custom_call" | custom-call | tf_op jit(solution)/shard_map/pallas_call | solution.py:331
  24.1 0.4 collective-permute-start.8
  24.6 2.2 %collective-permute-done.10.rest_1_ = f32[2,4,6,8,128]{4,3,2,1,0:T(8,128)S(1)} collective-permute-done((f32[2,4,6,8,128]{4,3,2,1,0:T(8,128)S(1)}, f32[2,4,6,8,128]{4,3,2,1,0:T(8,128)S(1)}, u32[]{:S(2)}, u32[]{:S(2)}) %collective-permute-start.10) | collective-permute-done | bytes 196640 | tf_op jit(solution)/shard_map/ppermute | solution.py:346
  26.8 0.0 collective-permute-start.7
  26.8 4.1 %collective-permute-done.11.rest_2_ = f32[2,4,6,8,128]{4,3,2,1,0:T(8,128)S(1)} collective-permute-done((f32[2,4,6,8,128]{4,3,2,1,0:T(8,128)S(1)}, f32[2,4,6,8,128]{4,3,2,1,0:T(8,128)S(1)}, u32[]{:S(2)}, u32[]{:S(2)}) %collective-permute-start.11) | collective-permute-done | bytes 196640 | tf_op jit(solution)/shard_map/ppermute | solution.py:346
  30.9 0.0 collective-permute-done.12.rest_3_
  30.9 0.6 shard_map.81.rest_9_
  31.4 0.4 collective-permute-start.16
  31.8 0.0 collective-permute-done.9.rest_8_
  31.8 0.0 collective-permute-done.7.weight_pair
  31.8 0.8 %collective-permute-done.8.rest_7_ = f32[320,128]{1,0:T(8,128)S(1)} collective-permute-done((f32[320,128]{1,0:T(8,128)S(1)}, f32[320,128]{1,0:T(8,128)S(1)}, u32[]{:S(2)}, u32[]{:S(2)}) %collective-permute-start.8) | collective-permute-done | bytes 163872 | tf_op jit(solution)/shard_map/ppermute | solution.py:346
  32.6 1.0 %shard_map.82 = (f32[2,4,5,8,128]{4,3,2,1,0:T(8,128)S(1)}, f32[2,4,5,8,128]{4,3,2,1,0:T(8,128)S(1)}, f32[2,4,5,8,128]{4,3,2,1,0:T(8,128)S(1)}, f32[2,4,5,8,128]{4,3,2,1,0:T(8,128)S(1)}) custom-call(s32[3]{0:T(128)S(1)} %pad_add_fusion.me, f32[4,32,128]{2,1,0:T(8,128)S(1)} %collective-permute-done.7.weight_pair, f32[224,128]{1,0:T(8,128)S(1)} %get-tuple-element.39.rest_0_, ...), custom_call_target="tpu_custom_call" | custom-call | tf_op jit(solution)/shard_map/pallas_call | solution.py:331
  33.7 2.2 %collective-permute-start.13 = (f32[2,4,5,8,128]{4,3,2,1,0:T(8,128)S(1)}, f32[2,4,5,8,128]{4,3,2,1,0:T(8,128)S(1)}, u32[]{:S(2)}, u32[]{:S(2)}) collective-permute-start(f32[2,4,5,8,128]{4,3,2,1,0:T(8,128)S(1)} %get-tuple-element.52), channel_id=1, source_target_pairs={{0,2},{1,3},{2,0},{3,1},{4,6},{5,7},{6,4},{7,5},{8,10},{9,11},{10,... | collective-permute-start | bytes 491528 | tf_op jit(solution)/shard_map/ppermute | solution.py:346
  35.9 0.3 collective-permute-start.14
  36.2 1.4 %collective-permute-start.15 = (f32[2,4,5,8,128]{4,3,2,1,0:T(8,128)S(1)}, f32[2,4,5,8,128]{4,3,2,1,0:T(8,128)S(1)}, u32[]{:S(2)}, u32[]{:S(2)}) collective-permute-start(f32[2,4,5,8,128]{4,3,2,1,0:T(8,128)S(1)} %get-tuple-element.54), channel_id=1, source_target_pairs={{0,6},{1,7},{2,4},{3,5},{4,2},{5,3},{6,0},{7,1},{8,14},{9,15},{10,... | collective-permute-start | bytes 491528 | tf_op jit(solution)/shard_map/ppermute | solution.py:346
  37.6 0.6 %shard_map.84 = (f32[6,2,4,8,128]{4,3,2,1,0:T(8,128)S(1)}, f32[6,2,4,8,128]{4,3,2,1,0:T(8,128)S(1)}, f32[6,2,4,8,128]{4,3,2,1,0:T(8,128)S(1)}) custom-call(s32[3]{0:T(128)S(1)} %pad_add_fusion.me, f32[2,4,6,8,128]{4,3,2,1,0:T(8,128)S(1)} %get-tuple-element.43.rest_0_, f32[2,4,6,8,128]{4,3,2,1,0:T(8,128)S(1)} %collective-permute-done.10.rest_1_, ...), custom_call_target="tpu_custom_call" | custom-call | tf_op jit(solution)/shard_map/pallas_call | solution.py:331
  38.2 0.1 collective-permute-start.20
  38.3 2.4 %collective-permute-done.13.rest_1_ = f32[2,4,5,8,128]{4,3,2,1,0:T(8,128)S(1)} collective-permute-done((f32[2,4,5,8,128]{4,3,2,1,0:T(8,128)S(1)}, f32[2,4,5,8,128]{4,3,2,1,0:T(8,128)S(1)}, u32[]{:S(2)}, u32[]{:S(2)}) %collective-permute-start.13) | collective-permute-done | bytes 163872 | tf_op jit(solution)/shard_map/ppermute | solution.py:346
  40.7 3.0 %collective-permute-start.21 = (f32[6,2,4,8,128]{4,3,2,1,0:T(8,128)S(1)}, f32[6,2,4,8,128]{4,3,2,1,0:T(8,128)S(1)}, u32[]{:S(2)}, u32[]{:S(2)}) collective-permute-start(f32[6,2,4,8,128]{4,3,2,1,0:T(8,128)S(1)} %get-tuple-element.61), channel_id=1, source_target_pairs={{0,24},{8,16},{16,8},{24,0},{1,25},{9,17},{17,9},{25,1},{2,26},{10... | collective-permute-start | bytes 589832 | tf_op jit(solution)/shard_map/ppermute | solution.py:346
  43.6 1.2 %collective-permute-done.14.rest_2_ = f32[2,4,5,8,128]{4,3,2,1,0:T(8,128)S(1)} collective-permute-done((f32[2,4,5,8,128]{4,3,2,1,0:T(8,128)S(1)}, f32[2,4,5,8,128]{4,3,2,1,0:T(8,128)S(1)}, u32[]{:S(2)}, u32[]{:S(2)}) %collective-permute-start.14) | collective-permute-done | bytes 163872 | tf_op jit(solution)/shard_map/ppermute | solution.py:346
  44.8 0.0 collective-permute-done.15.rest_3_
  44.8 0.0 collective-permute-done.16.rest_4_.rest_2_
  44.8 1.0 %shard_map.83 = (f32[5,2,32,128]{3,2,1,0:T(8,128)S(1)}, f32[5,2,32,128]{3,2,1,0:T(8,128)S(1)}, f32[5,2,32,128]{3,2,1,0:T(8,128)S(1)}, f32[5,2,32,128]{3,2,1,0:T(8,128)S(1)}) custom-call(s32[3]{0:T(128)S(1)} %pad_add_fusion.me, s32[2,128]{1,0:T(2,128)S(1)} %get-tuple-element.44.dest, f32[2,4,5,8,128]{4,3,2,1,0:T(8,128)S(1)} %get-tuple-element.51.rest_0_.rest_4_, ...), custom_call_target="tpu_custom_call" | custom-call | tf_op jit(solution)/shard_map/pallas_call | solution.py:331
  45.8 1.3 %collective-permute-start.17 = (f32[5,2,32,128]{3,2,1,0:T(8,128)S(1)}, f32[5,2,32,128]{3,2,1,0:T(8,128)S(1)}, u32[]{:S(2)}, u32[]{:S(2)}) collective-permute-start(f32[5,2,32,128]{3,2,1,0:T(8,128)S(1)} %get-tuple-element.56), channel_id=1, source_target_pairs={{0,2},{1,3},{2,0},{3,1},{4,6},{5,7},{6,4},{7,5},{8,10},{9,11},{10,... | collective-permute-start | bytes 491528 | tf_op jit(solution)/shard_map/ppermute | solution.py:346
  47.1 1.4 %collective-permute-start.18 = (f32[5,2,32,128]{3,2,1,0:T(8,128)S(1)}, f32[5,2,32,128]{3,2,1,0:T(8,128)S(1)}, u32[]{:S(2)}, u32[]{:S(2)}) collective-permute-start(f32[5,2,32,128]{3,2,1,0:T(8,128)S(1)} %get-tuple-element.57), channel_id=1, source_target_pairs={{0,4},{1,5},{2,6},{3,7},{4,0},{5,1},{6,2},{7,3},{8,12},{9,13},{10,... | collective-permute-start | bytes 491528 | tf_op jit(solution)/shard_map/ppermute | solution.py:346
  48.5 0.9 %collective-permute-start.19 = (f32[5,2,32,128]{3,2,1,0:T(8,128)S(1)}, f32[5,2,32,128]{3,2,1,0:T(8,128)S(1)}, u32[]{:S(2)}, u32[]{:S(2)}) collective-permute-start(f32[5,2,32,128]{3,2,1,0:T(8,128)S(1)} %get-tuple-element.58), channel_id=1, source_target_pairs={{0,6},{1,7},{2,4},{3,5},{4,2},{5,3},{6,0},{7,1},{8,14},{9,15},{10,... | collective-permute-start | bytes 491528 | tf_op jit(solution)/shard_map/ppermute | solution.py:346
  49.4 0.5 collective-permute-done.20.rest_1_
  49.9 0.0 collective-permute-done.21.rest_3_
  49.9 1.7 %collective-permute-done.17.rest_4_.rest_1_ = f32[5,2,32,128]{3,2,1,0:T(8,128)S(1)} collective-permute-done((f32[5,2,32,128]{3,2,1,0:T(8,128)S(1)}, f32[5,2,32,128]{3,2,1,0:T(8,128)S(1)}, u32[]{:S(2)}, u32[]{:S(2)}) %collective-permute-start.17) | collective-permute-done | bytes 163872 | tf_op jit(solution)/shard_map/ppermute | solution.py:346
  51.6 1.0 %shard_map.85 = (f32[4,5,32,128]{3,2,1,0:T(8,128)S(1)}, f32[4,5,32,128]{3,2,1,0:T(8,128)S(1)}) custom-call(s32[3]{0:T(128)S(1)} %pad_add_fusion.me, f32[8,128]{1,0:T(8,128)S(1)} %get-tuple-element.36.mine, f32[8,128]{1,0:T(8,128)S(1)} %collective-permute-done.1.rest_4_.mine_pair, f32[6,2,4,8,128]{4,3,2,1,0:T(8,128)S(1)} %get-tuple-element.59.rest_0_, ...), custom_call_target="tpu_custom_call" | custom-call | tf_op jit(solution)/shard_map/pallas_call | solution.py:331
  52.6 2.4 %collective-permute-done.18.rest_2_ = f32[5,2,32,128]{3,2,1,0:T(8,128)S(1)} collective-permute-done((f32[5,2,32,128]{3,2,1,0:T(8,128)S(1)}, f32[5,2,32,128]{3,2,1,0:T(8,128)S(1)}, u32[]{:S(2)}, u32[]{:S(2)}) %collective-permute-start.18) | collective-permute-done | bytes 163872 | tf_op jit(solution)/shard_map/ppermute | solution.py:346
  55.0 0.0 collective-permute-done.19.rest_3_
  55.0 0.9 %shard_map.86 = (f32[640,128]{1,0:T(8,128)S(1)}, f32[640,128]{1,0:T(8,128)S(1)}) custom-call(s32[3]{0:T(128)S(1)} %pad_add_fusion.me, f32[5,32,32]{2,1,0:T(8,128)S(1)} %get-tuple-element.34.inverse, f32[5,2,32,128]{3,2,1,0:T(8,128)S(1)} %get-tuple-element.55.rest_0_, f32[5,2,32,128]{3,2,1,0:T(8,128)S(1)} %collective-permute-done.17.rest_4_.rest_1_, ...), custom_call_target="tpu_custom_call" | custom-call | tf_op jit(solution)/shard_map/pallas_call | solution.py:331
  55.9 0.1 collective-permute-start.22
  56.0 0.5 collective-permute-start.23
  56.5 1.1 %collective-permute-done.22 = f32[640,128]{1,0:T(8,128)S(1)} collective-permute-done((f32[640,128]{1,0:T(8,128)S(1)}, f32[640,128]{1,0:T(8,128)S(1)}, u32[]{:S(2)}, u32[]{:S(2)}) %collective-permute-start.22) | collective-permute-done | bytes 327712 | tf_op jit(solution)/shard_map/ppermute | solution.py:346
  57.6 0.8 %add.12 = f32[640,128]{1,0:T(8,128)} add(f32[640,128]{1,0:T(8,128)S(1)} %get-tuple-element.63, f32[640,128]{1,0:T(8,128)S(1)} %collective-permute-done.22) | non-fusion elementwise | flops 81920 | bytes 983040 | tf_op jit(solution)/shard_map/add | solution.py:480
  58.4 0.0 collective-permute-done.23
  58.4 0.8 %add_bitcast_fusion = f32[1,4,32,5,128]{4,2,3,1,0:T(8,128)} fusion(f32[4,5,32,128]{3,2,1,0:T(8,128)S(1)} %get-tuple-element.65, f32[4,5,32,128]{3,2,1,0:T(8,128)S(1)} %collective-permute-done.23), kind=kLoop, calls=%fused_computation | loop fusion | flops 81920 | bytes 983040 | tf_op jit(solution)/shard_map/broadcast_in_dim | solution.py:482
Async XLA Ops:
  0.6 7.1 %collective-permute-start.2 = (f32[640,128]{1,0:T(8,128)}, f32[640,128]{1,0:T(8,128)S(1)}, u32[]{:S(2)}, u32[]{:S(2)}) collective-permute-start(f32[640,128]{1,0:T(8,128)} %bitcast.25), channel_id=1, source_target_pairs={{0,1},{1,0},{2,3},{3,2},{4,5},{5,4},{6,7},{7,6},{8,9},{9,8},{10,11... | collective-permute-start | bytes 983048 | tf_op jit(solution)/shard_map/ppermute | solution.py:346
  2.4 20.2 %collective-permute-start.6 = (f32[648,128]{1,0:T(8,128)S(1)}, f32[648,128]{1,0:T(8,128)S(1)}, u32[]{:S(2)}, u32[]{:S(2)}) collective-permute-start(f32[648,128]{1,0:T(8,128)S(1)} %get-tuple-element.35.rest_4_), channel_id=1, source_target_pairs={{0,8},{8,0},{16,24},{24,16},{1,9},{9,1},{17,25},{25,17},{2,10},{10... | collective-permute-start | bytes 995336 | tf_op jit(solution)/shard_map/ppermute | solution.py:346
  5.1 18.1 %collective-permute-start = (f32[648,128]{1,0:T(8,128)S(1)}, f32[648,128]{1,0:T(8,128)S(1)}, u32[]{:S(2)}, u32[]{:S(2)}) collective-permute-start(f32[648,128]{1,0:T(8,128)S(1)} %get-tuple-element.35.rest_4_), channel_id=1, source_target_pairs={{0,16},{8,24},{16,0},{24,8},{1,17},{9,25},{17,1},{25,9},{2,18},{10... | collective-permute-start | bytes 995336 | tf_op jit(solution)/shard_map/ppermute | solution.py:346
  7.7 4.1 %collective-permute-start.1 = (f32[8,128]{1,0:T(8,128)S(1)}, f32[8,128]{1,0:T(8,128)S(1)}, u32[]{:S(2)}, u32[]{:S(2)}) collective-permute-start(f32[8,128]{1,0:T(8,128)S(1)} %get-tuple-element.36.mine), channel_id=1, source_target_pairs={{0,1},{1,0},{2,3},{3,2},{4,5},{5,4},{6,7},{7,6},{8,9},{9,8},{10,11... | collective-permute-start | bytes 12296 | tf_op jit(solution)/shard_map/ppermute | solution.py:346
  8.7 5.6 %collective-permute-start.3 = (f32[224,128]{1,0:T(8,128)S(1)}, f32[224,128]{1,0:T(8,128)S(1)}, u32[]{:S(2)}, u32[]{:S(2)}) collective-permute-start(f32[224,128]{1,0:T(8,128)S(1)} %get-tuple-element.40), channel_id=1, source_target_pairs={{0,2},{1,3},{2,0},{3,1},{4,6},{5,7},{6,4},{7,5},{8,10},{9,11},{10,... | collective-permute-start | bytes 344072 | tf_op jit(solution)/shard_map/ppermute | solution.py:346
  10.3 7.7 %collective-permute-start.4 = (f32[224,128]{1,0:T(8,128)S(1)}, f32[224,128]{1,0:T(8,128)S(1)}, u32[]{:S(2)}, u32[]{:S(2)}) collective-permute-start(f32[224,128]{1,0:T(8,128)S(1)} %get-tuple-element.41), channel_id=1, source_target_pairs={{0,4},{1,5},{2,6},{3,7},{4,0},{5,1},{6,2},{7,3},{8,12},{9,13},{10,... | collective-permute-start | bytes 344072 | tf_op jit(solution)/shard_map/ppermute | solution.py:346
  11.8 6.2 %collective-permute-start.5 = (f32[224,128]{1,0:T(8,128)S(1)}, f32[224,128]{1,0:T(8,128)S(1)}, u32[]{:S(2)}, u32[]{:S(2)}) collective-permute-start(f32[224,128]{1,0:T(8,128)S(1)} %get-tuple-element.42), channel_id=1, source_target_pairs={{0,6},{1,7},{2,4},{3,5},{4,2},{5,3},{6,0},{7,1},{8,14},{9,15},{10,... | collective-permute-start | bytes 344072 | tf_op jit(solution)/shard_map/ppermute | solution.py:346
  19.1 7.7 %collective-permute-start.10 = (f32[2,4,6,8,128]{4,3,2,1,0:T(8,128)S(1)}, f32[2,4,6,8,128]{4,3,2,1,0:T(8,128)S(1)}, u32[]{:S(2)}, u32[]{:S(2)}) collective-permute-start(f32[2,4,6,8,128]{4,3,2,1,0:T(8,128)S(1)} %get-tuple-element.48), channel_id=1, source_target_pairs={{0,2},{1,3},{2,0},{3,1},{4,6},{5,7},{6,4},{7,5},{8,10},{9,11},{10,... | collective-permute-start | bytes 589832 | tf_op jit(solution)/shard_map/ppermute | solution.py:346
  20.4 10.5 %collective-permute-start.11 = (f32[2,4,6,8,128]{4,3,2,1,0:T(8,128)S(1)}, f32[2,4,6,8,128]{4,3,2,1,0:T(8,128)S(1)}, u32[]{:S(2)}, u32[]{:S(2)}) collective-permute-start(f32[2,4,6,8,128]{4,3,2,1,0:T(8,128)S(1)} %get-tuple-element.49), channel_id=1, source_target_pairs={{0,4},{1,5},{2,6},{3,7},{4,0},{5,1},{6,2},{7,3},{8,12},{9,13},{10,... | collective-permute-start | bytes 589832 | tf_op jit(solution)/shard_map/ppermute | solution.py:346
  21.2 9.6 %collective-permute-start.12 = (f32[2,4,6,8,128]{4,3,2,1,0:T(8,128)S(1)}, f32[2,4,6,8,128]{4,3,2,1,0:T(8,128)S(1)}, u32[]{:S(2)}, u32[]{:S(2)}) collective-permute-start(f32[2,4,6,8,128]{4,3,2,1,0:T(8,128)S(1)} %get-tuple-element.50), channel_id=1, source_target_pairs={{0,6},{1,7},{2,4},{3,5},{4,2},{5,3},{6,0},{7,1},{8,14},{9,15},{10,... | collective-permute-start | bytes 589832 | tf_op jit(solution)/shard_map/ppermute | solution.py:346
  22.6 9.2 %collective-permute-start.9 = (f32[328,128]{1,0:T(8,128)S(1)}, f32[328,128]{1,0:T(8,128)S(1)}, u32[]{:S(2)}, u32[]{:S(2)}) collective-permute-start(f32[328,128]{1,0:T(8,128)S(1)} %get-tuple-element.47), channel_id=1, source_target_pairs={{0,24},{8,16},{16,8},{24,0},{1,25},{9,17},{17,9},{25,1},{2,26},{10... | collective-permute-start | bytes 503816 | tf_op jit(solution)/shard_map/ppermute | solution.py:346
  24.1 8.5 %collective-permute-start.8 = (f32[320,128]{1,0:T(8,128)S(1)}, f32[320,128]{1,0:T(8,128)S(1)}, u32[]{:S(2)}, u32[]{:S(2)}) collective-permute-start(f32[320,128]{1,0:T(8,128)S(1)} %get-tuple-element.46), channel_id=1, source_target_pairs={{0,8},{8,0},{16,24},{24,16},{1,9},{9,1},{17,25},{25,17},{2,10},{10... | collective-permute-start | bytes 491528 | tf_op jit(solution)/shard_map/ppermute | solution.py:346
  26.8 5.1 %collective-permute-start.7 = (f32[4,32,128]{2,1,0:T(8,128)S(1)}, f32[4,32,128]{2,1,0:T(8,128)S(1)}, u32[]{:S(2)}, u32[]{:S(2)}) collective-permute-start(f32[4,32,128]{2,1,0:T(8,128)S(1)} %get-tuple-element.45), channel_id=1, source_target_pairs={{0,1},{1,0},{2,3},{3,2},{4,5},{5,4},{6,7},{7,6},{8,9},{9,8},{10,11... | collective-permute-start | bytes 196616 | tf_op jit(solution)/shard_map/ppermute | solution.py:346
  31.4 13.4 %collective-permute-start.16 = (f32[6,2,4,8,128]{4,3,2,1,0:T(8,128)S(1)}, f32[6,2,4,8,128]{4,3,2,1,0:T(8,128)S(1)}, u32[]{:S(2)}, u32[]{:S(2)}) collective-permute-start(f32[6,2,4,8,128]{4,3,2,1,0:T(8,128)S(1)} %shard_map.81.rest_9_), channel_id=1, source_target_pairs={{0,16},{8,24},{16,0},{24,8},{1,17},{9,25},{17,1},{25,9},{2,18},{10... | collective-permute-start | bytes 589832 | tf_op jit(solution)/shard_map/ppermute | solution.py:346
  33.7 7.0 %collective-permute-start.13 = (f32[2,4,5,8,128]{4,3,2,1,0:T(8,128)S(1)}, f32[2,4,5,8,128]{4,3,2,1,0:T(8,128)S(1)}, u32[]{:S(2)}, u32[]{:S(2)}) collective-permute-start(f32[2,4,5,8,128]{4,3,2,1,0:T(8,128)S(1)} %get-tuple-element.52), channel_id=1, source_target_pairs={{0,2},{1,3},{2,0},{3,1},{4,6},{5,7},{6,4},{7,5},{8,10},{9,11},{10,... | collective-permute-start | bytes 491528 | tf_op jit(solution)/shard_map/ppermute | solution.py:346
  35.9 8.9 %collective-permute-start.14 = (f32[2,4,5,8,128]{4,3,2,1,0:T(8,128)S(1)}, f32[2,4,5,8,128]{4,3,2,1,0:T(8,128)S(1)}, u32[]{:S(2)}, u32[]{:S(2)}) collective-permute-start(f32[2,4,5,8,128]{4,3,2,1,0:T(8,128)S(1)} %get-tuple-element.53), channel_id=1, source_target_pairs={{0,4},{1,5},{2,6},{3,7},{4,0},{5,1},{6,2},{7,3},{8,12},{9,13},{10,... | collective-permute-start | bytes 491528 | tf_op jit(solution)/shard_map/ppermute | solution.py:346
  36.2 8.6 %collective-permute-start.15 = (f32[2,4,5,8,128]{4,3,2,1,0:T(8,128)S(1)}, f32[2,4,5,8,128]{4,3,2,1,0:T(8,128)S(1)}, u32[]{:S(2)}, u32[]{:S(2)}) collective-permute-start(f32[2,4,5,8,128]{4,3,2,1,0:T(8,128)S(1)} %get-tuple-element.54), channel_id=1, source_target_pairs={{0,6},{1,7},{2,4},{3,5},{4,2},{5,3},{6,0},{7,1},{8,14},{9,15},{10,... | collective-permute-start | bytes 491528 | tf_op jit(solution)/shard_map/ppermute | solution.py:346
  38.2 11.7 %collective-permute-start.20 = (f32[6,2,4,8,128]{4,3,2,1,0:T(8,128)S(1)}, f32[6,2,4,8,128]{4,3,2,1,0:T(8,128)S(1)}, u32[]{:S(2)}, u32[]{:S(2)}) collective-permute-start(f32[6,2,4,8,128]{4,3,2,1,0:T(8,128)S(1)} %get-tuple-element.60), channel_id=1, source_target_pairs={{0,8},{8,0},{16,24},{24,16},{1,9},{9,1},{17,25},{25,17},{2,10},{10... | collective-permute-start | bytes 589832 | tf_op jit(solution)/shard_map/ppermute | solution.py:346
  40.7 9.2 %collective-permute-start.21 = (f32[6,2,4,8,128]{4,3,2,1,0:T(8,128)S(1)}, f32[6,2,4,8,128]{4,3,2,1,0:T(8,128)S(1)}, u32[]{:S(2)}, u32[]{:S(2)}) collective-permute-start(f32[6,2,4,8,128]{4,3,2,1,0:T(8,128)S(1)} %get-tuple-element.61), channel_id=1, source_target_pairs={{0,24},{8,16},{16,8},{24,0},{1,25},{9,17},{17,9},{25,1},{2,26},{10... | collective-permute-start | bytes 589832 | tf_op jit(solution)/shard_map/ppermute | solution.py:346
  45.8 5.8 %collective-permute-start.17 = (f32[5,2,32,128]{3,2,1,0:T(8,128)S(1)}, f32[5,2,32,128]{3,2,1,0:T(8,128)S(1)}, u32[]{:S(2)}, u32[]{:S(2)}) collective-permute-start(f32[5,2,32,128]{3,2,1,0:T(8,128)S(1)} %get-tuple-element.56), channel_id=1, source_target_pairs={{0,2},{1,3},{2,0},{3,1},{4,6},{5,7},{6,4},{7,5},{8,10},{9,11},{10,... | collective-permute-start | bytes 491528 | tf_op jit(solution)/shard_map/ppermute | solution.py:346
  47.1 8.0 %collective-permute-start.18 = (f32[5,2,32,128]{3,2,1,0:T(8,128)S(1)}, f32[5,2,32,128]{3,2,1,0:T(8,128)S(1)}, u32[]{:S(2)}, u32[]{:S(2)}) collective-permute-start(f32[5,2,32,128]{3,2,1,0:T(8,128)S(1)} %get-tuple-element.57), channel_id=1, source_target_pairs={{0,4},{1,5},{2,6},{3,7},{4,0},{5,1},{6,2},{7,3},{8,12},{9,13},{10,... | collective-permute-start | bytes 491528 | tf_op jit(solution)/shard_map/ppermute | solution.py:346
  48.5 6.6 %collective-permute-start.19 = (f32[5,2,32,128]{3,2,1,0:T(8,128)S(1)}, f32[5,2,32,128]{3,2,1,0:T(8,128)S(1)}, u32[]{:S(2)}, u32[]{:S(2)}) collective-permute-start(f32[5,2,32,128]{3,2,1,0:T(8,128)S(1)} %get-tuple-element.58), channel_id=1, source_target_pairs={{0,6},{1,7},{2,4},{3,5},{4,2},{5,3},{6,0},{7,1},{8,14},{9,15},{10,... | collective-permute-start | bytes 491528 | tf_op jit(solution)/shard_map/ppermute | solution.py:346
  55.9 1.7 %collective-permute-start.22 = (f32[640,128]{1,0:T(8,128)S(1)}, f32[640,128]{1,0:T(8,128)S(1)}, u32[]{:S(2)}, u32[]{:S(2)}) collective-permute-start(f32[640,128]{1,0:T(8,128)S(1)} %get-tuple-element.64), channel_id=1, source_target_pairs={{0,1},{1,0},{2,3},{3,2},{4,5},{5,4},{6,7},{7,6},{8,9},{9,8},{10,11... | collective-permute-start | bytes 983048 | tf_op jit(solution)/shard_map/ppermute | solution.py:346
  56.0 2.4 %collective-permute-start.23 = (f32[4,5,32,128]{3,2,1,0:T(8,128)S(1)}, f32[4,5,32,128]{3,2,1,0:T(8,128)S(1)}, u32[]{:S(2)}, u32[]{:S(2)}) collective-permute-start(f32[4,5,32,128]{3,2,1,0:T(8,128)S(1)} %get-tuple-element.62.rest_4_), channel_id=1, source_target_pairs={{0,1},{1,0},{2,3},{3,2},{4,5},{5,4},{6,7},{7,6},{8,9},{9,8},{10,11... | collective-permute-start | bytes 983048 | tf_op jit(solution)/shard_map/ppermute | solution.py:346

commit v5 on v4

--- a/solution.py
+++ b/solution.py
@@ -321,18 +321,37 @@
             pair[at, :] = other[:, b * LANES : (b + 1) * LANES]
 
 
-def call(kernel, dims, args, outs, scratch=(), after=(), outside=False, limit=48):
+def finish_kernel(dims, me, mine, got, *rest):
+    out, total, sems = rest[-3:]
+    pieces = sems.shape[0]
+    step = total.shape[0] // pieces
+    copies = []
+    for i in range(pieces):
+        rows = pl.ds(i * step, step)
+        total[rows, :] = mine[rows, :] + got[rows, :]
+        copies.append(pltpu.make_async_copy(total.at[rows], out.at[rows], sems.at[i]))
+        copies[-1].start()
+    for copy in copies:
+        copy.wait()
+
+
+def place():
+    slab = lax.axis_index("slab")
+    return lax.axis_index("lat"), lax.div(slab, 2), lax.rem(slab, 2)
+
+
+def call(kernel, dims, args, outs, scratch=(), after=(), outside=False, to_main=False, limit=48):
     inside = pl.BlockSpec(memory_space=pltpu.VMEM)
     anywhere = pl.BlockSpec(memory_space=pl.ANY)
     if outside:
         specs = [anywhere] * len(args)
     else:
-        specs = [pl.BlockSpec(memory_space=pltpu.SMEM)] + [inside] * (len(args) - 1)
+        specs = [inside] * len(args)
     return pl.pallas_call(
-        functools.partial(kernel, dims),
+        functools.partial(kernel, dims) if outside else lambda *refs: kernel(dims, place(), *refs),
         out_shape=[shape if hasattr(shape, "dtype") else jax.ShapeDtypeStruct(shape, F32) for shape in outs],
         in_specs=specs + [anywhere] * len(after),
-        out_specs=[inside] * len(outs),
+        out_specs=[anywhere if to_main else inside] * len(outs),
         scratch_shapes=[pltpu.VMEM(shape, F32) if isinstance(shape, tuple) else shape for shape in scratch],
         compiler_params=pltpu.CompilerParams(vmem_limit_bytes=limit * 1024 * 1024),
     )(*args, *after)
@@ -355,8 +374,6 @@
     row_total = lev_dev * blocks
     span = lev_dev * 2 * here
     dims = (lats, slabs, chips, cap, lev_dev, here, fields)
-    lat, slab = lax.axis_index("lat"), lax.axis_index("slab")
-    me = jnp.stack([lat, slab // 2, slab % 2]).astype(jnp.int32)
 
     def pair(array):
         return swap(array, "slab", 1, slabs)
@@ -403,7 +420,7 @@
         call(
             start_kernel,
             dims,
-            (me, cot_here, inverse_here, pair(cot), weights_here, mine),
+            (cot_here, inverse_here, pair(cot), weights_here, mine),
             [(fields * span + 2 * lats * cap, width)] * chips,
             [(fields, levels * 2 * here, width), (chips, 2, lats * cap, width)],
         )
@@ -411,7 +428,7 @@
     *slot_back, weight_other = call(
         back_kernel,
         dims,
-        (me, mine, weights_here, *first),
+        (mine, weights_here, *first),
         [(2, lats, fields + 1, cap, width)] * chips + [(chips, lats * cap, width)],
         [(row_total, (fields + 1) * width), (chips, 2, lats, fields + 1, cap, width)],
         after=[mine_pair],
@@ -420,7 +437,7 @@
     first_half, dests = call(
         hold_kernel,
         dims,
-        (me, far, mine, mine_pair),
+        (far, mine, mine_pair),
         [(cut, width), jax.ShapeDtypeStruct((2, row_total), jnp.int32)],
         [pltpu.SemaphoreType.DMA(())],
         after=[slot_back[0], near],
@@ -436,17 +453,17 @@
     soon = [j for j in range(lats) if j == 2]
     late = [j for j in range(lats) if j != 2]
     message = (fields + 1, 2, chips, cap, width)
-    sorted_soon = call(functools.partial(sort_kernel, soon), dims, (me, *slot_back), [message] * len(soon))
+    sorted_soon = call(functools.partial(sort_kernel, soon), dims, slot_back, [message] * len(soon))
     mixed = call(
         mix_kernel,
         dims,
-        (me, pair(weight_other), *first, *states),
+        (pair(weight_other), *first, *states),
         [(2, lats, fields, cap, width)] * chips,
         [(lats, 2, chips, cap, width), (2, chips, fields, cap, width)],
         after=sorted_soon,
     )
     sorted_late = call(
-        functools.partial(sort_kernel, late), dims, (me, *slot_back), [message] * len(late), after=mixed[:1]
+        functools.partial(sort_kernel, late), dims, slot_back, [message] * len(late), after=mixed[:1]
     )
     returned = [None] * lats
     for j, sorted_back in zip(soon + late, [*sorted_soon, *sorted_late]):
@@ -454,7 +471,7 @@
     moved = call(
         arrive_kernel,
         dims,
-        (me, dests, *over_chips(mixed)),
+        (dests, *over_chips(mixed)),
         [(fields, 2, span, width)] * chips,
         [(fields, lats * chips, cap, width), (chips, fields, span, width)],
         after=returned[2:3],
@@ -463,7 +480,7 @@
     adjoint, adjoint_pair = call(
         add_kernel,
         dims,
-        (me, mine, mine_pair, *returned),
+        (mine, mine_pair, *returned),
         [(lev_dev, fields, blocks, width)] * 2,
         [(fields + 1, lats, chips, cap, width)],
         after=moved[1:2],
@@ -471,13 +488,21 @@
     tangent, tangent_pair = call(
         diffuse_kernel,
         dims,
-        (me, inverse_here, *moved),
+        (inverse_here, *moved),
         [cot.shape, cot.shape],
         [(fields, levels * 2 * here, width)],
         after=[adjoint_pair],
     )
     adjoint = adjoint + pair(adjoint_pair)
-    tangent = tangent + pair(tangent_pair)
+    (tangent,) = call(
+        finish_kernel,
+        dims,
+        (tangent, pair(tangent_pair)),
+        [tangent.shape],
+        [tangent.shape, pltpu.SemaphoreType.DMA((fields,))],
+        after=[adjoint],
+        to_main=True,
+    )
     tangent_out = tangent.reshape(1, levels, fields, here, width).transpose(0, 1, 3, 2, 4)
     adjoint_out = adjoint.transpose(0, 2, 1, 3)[None]
     return tangent_out, adjoint_out

time: 59.4 us -> 57.7 us (0.971)
  Pallas kernels: 9.33 us -> 5.21 us
  starting transfers between devices: 25.3 us -> 27.5 us
  waiting for transfers between devices: 22.2 us -> 23.9 us
  other arithmetic: 1.6 us -> 0.05 us
    pallas_call x10 -> x11, Pallas kernels: 9.33 us -> 5.21 us  [call(): pl.pallas_call(functools.partial(kernel, dims) if outside else lambda *re...]
    ppermute x24, starting transfers between devices: 25.3 us -> 27.5 us  [swap(): return lax.ppermute(array, axis, [(i, i ^ bit) for i in range(count)])]
    ppermute x24, waiting for transfers between devices: 22.2 us -> 23.9 us  [swap(): return lax.ppermute(array, axis, [(i, i ^ bit) for i in range(count)])]
    broadcast_in_dim x1 -> x0, other arithmetic: 0.77 us -> none  [body(): adjoint_out = adjoint.transpose(0, 2, 1, 3)[None]]
    add x1, other arithmetic: 0.76 us -> 0.05 us  [body(): adjoint = adjoint + pair(adjoint_pair)]
  transfers between devices with their start and end apart: 24 -> 24, of which waited for: 11 -> 12; matrix products, arithmetic and copies ran while one was open for 1% -> 0% of each run, Pallas kernels for 14% -> 8%
where the time goes in v5:
time: 57.7 us; the launch traced here: 57.5 us
  starting transfers between devices  27.5 us (48%)
  waiting for transfers between devices  23.9 us (41%)
  Pallas kernels  5.21 us (9%)
  between operations  0.78 us (1%)
    ppermute x24, starting transfers between devices, swap(): return lax.ppermute(array, axis, [(i, i ^ bit) for i in range(count)])  27.5 us
    ppermute x24, waiting for transfers between devices, swap(): return lax.ppermute(array, axis, [(i, i ^ bit) for i in range(count)])  23.9 us
    pallas_call x11, Pallas kernels, call(): pl.pallas_call(functools.partial(kernel, dims) if outside else lambda *re...  5.21 us
  transfers between devices with their start and end apart: 24, of which 12 were waited for; matrix products, arithmetic and copies ran while one was open for 0% of the time, Pallas kernels for 8%

profile of v5, /device:TPU:0, one launch (start us, length us, event | category | flops | bytes accessed | tf_op | source)
XLA Modules:
  0.0 57.5 jit_solution(17643383892105075710)
XLA Ops:
  0.6 0.5 collective-permute-start.2
  1.1 1.3 %shard_map.77 = (f32[648,128]{1,0:T(8,128)S(1)}, f32[328,128]{1,0:T(8,128)S(1)}, f32[8,128]{1,0:T(8,128)S(1)}, f32[640,128]{1,0:T(8,128)S(1)}, f32[128,128]{1,0:T(8,128)S(1)}, /*index=5*/f32[5,32,32]{2,1,0:T(8,128)S(1)}) custom-call(f32[640,128]{1,0:T(8,128)} %bitcast.22, s32[4,8,8]{2,1,0:T(8,128)} %bitcast.27, s32[1,128]{1,0:T(1,128)} %bitcast.28, ...), custom_call_target="tpu_custom_call" | custom-call | tf_op jit(solution)/shard_map/pallas_call | solution.py:350
  2.4 2.7 %collective-permute-start.6 = (f32[648,128]{1,0:T(8,128)S(1)}, f32[648,128]{1,0:T(8,128)S(1)}, u32[]{:S(2)}, u32[]{:S(2)}) collective-permute-start(f32[648,128]{1,0:T(8,128)S(1)} %get-tuple-element.35.refs_5_), channel_id=1, source_target_pairs={{0,8},{8,0},{16,24},{24,16},{1,9},{9,1},{17,25},{25,17},{2,10},{10... | collective-permute-start | bytes 995336 | tf_op jit(solution)/shard_map/ppermute | solution.py:365
  5.1 2.6 %collective-permute-start = (f32[648,128]{1,0:T(8,128)S(1)}, f32[648,128]{1,0:T(8,128)S(1)}, u32[]{:S(2)}, u32[]{:S(2)}) collective-permute-start(f32[648,128]{1,0:T(8,128)S(1)} %get-tuple-element.35.refs_5_), channel_id=1, source_target_pairs={{0,16},{8,24},{16,0},{24,8},{1,17},{9,25},{17,1},{25,9},{2,18},{10... | collective-permute-start | bytes 995336 | tf_op jit(solution)/shard_map/ppermute | solution.py:365
  7.7 0.0 collective-permute-start.1
  7.7 0.0 collective-permute-done.2.refs_2_
  7.7 0.4 shard_map.78
  8.1 1.6 %collective-permute-start.3 = (f32[224,128]{1,0:T(8,128)S(1)}, f32[224,128]{1,0:T(8,128)S(1)}, u32[]{:S(2)}, u32[]{:S(2)}) collective-permute-start(f32[224,128]{1,0:T(8,128)S(1)} %get-tuple-element.40), channel_id=1, source_target_pairs={{0,2},{1,3},{2,0},{3,1},{4,6},{5,7},{6,4},{7,5},{8,10},{9,11},{10,... | collective-permute-start | bytes 344072 | tf_op jit(solution)/shard_map/ppermute | solution.py:365
  9.6 1.5 %collective-permute-start.4 = (f32[224,128]{1,0:T(8,128)S(1)}, f32[224,128]{1,0:T(8,128)S(1)}, u32[]{:S(2)}, u32[]{:S(2)}) collective-permute-start(f32[224,128]{1,0:T(8,128)S(1)} %get-tuple-element.41), channel_id=1, source_target_pairs={{0,4},{1,5},{2,6},{3,7},{4,0},{5,1},{6,2},{7,3},{8,12},{9,13},{10,... | collective-permute-start | bytes 344072 | tf_op jit(solution)/shard_map/ppermute | solution.py:365
  11.2 0.0 collective-permute-done.1.refs_6_.refs_2_.refs_1_
  11.2 0.5 collective-permute-start.5
  11.6 2.1 %collective-permute-done.3.refs_3_.refs_2_ = f32[224,128]{1,0:T(8,128)S(1)} collective-permute-done((f32[224,128]{1,0:T(8,128)S(1)}, f32[224,128]{1,0:T(8,128)S(1)}, u32[]{:S(2)}, u32[]{:S(2)}) %collective-permute-start.3) | collective-permute-done | bytes 114720 | tf_op jit(solution)/shard_map/ppermute | solution.py:365
  13.7 3.7 %collective-permute-done.4.refs_4_.refs_3_ = f32[224,128]{1,0:T(8,128)S(1)} collective-permute-done((f32[224,128]{1,0:T(8,128)S(1)}, f32[224,128]{1,0:T(8,128)S(1)}, u32[]{:S(2)}, u32[]{:S(2)}) %collective-permute-start.4) | collective-permute-done | bytes 114720 | tf_op jit(solution)/shard_map/ppermute | solution.py:365
  17.4 0.0 collective-permute-done.5.refs_5_.refs_4_
  17.4 0.5 shard_map.79
  17.9 1.3 %collective-permute-start.10 = (f32[2,4,6,8,128]{4,3,2,1,0:T(8,128)S(1)}, f32[2,4,6,8,128]{4,3,2,1,0:T(8,128)S(1)}, u32[]{:S(2)}, u32[]{:S(2)}) collective-permute-start(f32[2,4,6,8,128]{4,3,2,1,0:T(8,128)S(1)} %get-tuple-element.48), channel_id=1, source_target_pairs={{0,2},{1,3},{2,0},{3,1},{4,6},{5,7},{6,4},{7,5},{8,10},{9,11},{10,... | collective-permute-start | bytes 589832 | tf_op jit(solution)/shard_map/ppermute | solution.py:365
  19.2 0.8 %collective-permute-start.11 = (f32[2,4,6,8,128]{4,3,2,1,0:T(8,128)S(1)}, f32[2,4,6,8,128]{4,3,2,1,0:T(8,128)S(1)}, u32[]{:S(2)}, u32[]{:S(2)}) collective-permute-start(f32[2,4,6,8,128]{4,3,2,1,0:T(8,128)S(1)} %get-tuple-element.49), channel_id=1, source_target_pairs={{0,4},{1,5},{2,6},{3,7},{4,0},{5,1},{6,2},{7,3},{8,12},{9,13},{10,... | collective-permute-start | bytes 589832 | tf_op jit(solution)/shard_map/ppermute | solution.py:365
  20.0 1.4 %collective-permute-start.12 = (f32[2,4,6,8,128]{4,3,2,1,0:T(8,128)S(1)}, f32[2,4,6,8,128]{4,3,2,1,0:T(8,128)S(1)}, u32[]{:S(2)}, u32[]{:S(2)}) collective-permute-start(f32[2,4,6,8,128]{4,3,2,1,0:T(8,128)S(1)} %get-tuple-element.50), channel_id=1, source_target_pairs={{0,6},{1,7},{2,4},{3,5},{4,2},{5,3},{6,0},{7,1},{8,14},{9,15},{10,... | collective-permute-start | bytes 589832 | tf_op jit(solution)/shard_map/ppermute | solution.py:365
  21.5 0.0 collective-permute-done.6.refs_4_.refs_6_
  21.5 1.7 %collective-permute-start.9 = (f32[328,128]{1,0:T(8,128)S(1)}, f32[328,128]{1,0:T(8,128)S(1)}, u32[]{:S(2)}, u32[]{:S(2)}) collective-permute-start(f32[328,128]{1,0:T(8,128)S(1)} %get-tuple-element.47), channel_id=1, source_target_pairs={{0,24},{8,16},{16,8},{24,0},{1,25},{9,17},{17,9},{25,1},{2,26},{10... | collective-permute-start | bytes 503816 | tf_op jit(solution)/shard_map/ppermute | solution.py:365
  23.2 0.0 collective-permute-done.refs_0_.refs_7_
  23.2 0.4 shard_map.80
  23.6 0.4 collective-permute-start.8
  24.0 1.6 %collective-permute-done.10.refs_1_ = f32[2,4,6,8,128]{4,3,2,1,0:T(8,128)S(1)} collective-permute-done((f32[2,4,6,8,128]{4,3,2,1,0:T(8,128)S(1)}, f32[2,4,6,8,128]{4,3,2,1,0:T(8,128)S(1)}, u32[]{:S(2)}, u32[]{:S(2)}) %collective-permute-start.10) | collective-permute-done | bytes 196640 | tf_op jit(solution)/shard_map/ppermute | solution.py:365
  25.6 0.0 collective-permute-start.7
  25.6 4.1 %collective-permute-done.11.refs_2_ = f32[2,4,6,8,128]{4,3,2,1,0:T(8,128)S(1)} collective-permute-done((f32[2,4,6,8,128]{4,3,2,1,0:T(8,128)S(1)}, f32[2,4,6,8,128]{4,3,2,1,0:T(8,128)S(1)}, u32[]{:S(2)}, u32[]{:S(2)}) %collective-permute-start.11) | collective-permute-done | bytes 196640 | tf_op jit(solution)/shard_map/ppermute | solution.py:365
  29.7 0.0 collective-permute-done.12.refs_3_
  29.7 0.4 collective-permute-start.16
  30.1 0.2 collective-permute-done.9.refs_9_
  30.3 0.0 collective-permute-done.7.refs_0_
  30.3 2.4 %collective-permute-done.8.refs_8_ = f32[320,128]{1,0:T(8,128)S(1)} collective-permute-done((f32[320,128]{1,0:T(8,128)S(1)}, f32[320,128]{1,0:T(8,128)S(1)}, u32[]{:S(2)}, u32[]{:S(2)}) %collective-permute-start.8) | collective-permute-done | bytes 163872 | tf_op jit(solution)/shard_map/ppermute | solution.py:365
  32.6 0.5 shard_map.82
  33.2 2.3 %collective-permute-start.13 = (f32[2,4,5,8,128]{4,3,2,1,0:T(8,128)S(1)}, f32[2,4,5,8,128]{4,3,2,1,0:T(8,128)S(1)}, u32[]{:S(2)}, u32[]{:S(2)}) collective-permute-start(f32[2,4,5,8,128]{4,3,2,1,0:T(8,128)S(1)} %get-tuple-element.52), channel_id=1, source_target_pairs={{0,2},{1,3},{2,0},{3,1},{4,6},{5,7},{6,4},{7,5},{8,10},{9,11},{10,... | collective-permute-start | bytes 491528 | tf_op jit(solution)/shard_map/ppermute | solution.py:365
  35.5 1.3 %collective-permute-start.14 = (f32[2,4,5,8,128]{4,3,2,1,0:T(8,128)S(1)}, f32[2,4,5,8,128]{4,3,2,1,0:T(8,128)S(1)}, u32[]{:S(2)}, u32[]{:S(2)}) collective-permute-start(f32[2,4,5,8,128]{4,3,2,1,0:T(8,128)S(1)} %get-tuple-element.53), channel_id=1, source_target_pairs={{0,4},{1,5},{2,6},{3,7},{4,0},{5,1},{6,2},{7,3},{8,12},{9,13},{10,... | collective-permute-start | bytes 491528 | tf_op jit(solution)/shard_map/ppermute | solution.py:365
  36.7 0.6 collective-permute-start.15
  37.3 0.1 shard_map.84
  37.4 0.7 %collective-permute-start.20 = (f32[6,2,4,8,128]{4,3,2,1,0:T(8,128)S(1)}, f32[6,2,4,8,128]{4,3,2,1,0:T(8,128)S(1)}, u32[]{:S(2)}, u32[]{:S(2)}) collective-permute-start(f32[6,2,4,8,128]{4,3,2,1,0:T(8,128)S(1)} %get-tuple-element.60), channel_id=1, source_target_pairs={{0,8},{8,0},{16,24},{24,16},{1,9},{9,1},{17,25},{25,17},{2,10},{10... | collective-permute-start | bytes 589832 | tf_op jit(solution)/shard_map/ppermute | solution.py:365
  38.1 2.3 %collective-permute-done.13.refs_2_ = f32[2,4,5,8,128]{4,3,2,1,0:T(8,128)S(1)} collective-permute-done((f32[2,4,5,8,128]{4,3,2,1,0:T(8,128)S(1)}, f32[2,4,5,8,128]{4,3,2,1,0:T(8,128)S(1)}, u32[]{:S(2)}, u32[]{:S(2)}) %collective-permute-start.13) | collective-permute-done | bytes 163872 | tf_op jit(solution)/shard_map/ppermute | solution.py:365
  40.3 3.6 %collective-permute-start.21 = (f32[6,2,4,8,128]{4,3,2,1,0:T(8,128)S(1)}, f32[6,2,4,8,128]{4,3,2,1,0:T(8,128)S(1)}, u32[]{:S(2)}, u32[]{:S(2)}) collective-permute-start(f32[6,2,4,8,128]{4,3,2,1,0:T(8,128)S(1)} %get-tuple-element.61), channel_id=1, source_target_pairs={{0,24},{8,16},{16,8},{24,0},{1,25},{9,17},{17,9},{25,1},{2,26},{10... | collective-permute-start | bytes 589832 | tf_op jit(solution)/shard_map/ppermute | solution.py:365
  44.0 0.5 collective-permute-done.14.refs_3_
  44.5 0.0 collective-permute-done.15.refs_4_
  44.5 0.0 collective-permute-done.16.refs_5_.refs_4_
  44.5 0.4 shard_map.83
  44.9 1.3 %collective-permute-start.17 = (f32[5,2,32,128]{3,2,1,0:T(8,128)S(1)}, f32[5,2,32,128]{3,2,1,0:T(8,128)S(1)}, u32[]{:S(2)}, u32[]{:S(2)}) collective-permute-start(f32[5,2,32,128]{3,2,1,0:T(8,128)S(1)} %get-tuple-element.56), channel_id=1, source_target_pairs={{0,2},{1,3},{2,0},{3,1},{4,6},{5,7},{6,4},{7,5},{8,10},{9,11},{10,... | collective-permute-start | bytes 491528 | tf_op jit(solution)/shard_map/ppermute | solution.py:365
  46.2 1.3 %collective-permute-start.18 = (f32[5,2,32,128]{3,2,1,0:T(8,128)S(1)}, f32[5,2,32,128]{3,2,1,0:T(8,128)S(1)}, u32[]{:S(2)}, u32[]{:S(2)}) collective-permute-start(f32[5,2,32,128]{3,2,1,0:T(8,128)S(1)} %get-tuple-element.57), channel_id=1, source_target_pairs={{0,4},{1,5},{2,6},{3,7},{4,0},{5,1},{6,2},{7,3},{8,12},{9,13},{10,... | collective-permute-start | bytes 491528 | tf_op jit(solution)/shard_map/ppermute | solution.py:365
  47.5 1.0 %collective-permute-start.19 = (f32[5,2,32,128]{3,2,1,0:T(8,128)S(1)}, f32[5,2,32,128]{3,2,1,0:T(8,128)S(1)}, u32[]{:S(2)}, u32[]{:S(2)}) collective-permute-start(f32[5,2,32,128]{3,2,1,0:T(8,128)S(1)} %get-tuple-element.58), channel_id=1, source_target_pairs={{0,6},{1,7},{2,4},{3,5},{4,2},{5,3},{6,0},{7,1},{8,14},{9,15},{10,... | collective-permute-start | bytes 491528 | tf_op jit(solution)/shard_map/ppermute | solution.py:365
  48.5 0.0 collective-permute-done.20.refs_3_
  48.5 0.4 collective-permute-done.21.refs_5_
  48.9 2.9 %collective-permute-done.17.refs_6_.refs_2_ = f32[5,2,32,128]{3,2,1,0:T(8,128)S(1)} collective-permute-done((f32[5,2,32,128]{3,2,1,0:T(8,128)S(1)}, f32[5,2,32,128]{3,2,1,0:T(8,128)S(1)}, u32[]{:S(2)}, u32[]{:S(2)}) %collective-permute-start.17) | collective-permute-done | bytes 163872 | tf_op jit(solution)/shard_map/ppermute | solution.py:365
  51.9 0.5 shard_map.85
  52.4 0.1 collective-permute-start.23
  52.5 2.2 %collective-permute-done.18.refs_3_ = f32[5,2,32,128]{3,2,1,0:T(8,128)S(1)} collective-permute-done((f32[5,2,32,128]{3,2,1,0:T(8,128)S(1)}, f32[5,2,32,128]{3,2,1,0:T(8,128)S(1)}, u32[]{:S(2)}, u32[]{:S(2)}) %collective-permute-start.18) | collective-permute-done | bytes 163872 | tf_op jit(solution)/shard_map/ppermute | solution.py:365
  54.6 0.0 collective-permute-done.19.refs_4_
  54.6 0.3 shard_map.86
  55.0 0.1 collective-permute-start.22
  55.1 0.0 collective-permute-done.23
  55.1 0.0 copy-start
  55.1 1.5 %collective-permute-done.22.refs_1_ = f32[640,128]{1,0:T(8,128)S(1)} collective-permute-done((f32[640,128]{1,0:T(8,128)S(1)}, f32[640,128]{1,0:T(8,128)S(1)}, u32[]{:S(2)}, u32[]{:S(2)}) %collective-permute-start.22) | collective-permute-done | bytes 327712 | tf_op jit(solution)/shard_map/ppermute | solution.py:365
  56.7 0.8 %shard_map.87 = f32[640,128]{1,0:T(8,128)} custom-call(f32[640,128]{1,0:T(8,128)S(1)} %get-tuple-element.63.refs_0_, f32[640,128]{1,0:T(8,128)S(1)} %collective-permute-done.22.refs_1_, f32[4,5,32,128]{3,2,1,0:T(8,128)S(1)} %add.3.refs_2_), custom_call_target="tpu_custom_call" | custom-call | tf_op jit(solution)/shard_map/pallas_call | solution.py:350
  57.4 0.0 copy-done
  (2 shorter events, 0.1 us)
Async XLA Ops:
  0.6 7.0 %collective-permute-start.2 = (f32[640,128]{1,0:T(8,128)}, f32[640,128]{1,0:T(8,128)S(1)}, u32[]{:S(2)}, u32[]{:S(2)}) collective-permute-start(f32[640,128]{1,0:T(8,128)} %bitcast.23), channel_id=1, source_target_pairs={{0,1},{1,0},{2,3},{3,2},{4,5},{5,4},{6,7},{7,6},{8,9},{9,8},{10,11... | collective-permute-start | bytes 983048 | tf_op jit(solution)/shard_map/ppermute | solution.py:365
  2.4 19.0 %collective-permute-start.6 = (f32[648,128]{1,0:T(8,128)S(1)}, f32[648,128]{1,0:T(8,128)S(1)}, u32[]{:S(2)}, u32[]{:S(2)}) collective-permute-start(f32[648,128]{1,0:T(8,128)S(1)} %get-tuple-element.35.refs_5_), channel_id=1, source_target_pairs={{0,8},{8,0},{16,24},{24,16},{1,9},{9,1},{17,25},{25,17},{2,10},{10... | collective-permute-start | bytes 995336 | tf_op jit(solution)/shard_map/ppermute | solution.py:365
  5.1 18.1 %collective-permute-start = (f32[648,128]{1,0:T(8,128)S(1)}, f32[648,128]{1,0:T(8,128)S(1)}, u32[]{:S(2)}, u32[]{:S(2)}) collective-permute-start(f32[648,128]{1,0:T(8,128)S(1)} %get-tuple-element.35.refs_5_), channel_id=1, source_target_pairs={{0,16},{8,24},{16,0},{24,8},{1,17},{9,25},{17,1},{25,9},{2,18},{10... | collective-permute-start | bytes 995336 | tf_op jit(solution)/shard_map/ppermute | solution.py:365
  7.7 3.5 %collective-permute-start.1 = (f32[8,128]{1,0:T(8,128)S(1)}, f32[8,128]{1,0:T(8,128)S(1)}, u32[]{:S(2)}, u32[]{:S(2)}) collective-permute-start(f32[8,128]{1,0:T(8,128)S(1)} %get-tuple-element.36.refs_4_.refs_0_.refs_1_), channel_id=1, source_target_pairs={{0,1},{1,0},{2,3},{3,2},{4,5},{5,4},{6,7},{7,6},{8,9},{9,8},{10,11... | collective-permute-start | bytes 12296 | tf_op jit(solution)/shard_map/ppermute | solution.py:365
  8.1 5.6 %collective-permute-start.3 = (f32[224,128]{1,0:T(8,128)S(1)}, f32[224,128]{1,0:T(8,128)S(1)}, u32[]{:S(2)}, u32[]{:S(2)}) collective-permute-start(f32[224,128]{1,0:T(8,128)S(1)} %get-tuple-element.40), channel_id=1, source_target_pairs={{0,2},{1,3},{2,0},{3,1},{4,6},{5,7},{6,4},{7,5},{8,10},{9,11},{10,... | collective-permute-start | bytes 344072 | tf_op jit(solution)/shard_map/ppermute | solution.py:365
  9.6 7.7 %collective-permute-start.4 = (f32[224,128]{1,0:T(8,128)S(1)}, f32[224,128]{1,0:T(8,128)S(1)}, u32[]{:S(2)}, u32[]{:S(2)}) collective-permute-start(f32[224,128]{1,0:T(8,128)S(1)} %get-tuple-element.41), channel_id=1, source_target_pairs={{0,4},{1,5},{2,6},{3,7},{4,0},{5,1},{6,2},{7,3},{8,12},{9,13},{10,... | collective-permute-start | bytes 344072 | tf_op jit(solution)/shard_map/ppermute | solution.py:365
  11.2 6.2 %collective-permute-start.5 = (f32[224,128]{1,0:T(8,128)S(1)}, f32[224,128]{1,0:T(8,128)S(1)}, u32[]{:S(2)}, u32[]{:S(2)}) collective-permute-start(f32[224,128]{1,0:T(8,128)S(1)} %get-tuple-element.42), channel_id=1, source_target_pairs={{0,6},{1,7},{2,4},{3,5},{4,2},{5,3},{6,0},{7,1},{8,14},{9,15},{10,... | collective-permute-start | bytes 344072 | tf_op jit(solution)/shard_map/ppermute | solution.py:365
  17.9 7.7 %collective-permute-start.10 = (f32[2,4,6,8,128]{4,3,2,1,0:T(8,128)S(1)}, f32[2,4,6,8,128]{4,3,2,1,0:T(8,128)S(1)}, u32[]{:S(2)}, u32[]{:S(2)}) collective-permute-start(f32[2,4,6,8,128]{4,3,2,1,0:T(8,128)S(1)} %get-tuple-element.48), channel_id=1, source_target_pairs={{0,2},{1,3},{2,0},{3,1},{4,6},{5,7},{6,4},{7,5},{8,10},{9,11},{10,... | collective-permute-start | bytes 589832 | tf_op jit(solution)/shard_map/ppermute | solution.py:365
  19.2 10.5 %collective-permute-start.11 = (f32[2,4,6,8,128]{4,3,2,1,0:T(8,128)S(1)}, f32[2,4,6,8,128]{4,3,2,1,0:T(8,128)S(1)}, u32[]{:S(2)}, u32[]{:S(2)}) collective-permute-start(f32[2,4,6,8,128]{4,3,2,1,0:T(8,128)S(1)} %get-tuple-element.49), channel_id=1, source_target_pairs={{0,4},{1,5},{2,6},{3,7},{4,0},{5,1},{6,2},{7,3},{8,12},{9,13},{10,... | collective-permute-start | bytes 589832 | tf_op jit(solution)/shard_map/ppermute | solution.py:365
  20.0 9.6 %collective-permute-start.12 = (f32[2,4,6,8,128]{4,3,2,1,0:T(8,128)S(1)}, f32[2,4,6,8,128]{4,3,2,1,0:T(8,128)S(1)}, u32[]{:S(2)}, u32[]{:S(2)}) collective-permute-start(f32[2,4,6,8,128]{4,3,2,1,0:T(8,128)S(1)} %get-tuple-element.50), channel_id=1, source_target_pairs={{0,6},{1,7},{2,4},{3,5},{4,2},{5,3},{6,0},{7,1},{8,14},{9,15},{10,... | collective-permute-start | bytes 589832 | tf_op jit(solution)/shard_map/ppermute | solution.py:365
  21.5 8.8 %collective-permute-start.9 = (f32[328,128]{1,0:T(8,128)S(1)}, f32[328,128]{1,0:T(8,128)S(1)}, u32[]{:S(2)}, u32[]{:S(2)}) collective-permute-start(f32[328,128]{1,0:T(8,128)S(1)} %get-tuple-element.47), channel_id=1, source_target_pairs={{0,24},{8,16},{16,8},{24,0},{1,25},{9,17},{17,9},{25,1},{2,26},{10... | collective-permute-start | bytes 503816 | tf_op jit(solution)/shard_map/ppermute | solution.py:365
  23.6 9.1 %collective-permute-start.8 = (f32[320,128]{1,0:T(8,128)S(1)}, f32[320,128]{1,0:T(8,128)S(1)}, u32[]{:S(2)}, u32[]{:S(2)}) collective-permute-start(f32[320,128]{1,0:T(8,128)S(1)} %get-tuple-element.46), channel_id=1, source_target_pairs={{0,8},{8,0},{16,24},{24,16},{1,9},{9,1},{17,25},{25,17},{2,10},{10... | collective-permute-start | bytes 491528 | tf_op jit(solution)/shard_map/ppermute | solution.py:365
  25.6 4.7 %collective-permute-start.7 = (f32[4,32,128]{2,1,0:T(8,128)S(1)}, f32[4,32,128]{2,1,0:T(8,128)S(1)}, u32[]{:S(2)}, u32[]{:S(2)}) collective-permute-start(f32[4,32,128]{2,1,0:T(8,128)S(1)} %get-tuple-element.45), channel_id=1, source_target_pairs={{0,1},{1,0},{2,3},{3,2},{4,5},{5,4},{6,7},{7,6},{8,9},{9,8},{10,11... | collective-permute-start | bytes 196616 | tf_op jit(solution)/shard_map/ppermute | solution.py:365
  29.7 14.8 %collective-permute-start.16 = (f32[6,2,4,8,128]{4,3,2,1,0:T(8,128)S(1)}, f32[6,2,4,8,128]{4,3,2,1,0:T(8,128)S(1)}, u32[]{:S(2)}, u32[]{:S(2)}) collective-permute-start(f32[6,2,4,8,128]{4,3,2,1,0:T(8,128)S(1)} %shard_map.81.refs_10_), channel_id=1, source_target_pairs={{0,16},{8,24},{16,0},{24,8},{1,17},{9,25},{17,1},{25,9},{2,18},{10... | collective-permute-start | bytes 589832 | tf_op jit(solution)/shard_map/ppermute | solution.py:365
  33.2 7.2 %collective-permute-start.13 = (f32[2,4,5,8,128]{4,3,2,1,0:T(8,128)S(1)}, f32[2,4,5,8,128]{4,3,2,1,0:T(8,128)S(1)}, u32[]{:S(2)}, u32[]{:S(2)}) collective-permute-start(f32[2,4,5,8,128]{4,3,2,1,0:T(8,128)S(1)} %get-tuple-element.52), channel_id=1, source_target_pairs={{0,2},{1,3},{2,0},{3,1},{4,6},{5,7},{6,4},{7,5},{8,10},{9,11},{10,... | collective-permute-start | bytes 491528 | tf_op jit(solution)/shard_map/ppermute | solution.py:365
  35.5 9.0 %collective-permute-start.14 = (f32[2,4,5,8,128]{4,3,2,1,0:T(8,128)S(1)}, f32[2,4,5,8,128]{4,3,2,1,0:T(8,128)S(1)}, u32[]{:S(2)}, u32[]{:S(2)}) collective-permute-start(f32[2,4,5,8,128]{4,3,2,1,0:T(8,128)S(1)} %get-tuple-element.53), channel_id=1, source_target_pairs={{0,4},{1,5},{2,6},{3,7},{4,0},{5,1},{6,2},{7,3},{8,12},{9,13},{10,... | collective-permute-start | bytes 491528 | tf_op jit(solution)/shard_map/ppermute | solution.py:365
  36.7 7.8 %collective-permute-start.15 = (f32[2,4,5,8,128]{4,3,2,1,0:T(8,128)S(1)}, f32[2,4,5,8,128]{4,3,2,1,0:T(8,128)S(1)}, u32[]{:S(2)}, u32[]{:S(2)}) collective-permute-start(f32[2,4,5,8,128]{4,3,2,1,0:T(8,128)S(1)} %get-tuple-element.54), channel_id=1, source_target_pairs={{0,6},{1,7},{2,4},{3,5},{4,2},{5,3},{6,0},{7,1},{8,14},{9,15},{10,... | collective-permute-start | bytes 491528 | tf_op jit(solution)/shard_map/ppermute | solution.py:365
  37.4 11.1 %collective-permute-start.20 = (f32[6,2,4,8,128]{4,3,2,1,0:T(8,128)S(1)}, f32[6,2,4,8,128]{4,3,2,1,0:T(8,128)S(1)}, u32[]{:S(2)}, u32[]{:S(2)}) collective-permute-start(f32[6,2,4,8,128]{4,3,2,1,0:T(8,128)S(1)} %get-tuple-element.60), channel_id=1, source_target_pairs={{0,8},{8,0},{16,24},{24,16},{1,9},{9,1},{17,25},{25,17},{2,10},{10... | collective-permute-start | bytes 589832 | tf_op jit(solution)/shard_map/ppermute | solution.py:365
  40.3 8.6 %collective-permute-start.21 = (f32[6,2,4,8,128]{4,3,2,1,0:T(8,128)S(1)}, f32[6,2,4,8,128]{4,3,2,1,0:T(8,128)S(1)}, u32[]{:S(2)}, u32[]{:S(2)}) collective-permute-start(f32[6,2,4,8,128]{4,3,2,1,0:T(8,128)S(1)} %get-tuple-element.61), channel_id=1, source_target_pairs={{0,24},{8,16},{16,8},{24,0},{1,25},{9,17},{17,9},{25,1},{2,26},{10... | collective-permute-start | bytes 589832 | tf_op jit(solution)/shard_map/ppermute | solution.py:365
  44.9 6.9 %collective-permute-start.17 = (f32[5,2,32,128]{3,2,1,0:T(8,128)S(1)}, f32[5,2,32,128]{3,2,1,0:T(8,128)S(1)}, u32[]{:S(2)}, u32[]{:S(2)}) collective-permute-start(f32[5,2,32,128]{3,2,1,0:T(8,128)S(1)} %get-tuple-element.56), channel_id=1, source_target_pairs={{0,2},{1,3},{2,0},{3,1},{4,6},{5,7},{6,4},{7,5},{8,10},{9,11},{10,... | collective-permute-start | bytes 491528 | tf_op jit(solution)/shard_map/ppermute | solution.py:365
  46.2 8.4 %collective-permute-start.18 = (f32[5,2,32,128]{3,2,1,0:T(8,128)S(1)}, f32[5,2,32,128]{3,2,1,0:T(8,128)S(1)}, u32[]{:S(2)}, u32[]{:S(2)}) collective-permute-start(f32[5,2,32,128]{3,2,1,0:T(8,128)S(1)} %get-tuple-element.57), channel_id=1, source_target_pairs={{0,4},{1,5},{2,6},{3,7},{4,0},{5,1},{6,2},{7,3},{8,12},{9,13},{10,... | collective-permute-start | bytes 491528 | tf_op jit(solution)/shard_map/ppermute | solution.py:365
  47.5 7.1 %collective-permute-start.19 = (f32[5,2,32,128]{3,2,1,0:T(8,128)S(1)}, f32[5,2,32,128]{3,2,1,0:T(8,128)S(1)}, u32[]{:S(2)}, u32[]{:S(2)}) collective-permute-start(f32[5,2,32,128]{3,2,1,0:T(8,128)S(1)} %get-tuple-element.58), channel_id=1, source_target_pairs={{0,6},{1,7},{2,4},{3,5},{4,2},{5,3},{6,0},{7,1},{8,14},{9,15},{10,... | collective-permute-start | bytes 491528 | tf_op jit(solution)/shard_map/ppermute | solution.py:365
  52.4 2.7 %collective-permute-start.23 = (f32[4,5,32,128]{3,2,1,0:T(8,128)S(1)}, f32[4,5,32,128]{3,2,1,0:T(8,128)S(1)}, u32[]{:S(2)}, u32[]{:S(2)}) collective-permute-start(f32[4,5,32,128]{3,2,1,0:T(8,128)S(1)} %get-tuple-element.62.refs_5_), channel_id=1, source_target_pairs={{0,1},{1,0},{2,3},{3,2},{4,5},{5,4},{6,7},{7,6},{8,9},{9,8},{10,11... | collective-permute-start | bytes 983048 | tf_op jit(solution)/shard_map/ppermute | solution.py:365
  55.0 1.7 %collective-permute-start.22 = (f32[640,128]{1,0:T(8,128)S(1)}, f32[640,128]{1,0:T(8,128)S(1)}, u32[]{:S(2)}, u32[]{:S(2)}) collective-permute-start(f32[640,128]{1,0:T(8,128)S(1)} %get-tuple-element.64), channel_id=1, source_target_pairs={{0,1},{1,0},{2,3},{3,2},{4,5},{5,4},{6,7},{7,6},{8,9},{9,8},{10,11... | collective-permute-start | bytes 983048 | tf_op jit(solution)/shard_map/ppermute | solution.py:365
  55.1 2.3 %copy-start = (f32[4,5,32,128]{3,2,1,0:T(8,128)}, f32[4,5,32,128]{3,2,1,0:T(8,128)S(1)}, u32[]{:S(2)}) copy-start(f32[4,5,32,128]{3,2,1,0:T(8,128)S(1)} %add.3.refs_2_) | copy-start | bytes 983044

commit v6 on v5

--- a/solution.py
+++ b/solution.py
@@ -390,7 +390,7 @@
     inverse = diffusion_inverse[0]
     dest = dest_slot[0]
 
-    cut = row_total * fields // 2
+    cut = blocks * (2 * lev_dev * fields // 5)
     packed, second_half, mine, cot_here, weights_here, inverse_here = call(
         pack_kernel,
         dims,

time: 57.7 us -> 56.6 us (0.981)
  waiting for transfers between devices: 23.9 us -> 22.1 us
  starting transfers between devices: 27.5 us -> 28.2 us
    ppermute x24, waiting for transfers between devices: 23.9 us -> 22.1 us  [swap(): return lax.ppermute(array, axis, [(i, i ^ bit) for i in range(count)])]
    ppermute x24, starting transfers between devices: 27.5 us -> 28.2 us  [swap(): return lax.ppermute(array, axis, [(i, i ^ bit) for i in range(count)])]
  transfers between devices with their start and end apart: 24 -> 24, of which waited for: 12 -> 14; matrix products, arithmetic and copies ran while one was open for 0% -> 0% of each run, Pallas kernels for 8% -> 8%
where the time goes in v6:
time: 56.6 us; the launch traced here: 56.4 us
  starting transfers between devices  28.2 us (50%)
  waiting for transfers between devices  22.1 us (39%)
  Pallas kernels  5.17 us (9%)
  between operations  0.78 us (1%)
    ppermute x24, starting transfers between devices, swap(): return lax.ppermute(array, axis, [(i, i ^ bit) for i in range(count)])  28.2 us
    ppermute x24, waiting for transfers between devices, swap(): return lax.ppermute(array, axis, [(i, i ^ bit) for i in range(count)])  22.1 us
    pallas_call x11, Pallas kernels, call(): pl.pallas_call(functools.partial(kernel, dims) if outside else lambda *re...  5.17 us
  transfers between devices with their start and end apart: 24, of which 14 were waited for; matrix products, arithmetic and copies ran while one was open for 0% of the time, Pallas kernels for 8%

profile of v6, /device:TPU:0, one launch (start us, length us, event | category | flops | bytes accessed | tf_op | source)
XLA Modules:
  0.0 56.4 jit_solution(4333034426176707603)
XLA Ops:
  0.6 0.5 collective-permute-start.2
  1.1 1.3 %shard_map.77 = (f32[648,128]{1,0:T(8,128)S(1)}, f32[392,128]{1,0:T(8,128)S(1)}, f32[8,128]{1,0:T(8,128)S(1)}, f32[640,128]{1,0:T(8,128)S(1)}, f32[128,128]{1,0:T(8,128)S(1)}, /*index=5*/f32[5,32,32]{2,1,0:T(8,128)S(1)}) custom-call(f32[640,128]{1,0:T(8,128)} %bitcast.22, s32[4,8,8]{2,1,0:T(8,128)} %bitcast.27, s32[1,128]{1,0:T(1,128)} %bitcast.28, ...), custom_call_target="tpu_custom_call" | custom-call | tf_op jit(solution)/shard_map/pallas_call | solution.py:350
  2.4 2.7 %collective-permute-start.6 = (f32[648,128]{1,0:T(8,128)S(1)}, f32[648,128]{1,0:T(8,128)S(1)}, u32[]{:S(2)}, u32[]{:S(2)}) collective-permute-start(f32[648,128]{1,0:T(8,128)S(1)} %get-tuple-element.35.refs_5_), channel_id=1, source_target_pairs={{0,8},{8,0},{16,24},{24,16},{1,9},{9,1},{17,25},{25,17},{2,10},{10... | collective-permute-start | bytes 995336 | tf_op jit(solution)/shard_map/ppermute | solution.py:365
  5.1 2.6 %collective-permute-start = (f32[648,128]{1,0:T(8,128)S(1)}, f32[648,128]{1,0:T(8,128)S(1)}, u32[]{:S(2)}, u32[]{:S(2)}) collective-permute-start(f32[648,128]{1,0:T(8,128)S(1)} %get-tuple-element.35.refs_5_), channel_id=1, source_target_pairs={{0,16},{8,24},{16,0},{24,8},{1,17},{9,25},{17,1},{25,9},{2,18},{10... | collective-permute-start | bytes 995336 | tf_op jit(solution)/shard_map/ppermute | solution.py:365
  7.7 0.0 collective-permute-start.1
  7.7 0.0 collective-permute-done.2.refs_2_
  7.7 0.4 shard_map.78
  8.1 1.6 %collective-permute-start.3 = (f32[224,128]{1,0:T(8,128)S(1)}, f32[224,128]{1,0:T(8,128)S(1)}, u32[]{:S(2)}, u32[]{:S(2)}) collective-permute-start(f32[224,128]{1,0:T(8,128)S(1)} %get-tuple-element.40), channel_id=1, source_target_pairs={{0,2},{1,3},{2,0},{3,1},{4,6},{5,7},{6,4},{7,5},{8,10},{9,11},{10,... | collective-permute-start | bytes 344072 | tf_op jit(solution)/shard_map/ppermute | solution.py:365
  9.7 1.5 %collective-permute-start.4 = (f32[224,128]{1,0:T(8,128)S(1)}, f32[224,128]{1,0:T(8,128)S(1)}, u32[]{:S(2)}, u32[]{:S(2)}) collective-permute-start(f32[224,128]{1,0:T(8,128)S(1)} %get-tuple-element.41), channel_id=1, source_target_pairs={{0,4},{1,5},{2,6},{3,7},{4,0},{5,1},{6,2},{7,3},{8,12},{9,13},{10,... | collective-permute-start | bytes 344072 | tf_op jit(solution)/shard_map/ppermute | solution.py:365
  11.2 0.0 collective-permute-done.1.refs_6_.refs_2_.refs_1_
  11.2 0.5 collective-permute-start.5
  11.6 2.1 %collective-permute-done.3.refs_3_.refs_2_ = f32[224,128]{1,0:T(8,128)S(1)} collective-permute-done((f32[224,128]{1,0:T(8,128)S(1)}, f32[224,128]{1,0:T(8,128)S(1)}, u32[]{:S(2)}, u32[]{:S(2)}) %collective-permute-start.3) | collective-permute-done | bytes 114720 | tf_op jit(solution)/shard_map/ppermute | solution.py:365
  13.7 3.7 %collective-permute-done.4.refs_4_.refs_3_ = f32[224,128]{1,0:T(8,128)S(1)} collective-permute-done((f32[224,128]{1,0:T(8,128)S(1)}, f32[224,128]{1,0:T(8,128)S(1)}, u32[]{:S(2)}, u32[]{:S(2)}) %collective-permute-start.4) | collective-permute-done | bytes 114720 | tf_op jit(solution)/shard_map/ppermute | solution.py:365
  17.4 0.0 collective-permute-done.5.refs_5_.refs_4_
  17.4 0.5 shard_map.79
  17.9 1.3 %collective-permute-start.10 = (f32[2,4,6,8,128]{4,3,2,1,0:T(8,128)S(1)}, f32[2,4,6,8,128]{4,3,2,1,0:T(8,128)S(1)}, u32[]{:S(2)}, u32[]{:S(2)}) collective-permute-start(f32[2,4,6,8,128]{4,3,2,1,0:T(8,128)S(1)} %get-tuple-element.48), channel_id=1, source_target_pairs={{0,2},{1,3},{2,0},{3,1},{4,6},{5,7},{6,4},{7,5},{8,10},{9,11},{10,... | collective-permute-start | bytes 589832 | tf_op jit(solution)/shard_map/ppermute | solution.py:365
  19.2 0.2 collective-permute-start.9
  19.5 0.8 %collective-permute-start.11 = (f32[2,4,6,8,128]{4,3,2,1,0:T(8,128)S(1)}, f32[2,4,6,8,128]{4,3,2,1,0:T(8,128)S(1)}, u32[]{:S(2)}, u32[]{:S(2)}) collective-permute-start(f32[2,4,6,8,128]{4,3,2,1,0:T(8,128)S(1)} %get-tuple-element.49), channel_id=1, source_target_pairs={{0,4},{1,5},{2,6},{3,7},{4,0},{5,1},{6,2},{7,3},{8,12},{9,13},{10,... | collective-permute-start | bytes 589832 | tf_op jit(solution)/shard_map/ppermute | solution.py:365
  20.3 0.3 collective-permute-done.6.refs_4_.refs_6_
  20.6 2.6 %collective-permute-start.12 = (f32[2,4,6,8,128]{4,3,2,1,0:T(8,128)S(1)}, f32[2,4,6,8,128]{4,3,2,1,0:T(8,128)S(1)}, u32[]{:S(2)}, u32[]{:S(2)}) collective-permute-start(f32[2,4,6,8,128]{4,3,2,1,0:T(8,128)S(1)} %get-tuple-element.50), channel_id=1, source_target_pairs={{0,6},{1,7},{2,4},{3,5},{4,2},{5,3},{6,0},{7,1},{8,14},{9,15},{10,... | collective-permute-start | bytes 589832 | tf_op jit(solution)/shard_map/ppermute | solution.py:365
  23.2 4.3 %collective-permute-done.refs_0_.refs_7_ = f32[648,128]{1,0:T(8,128)S(1)} collective-permute-done((f32[648,128]{1,0:T(8,128)S(1)}, f32[648,128]{1,0:T(8,128)S(1)}, u32[]{:S(2)}, u32[]{:S(2)}) %collective-permute-start) | collective-permute-done | bytes 331808 | tf_op jit(solution)/shard_map/ppermute | solution.py:365
  27.4 0.3 shard_map.80
  27.8 0.4 collective-permute-start.8
  28.1 0.0 collective-permute-done.10.refs_1_
  28.1 0.0 collective-permute-start.7
  28.2 1.6 %collective-permute-done.11.refs_2_ = f32[2,4,6,8,128]{4,3,2,1,0:T(8,128)S(1)} collective-permute-done((f32[2,4,6,8,128]{4,3,2,1,0:T(8,128)S(1)}, f32[2,4,6,8,128]{4,3,2,1,0:T(8,128)S(1)}, u32[]{:S(2)}, u32[]{:S(2)}) %collective-permute-start.11) | collective-permute-done | bytes 196640 | tf_op jit(solution)/shard_map/ppermute | solution.py:365
  29.7 0.0 collective-permute-done.12.refs_3_
  29.7 1.9 %collective-permute-start.16 = (f32[6,2,4,8,128]{4,3,2,1,0:T(8,128)S(1)}, f32[6,2,4,8,128]{4,3,2,1,0:T(8,128)S(1)}, u32[]{:S(2)}, u32[]{:S(2)}) collective-permute-start(f32[6,2,4,8,128]{4,3,2,1,0:T(8,128)S(1)} %shard_map.81.refs_10_), channel_id=1, source_target_pairs={{0,16},{8,24},{16,0},{24,8},{1,17},{9,25},{17,1},{25,9},{2,18},{10... | collective-permute-start | bytes 589832 | tf_op jit(solution)/shard_map/ppermute | solution.py:365
  31.7 0.0 collective-permute-done.9.refs_9_
  31.7 0.0 collective-permute-done.7.refs_0_
  31.7 1.1 %collective-permute-done.8.refs_8_ = f32[256,128]{1,0:T(8,128)S(1)} collective-permute-done((f32[256,128]{1,0:T(8,128)S(1)}, f32[256,128]{1,0:T(8,128)S(1)}, u32[]{:S(2)}, u32[]{:S(2)}) %collective-permute-start.8) | collective-permute-done | bytes 131104 | tf_op jit(solution)/shard_map/ppermute | solution.py:365
  32.8 0.5 shard_map.82
  33.3 1.6 %collective-permute-start.13 = (f32[2,4,5,8,128]{4,3,2,1,0:T(8,128)S(1)}, f32[2,4,5,8,128]{4,3,2,1,0:T(8,128)S(1)}, u32[]{:S(2)}, u32[]{:S(2)}) collective-permute-start(f32[2,4,5,8,128]{4,3,2,1,0:T(8,128)S(1)} %get-tuple-element.52), channel_id=1, source_target_pairs={{0,2},{1,3},{2,0},{3,1},{4,6},{5,7},{6,4},{7,5},{8,10},{9,11},{10,... | collective-permute-start | bytes 491528 | tf_op jit(solution)/shard_map/ppermute | solution.py:365
  34.9 1.5 %collective-permute-start.14 = (f32[2,4,5,8,128]{4,3,2,1,0:T(8,128)S(1)}, f32[2,4,5,8,128]{4,3,2,1,0:T(8,128)S(1)}, u32[]{:S(2)}, u32[]{:S(2)}) collective-permute-start(f32[2,4,5,8,128]{4,3,2,1,0:T(8,128)S(1)} %get-tuple-element.53), channel_id=1, source_target_pairs={{0,4},{1,5},{2,6},{3,7},{4,0},{5,1},{6,2},{7,3},{8,12},{9,13},{10,... | collective-permute-start | bytes 491528 | tf_op jit(solution)/shard_map/ppermute | solution.py:365
  36.4 0.5 collective-permute-start.15
  36.9 0.1 shard_map.84
  36.9 1.2 %collective-permute-start.20 = (f32[6,2,4,8,128]{4,3,2,1,0:T(8,128)S(1)}, f32[6,2,4,8,128]{4,3,2,1,0:T(8,128)S(1)}, u32[]{:S(2)}, u32[]{:S(2)}) collective-permute-start(f32[6,2,4,8,128]{4,3,2,1,0:T(8,128)S(1)} %get-tuple-element.60), channel_id=1, source_target_pairs={{0,8},{8,0},{16,24},{24,16},{1,9},{9,1},{17,25},{25,17},{2,10},{10... | collective-permute-start | bytes 589832 | tf_op jit(solution)/shard_map/ppermute | solution.py:365
  38.1 1.9 %collective-permute-done.13.refs_2_ = f32[2,4,5,8,128]{4,3,2,1,0:T(8,128)S(1)} collective-permute-done((f32[2,4,5,8,128]{4,3,2,1,0:T(8,128)S(1)}, f32[2,4,5,8,128]{4,3,2,1,0:T(8,128)S(1)}, u32[]{:S(2)}, u32[]{:S(2)}) %collective-permute-start.13) | collective-permute-done | bytes 163872 | tf_op jit(solution)/shard_map/ppermute | solution.py:365
  40.0 3.2 %collective-permute-start.21 = (f32[6,2,4,8,128]{4,3,2,1,0:T(8,128)S(1)}, f32[6,2,4,8,128]{4,3,2,1,0:T(8,128)S(1)}, u32[]{:S(2)}, u32[]{:S(2)}) collective-permute-start(f32[6,2,4,8,128]{4,3,2,1,0:T(8,128)S(1)} %get-tuple-element.61), channel_id=1, source_target_pairs={{0,24},{8,16},{16,8},{24,0},{1,25},{9,17},{17,9},{25,1},{2,26},{10... | collective-permute-start | bytes 589832 | tf_op jit(solution)/shard_map/ppermute | solution.py:365
  43.2 0.5 collective-permute-done.14.refs_3_
  43.7 0.0 collective-permute-done.15.refs_4_
  43.7 0.7 %collective-permute-done.16.refs_5_.refs_4_ = f32[6,2,4,8,128]{4,3,2,1,0:T(8,128)S(1)} collective-permute-done((f32[6,2,4,8,128]{4,3,2,1,0:T(8,128)S(1)}, f32[6,2,4,8,128]{4,3,2,1,0:T(8,128)S(1)}, u32[]{:S(2)}, u32[]{:S(2)}) %collective-permute-start.16) | collective-permute-done | bytes 196640 | tf_op jit(solution)/shard_map/ppermute | solution.py:365
  44.4 0.4 shard_map.83
  44.9 0.9 %collective-permute-start.17 = (f32[5,2,32,128]{3,2,1,0:T(8,128)S(1)}, f32[5,2,32,128]{3,2,1,0:T(8,128)S(1)}, u32[]{:S(2)}, u32[]{:S(2)}) collective-permute-start(f32[5,2,32,128]{3,2,1,0:T(8,128)S(1)} %get-tuple-element.56), channel_id=1, source_target_pairs={{0,2},{1,3},{2,0},{3,1},{4,6},{5,7},{6,4},{7,5},{8,10},{9,11},{10,... | collective-permute-start | bytes 491528 | tf_op jit(solution)/shard_map/ppermute | solution.py:365
  45.8 1.6 %collective-permute-start.18 = (f32[5,2,32,128]{3,2,1,0:T(8,128)S(1)}, f32[5,2,32,128]{3,2,1,0:T(8,128)S(1)}, u32[]{:S(2)}, u32[]{:S(2)}) collective-permute-start(f32[5,2,32,128]{3,2,1,0:T(8,128)S(1)} %get-tuple-element.57), channel_id=1, source_target_pairs={{0,4},{1,5},{2,6},{3,7},{4,0},{5,1},{6,2},{7,3},{8,12},{9,13},{10,... | collective-permute-start | bytes 491528 | tf_op jit(solution)/shard_map/ppermute | solution.py:365
  47.3 1.1 %collective-permute-start.19 = (f32[5,2,32,128]{3,2,1,0:T(8,128)S(1)}, f32[5,2,32,128]{3,2,1,0:T(8,128)S(1)}, u32[]{:S(2)}, u32[]{:S(2)}) collective-permute-start(f32[5,2,32,128]{3,2,1,0:T(8,128)S(1)} %get-tuple-element.58), channel_id=1, source_target_pairs={{0,6},{1,7},{2,4},{3,5},{4,2},{5,3},{6,0},{7,1},{8,14},{9,15},{10,... | collective-permute-start | bytes 491528 | tf_op jit(solution)/shard_map/ppermute | solution.py:365
  48.4 1.1 %collective-permute-done.20.refs_3_ = f32[6,2,4,8,128]{4,3,2,1,0:T(8,128)S(1)} collective-permute-done((f32[6,2,4,8,128]{4,3,2,1,0:T(8,128)S(1)}, f32[6,2,4,8,128]{4,3,2,1,0:T(8,128)S(1)}, u32[]{:S(2)}, u32[]{:S(2)}) %collective-permute-start.20) | collective-permute-done | bytes 196640 | tf_op jit(solution)/shard_map/ppermute | solution.py:365
  49.6 0.0 collective-permute-done.21.refs_5_
  49.6 0.9 %collective-permute-done.17.refs_6_.refs_2_ = f32[5,2,32,128]{3,2,1,0:T(8,128)S(1)} collective-permute-done((f32[5,2,32,128]{3,2,1,0:T(8,128)S(1)}, f32[5,2,32,128]{3,2,1,0:T(8,128)S(1)}, u32[]{:S(2)}, u32[]{:S(2)}) %collective-permute-start.17) | collective-permute-done | bytes 163872 | tf_op jit(solution)/shard_map/ppermute | solution.py:365
  50.4 0.5 shard_map.85
  50.9 0.1 collective-permute-start.23
  51.0 0.9 %collective-permute-done.18.refs_3_ = f32[5,2,32,128]{3,2,1,0:T(8,128)S(1)} collective-permute-done((f32[5,2,32,128]{3,2,1,0:T(8,128)S(1)}, f32[5,2,32,128]{3,2,1,0:T(8,128)S(1)}, u32[]{:S(2)}, u32[]{:S(2)}) %collective-permute-start.18) | collective-permute-done | bytes 163872 | tf_op jit(solution)/shard_map/ppermute | solution.py:365
  52.0 1.6 %collective-permute-done.19.refs_4_ = f32[5,2,32,128]{3,2,1,0:T(8,128)S(1)} collective-permute-done((f32[5,2,32,128]{3,2,1,0:T(8,128)S(1)}, f32[5,2,32,128]{3,2,1,0:T(8,128)S(1)}, u32[]{:S(2)}, u32[]{:S(2)}) %collective-permute-start.19) | collective-permute-done | bytes 163872 | tf_op jit(solution)/shard_map/ppermute | solution.py:365
  53.5 0.3 shard_map.86
  53.9 0.1 collective-permute-start.22
  54.0 0.0 collective-permute-done.23
  54.0 0.0 copy-start
  54.0 1.5 %collective-permute-done.22.refs_1_ = f32[640,128]{1,0:T(8,128)S(1)} collective-permute-done((f32[640,128]{1,0:T(8,128)S(1)}, f32[640,128]{1,0:T(8,128)S(1)}, u32[]{:S(2)}, u32[]{:S(2)}) %collective-permute-start.22) | collective-permute-done | bytes 327712 | tf_op jit(solution)/shard_map/ppermute | solution.py:365
  55.6 0.8 %shard_map.87 = f32[640,128]{1,0:T(8,128)} custom-call(f32[640,128]{1,0:T(8,128)S(1)} %get-tuple-element.63.refs_0_, f32[640,128]{1,0:T(8,128)S(1)} %collective-permute-done.22.refs_1_, f32[4,5,32,128]{3,2,1,0:T(8,128)S(1)} %add.3.refs_2_), custom_call_target="tpu_custom_call" | custom-call | tf_op jit(solution)/shard_map/pallas_call | solution.py:350
  56.4 0.0 copy-done
  (2 shorter events, 0.1 us)
Async XLA Ops:
  0.6 7.1 %collective-permute-start.2 = (f32[640,128]{1,0:T(8,128)}, f32[640,128]{1,0:T(8,128)S(1)}, u32[]{:S(2)}, u32[]{:S(2)}) collective-permute-start(f32[640,128]{1,0:T(8,128)} %bitcast.23), channel_id=1, source_target_pairs={{0,1},{1,0},{2,3},{3,2},{4,5},{5,4},{6,7},{7,6},{8,9},{9,8},{10,11... | collective-permute-start | bytes 983048 | tf_op jit(solution)/shard_map/ppermute | solution.py:365
  2.4 18.1 %collective-permute-start.6 = (f32[648,128]{1,0:T(8,128)S(1)}, f32[648,128]{1,0:T(8,128)S(1)}, u32[]{:S(2)}, u32[]{:S(2)}) collective-permute-start(f32[648,128]{1,0:T(8,128)S(1)} %get-tuple-element.35.refs_5_), channel_id=1, source_target_pairs={{0,8},{8,0},{16,24},{24,16},{1,9},{9,1},{17,25},{25,17},{2,10},{10... | collective-permute-start | bytes 995336 | tf_op jit(solution)/shard_map/ppermute | solution.py:365
  5.1 22.3 %collective-permute-start = (f32[648,128]{1,0:T(8,128)S(1)}, f32[648,128]{1,0:T(8,128)S(1)}, u32[]{:S(2)}, u32[]{:S(2)}) collective-permute-start(f32[648,128]{1,0:T(8,128)S(1)} %get-tuple-element.35.refs_5_), channel_id=1, source_target_pairs={{0,16},{8,24},{16,0},{24,8},{1,17},{9,25},{17,1},{25,9},{2,18},{10... | collective-permute-start | bytes 995336 | tf_op jit(solution)/shard_map/ppermute | solution.py:365
  7.7 3.5 %collective-permute-start.1 = (f32[8,128]{1,0:T(8,128)S(1)}, f32[8,128]{1,0:T(8,128)S(1)}, u32[]{:S(2)}, u32[]{:S(2)}) collective-permute-start(f32[8,128]{1,0:T(8,128)S(1)} %get-tuple-element.36.refs_4_.refs_0_.refs_1_), channel_id=1, source_target_pairs={{0,1},{1,0},{2,3},{3,2},{4,5},{5,4},{6,7},{7,6},{8,9},{9,8},{10,11... | collective-permute-start | bytes 12296 | tf_op jit(solution)/shard_map/ppermute | solution.py:365
  8.1 5.6 %collective-permute-start.3 = (f32[224,128]{1,0:T(8,128)S(1)}, f32[224,128]{1,0:T(8,128)S(1)}, u32[]{:S(2)}, u32[]{:S(2)}) collective-permute-start(f32[224,128]{1,0:T(8,128)S(1)} %get-tuple-element.40), channel_id=1, source_target_pairs={{0,2},{1,3},{2,0},{3,1},{4,6},{5,7},{6,4},{7,5},{8,10},{9,11},{10,... | collective-permute-start | bytes 344072 | tf_op jit(solution)/shard_map/ppermute | solution.py:365
  9.7 7.7 %collective-permute-start.4 = (f32[224,128]{1,0:T(8,128)S(1)}, f32[224,128]{1,0:T(8,128)S(1)}, u32[]{:S(2)}, u32[]{:S(2)}) collective-permute-start(f32[224,128]{1,0:T(8,128)S(1)} %get-tuple-element.41), channel_id=1, source_target_pairs={{0,4},{1,5},{2,6},{3,7},{4,0},{5,1},{6,2},{7,3},{8,12},{9,13},{10,... | collective-permute-start | bytes 344072 | tf_op jit(solution)/shard_map/ppermute | solution.py:365
  11.2 6.2 %collective-permute-start.5 = (f32[224,128]{1,0:T(8,128)S(1)}, f32[224,128]{1,0:T(8,128)S(1)}, u32[]{:S(2)}, u32[]{:S(2)}) collective-permute-start(f32[224,128]{1,0:T(8,128)S(1)} %get-tuple-element.42), channel_id=1, source_target_pairs={{0,6},{1,7},{2,4},{3,5},{4,2},{5,3},{6,0},{7,1},{8,14},{9,15},{10,... | collective-permute-start | bytes 344072 | tf_op jit(solution)/shard_map/ppermute | solution.py:365
  17.9 10.2 %collective-permute-start.10 = (f32[2,4,6,8,128]{4,3,2,1,0:T(8,128)S(1)}, f32[2,4,6,8,128]{4,3,2,1,0:T(8,128)S(1)}, u32[]{:S(2)}, u32[]{:S(2)}) collective-permute-start(f32[2,4,6,8,128]{4,3,2,1,0:T(8,128)S(1)} %get-tuple-element.48), channel_id=1, source_target_pairs={{0,2},{1,3},{2,0},{3,1},{4,6},{5,7},{6,4},{7,5},{8,10},{9,11},{10,... | collective-permute-start | bytes 589832 | tf_op jit(solution)/shard_map/ppermute | solution.py:365
  19.2 12.4 %collective-permute-start.9 = (f32[392,128]{1,0:T(8,128)S(1)}, f32[392,128]{1,0:T(8,128)S(1)}, u32[]{:S(2)}, u32[]{:S(2)}) collective-permute-start(f32[392,128]{1,0:T(8,128)S(1)} %get-tuple-element.47), channel_id=1, source_target_pairs={{0,24},{8,16},{16,8},{24,0},{1,25},{9,17},{17,9},{25,1},{2,26},{10... | collective-permute-start | bytes 602120 | tf_op jit(solution)/shard_map/ppermute | solution.py:365
  19.5 10.2 %collective-permute-start.11 = (f32[2,4,6,8,128]{4,3,2,1,0:T(8,128)S(1)}, f32[2,4,6,8,128]{4,3,2,1,0:T(8,128)S(1)}, u32[]{:S(2)}, u32[]{:S(2)}) collective-permute-start(f32[2,4,6,8,128]{4,3,2,1,0:T(8,128)S(1)} %get-tuple-element.49), channel_id=1, source_target_pairs={{0,4},{1,5},{2,6},{3,7},{4,0},{5,1},{6,2},{7,3},{8,12},{9,13},{10,... | collective-permute-start | bytes 589832 | tf_op jit(solution)/shard_map/ppermute | solution.py:365
  20.6 9.2 %collective-permute-start.12 = (f32[2,4,6,8,128]{4,3,2,1,0:T(8,128)S(1)}, f32[2,4,6,8,128]{4,3,2,1,0:T(8,128)S(1)}, u32[]{:S(2)}, u32[]{:S(2)}) collective-permute-start(f32[2,4,6,8,128]{4,3,2,1,0:T(8,128)S(1)} %get-tuple-element.50), channel_id=1, source_target_pairs={{0,6},{1,7},{2,4},{3,5},{4,2},{5,3},{6,0},{7,1},{8,14},{9,15},{10,... | collective-permute-start | bytes 589832 | tf_op jit(solution)/shard_map/ppermute | solution.py:365
  27.8 5.0 %collective-permute-start.8 = (f32[256,128]{1,0:T(8,128)S(1)}, f32[256,128]{1,0:T(8,128)S(1)}, u32[]{:S(2)}, u32[]{:S(2)}) collective-permute-start(f32[256,128]{1,0:T(8,128)S(1)} %get-tuple-element.46), channel_id=1, source_target_pairs={{0,8},{8,0},{16,24},{24,16},{1,9},{9,1},{17,25},{25,17},{2,10},{10... | collective-permute-start | bytes 393224 | tf_op jit(solution)/shard_map/ppermute | solution.py:365
  28.1 3.5 %collective-permute-start.7 = (f32[4,32,128]{2,1,0:T(8,128)S(1)}, f32[4,32,128]{2,1,0:T(8,128)S(1)}, u32[]{:S(2)}, u32[]{:S(2)}) collective-permute-start(f32[4,32,128]{2,1,0:T(8,128)S(1)} %get-tuple-element.45), channel_id=1, source_target_pairs={{0,1},{1,0},{2,3},{3,2},{4,5},{5,4},{6,7},{7,6},{8,9},{9,8},{10,11... | collective-permute-start | bytes 196616 | tf_op jit(solution)/shard_map/ppermute | solution.py:365
  29.7 14.7 %collective-permute-start.16 = (f32[6,2,4,8,128]{4,3,2,1,0:T(8,128)S(1)}, f32[6,2,4,8,128]{4,3,2,1,0:T(8,128)S(1)}, u32[]{:S(2)}, u32[]{:S(2)}) collective-permute-start(f32[6,2,4,8,128]{4,3,2,1,0:T(8,128)S(1)} %shard_map.81.refs_10_), channel_id=1, source_target_pairs={{0,16},{8,24},{16,0},{24,8},{1,17},{9,25},{17,1},{25,9},{2,18},{10... | collective-permute-start | bytes 589832 | tf_op jit(solution)/shard_map/ppermute | solution.py:365
  33.3 6.7 %collective-permute-start.13 = (f32[2,4,5,8,128]{4,3,2,1,0:T(8,128)S(1)}, f32[2,4,5,8,128]{4,3,2,1,0:T(8,128)S(1)}, u32[]{:S(2)}, u32[]{:S(2)}) collective-permute-start(f32[2,4,5,8,128]{4,3,2,1,0:T(8,128)S(1)} %get-tuple-element.52), channel_id=1, source_target_pairs={{0,2},{1,3},{2,0},{3,1},{4,6},{5,7},{6,4},{7,5},{8,10},{9,11},{10,... | collective-permute-start | bytes 491528 | tf_op jit(solution)/shard_map/ppermute | solution.py:365
  34.9 8.8 %collective-permute-start.14 = (f32[2,4,5,8,128]{4,3,2,1,0:T(8,128)S(1)}, f32[2,4,5,8,128]{4,3,2,1,0:T(8,128)S(1)}, u32[]{:S(2)}, u32[]{:S(2)}) collective-permute-start(f32[2,4,5,8,128]{4,3,2,1,0:T(8,128)S(1)} %get-tuple-element.53), channel_id=1, source_target_pairs={{0,4},{1,5},{2,6},{3,7},{4,0},{5,1},{6,2},{7,3},{8,12},{9,13},{10,... | collective-permute-start | bytes 491528 | tf_op jit(solution)/shard_map/ppermute | solution.py:365
  36.4 7.3 %collective-permute-start.15 = (f32[2,4,5,8,128]{4,3,2,1,0:T(8,128)S(1)}, f32[2,4,5,8,128]{4,3,2,1,0:T(8,128)S(1)}, u32[]{:S(2)}, u32[]{:S(2)}) collective-permute-start(f32[2,4,5,8,128]{4,3,2,1,0:T(8,128)S(1)} %get-tuple-element.54), channel_id=1, source_target_pairs={{0,6},{1,7},{2,4},{3,5},{4,2},{5,3},{6,0},{7,1},{8,14},{9,15},{10,... | collective-permute-start | bytes 491528 | tf_op jit(solution)/shard_map/ppermute | solution.py:365
  36.9 12.6 %collective-permute-start.20 = (f32[6,2,4,8,128]{4,3,2,1,0:T(8,128)S(1)}, f32[6,2,4,8,128]{4,3,2,1,0:T(8,128)S(1)}, u32[]{:S(2)}, u32[]{:S(2)}) collective-permute-start(f32[6,2,4,8,128]{4,3,2,1,0:T(8,128)S(1)} %get-tuple-element.60), channel_id=1, source_target_pairs={{0,8},{8,0},{16,24},{24,16},{1,9},{9,1},{17,25},{25,17},{2,10},{10... | collective-permute-start | bytes 589832 | tf_op jit(solution)/shard_map/ppermute | solution.py:365
  40.0 9.5 %collective-permute-start.21 = (f32[6,2,4,8,128]{4,3,2,1,0:T(8,128)S(1)}, f32[6,2,4,8,128]{4,3,2,1,0:T(8,128)S(1)}, u32[]{:S(2)}, u32[]{:S(2)}) collective-permute-start(f32[6,2,4,8,128]{4,3,2,1,0:T(8,128)S(1)} %get-tuple-element.61), channel_id=1, source_target_pairs={{0,24},{8,16},{16,8},{24,0},{1,25},{9,17},{17,9},{25,1},{2,26},{10... | collective-permute-start | bytes 589832 | tf_op jit(solution)/shard_map/ppermute | solution.py:365
  44.9 5.6 %collective-permute-start.17 = (f32[5,2,32,128]{3,2,1,0:T(8,128)S(1)}, f32[5,2,32,128]{3,2,1,0:T(8,128)S(1)}, u32[]{:S(2)}, u32[]{:S(2)}) collective-permute-start(f32[5,2,32,128]{3,2,1,0:T(8,128)S(1)} %get-tuple-element.56), channel_id=1, source_target_pairs={{0,2},{1,3},{2,0},{3,1},{4,6},{5,7},{6,4},{7,5},{8,10},{9,11},{10,... | collective-permute-start | bytes 491528 | tf_op jit(solution)/shard_map/ppermute | solution.py:365
  45.8 6.2 %collective-permute-start.18 = (f32[5,2,32,128]{3,2,1,0:T(8,128)S(1)}, f32[5,2,32,128]{3,2,1,0:T(8,128)S(1)}, u32[]{:S(2)}, u32[]{:S(2)}) collective-permute-start(f32[5,2,32,128]{3,2,1,0:T(8,128)S(1)} %get-tuple-element.57), channel_id=1, source_target_pairs={{0,4},{1,5},{2,6},{3,7},{4,0},{5,1},{6,2},{7,3},{8,12},{9,13},{10,... | collective-permute-start | bytes 491528 | tf_op jit(solution)/shard_map/ppermute | solution.py:365
  47.3 6.2 %collective-permute-start.19 = (f32[5,2,32,128]{3,2,1,0:T(8,128)S(1)}, f32[5,2,32,128]{3,2,1,0:T(8,128)S(1)}, u32[]{:S(2)}, u32[]{:S(2)}) collective-permute-start(f32[5,2,32,128]{3,2,1,0:T(8,128)S(1)} %get-tuple-element.58), channel_id=1, source_target_pairs={{0,6},{1,7},{2,4},{3,5},{4,2},{5,3},{6,0},{7,1},{8,14},{9,15},{10,... | collective-permute-start | bytes 491528 | tf_op jit(solution)/shard_map/ppermute | solution.py:365
  50.9 3.0 %collective-permute-start.23 = (f32[4,5,32,128]{3,2,1,0:T(8,128)S(1)}, f32[4,5,32,128]{3,2,1,0:T(8,128)S(1)}, u32[]{:S(2)}, u32[]{:S(2)}) collective-permute-start(f32[4,5,32,128]{3,2,1,0:T(8,128)S(1)} %get-tuple-element.62.refs_5_), channel_id=1, source_target_pairs={{0,1},{1,0},{2,3},{3,2},{4,5},{5,4},{6,7},{7,6},{8,9},{9,8},{10,11... | collective-permute-start | bytes 983048 | tf_op jit(solution)/shard_map/ppermute | solution.py:365
  53.9 1.7 %collective-permute-start.22 = (f32[640,128]{1,0:T(8,128)S(1)}, f32[640,128]{1,0:T(8,128)S(1)}, u32[]{:S(2)}, u32[]{:S(2)}) collective-permute-start(f32[640,128]{1,0:T(8,128)S(1)} %get-tuple-element.64), channel_id=1, source_target_pairs={{0,1},{1,0},{2,3},{3,2},{4,5},{5,4},{6,7},{7,6},{8,9},{9,8},{10,11... | collective-permute-start | bytes 983048 | tf_op jit(solution)/shard_map/ppermute | solution.py:365
  54.0 2.3 %copy-start = (f32[4,5,32,128]{3,2,1,0:T(8,128)}, f32[4,5,32,128]{3,2,1,0:T(8,128)S(1)}, u32[]{:S(2)}) copy-start(f32[4,5,32,128]{3,2,1,0:T(8,128)S(1)} %add.3.refs_2_) | copy-start | bytes 983044

commit v7 on v6

--- a/solution.py
+++ b/solution.py
@@ -9,7 +9,6 @@
 
 LANES = 128
 F32 = jnp.float32
-EXACT = functools.partial(lax.dot_general, precision=lax.Precision.HIGHEST, preferred_element_type=F32)
 SHORT = functools.partial(lax.dot_general, preferred_element_type=F32)
 
 
@@ -29,6 +28,12 @@
     left = jnp.concatenate([left_high, left_low, left_high], axis=contract[0])
     right = jnp.concatenate([right_high, right_high, right_low], axis=0)
     return SHORT(left, right, ((contract, (0,)), ((), ())))
+
+
+def place_whole(numbers, table, dims):
+    high, low = two_parts(numbers)
+    table = table.astype(jnp.bfloat16)
+    return SHORT(high, table, dims) + SHORT(low, table, dims)
 
 
 def hot(rows, wanted):
@@ -73,7 +78,7 @@
     core = at // (chips * cap)
     chosen = row == (at // cap - core * chips) * 2 + core
     spread = jnp.where(iota((cap, slots), 1) % cap == iota((cap, slots), 0), 1.0, 0.0)
-    wide = EXACT(numbers, spread, (((1,), (0,)), ((), ())))
+    wide = place_whole(numbers, spread, (((1,), (0,)), ((), ())))
     out[total:, :] = jnp.zeros((out.shape[0] - total, LANES), F32)
     for g in range(lats):
         lanes = jnp.where(chosen, wide[g * slabs : (g + 1) * slabs], 0.0)
@@ -83,7 +88,7 @@
     row = iota((lats * slabs, slots), 0)
     at = iota((lats * slabs, slots), 1)
     spread = jnp.where(iota((cap, slots), 1) % cap == iota((cap, slots), 0), 1.0, 0.0)
-    wide = EXACT(numbers, spread, (((1,), (0,)), ((), ())))
+    wide = place_whole(numbers, spread, (((1,), (0,)), ((), ())))
     mine[...] = jnp.zeros(mine.shape, F32)
     for core in range(2):
         lanes = jnp.where(row == at // cap * 2 + core, wide, 0.0)
@@ -134,7 +139,7 @@
     level = (at - chip * span) // wide
     block = at - chip * span - level * wide
     order = jnp.where(iota((total, total), 0) == (level * chips + chip) * wide + block, 1.0, 0.0)
-    return EXACT(dest.astype(F32), order, (((1,), (0,)), ((), ()))).astype(jnp.int32)
+    return place_whole(dest.astype(F32), order, (((1,), (0,)), ((), ()))).astype(jnp.int32)
 
 
 def slot_table(dims, core, dest, by_chip):

time: 56.6 us -> 56.5 us (level)
  no operation moved by 1% of the time
where the time goes in v7:
time: 56.5 us; the launch traced here: 56.3 us
  starting transfers between devices  28.3 us (50%)
  waiting for transfers between devices  22.1 us (39%)
  Pallas kernels  5.09 us (9%)
  between operations  0.78 us (1%)
    ppermute x24, starting transfers between devices, swap(): return lax.ppermute(array, axis, [(i, i ^ bit) for i in range(count)])  28.3 us
    ppermute x24, waiting for transfers between devices, swap(): return lax.ppermute(array, axis, [(i, i ^ bit) for i in range(count)])  22.1 us
    pallas_call x11, Pallas kernels, call(): pl.pallas_call(functools.partial(kernel, dims) if outside else lambda *re...  5.09 us
  transfers between devices with their start and end apart: 24, of which 14 were waited for; matrix products, arithmetic and copies ran while one was open for 0% of the time, Pallas kernels for 8%

profile of v7, /device:TPU:0, one launch (start us, length us, event | category | flops | bytes accessed | tf_op | source)
XLA Modules:
  0.0 56.3 jit_solution(1698939637091975750)
XLA Ops:
  0.6 0.5 collective-permute-start.2
  1.1 1.3 %shard_map.77 = (f32[648,128]{1,0:T(8,128)S(1)}, f32[392,128]{1,0:T(8,128)S(1)}, f32[8,128]{1,0:T(8,128)S(1)}, f32[640,128]{1,0:T(8,128)S(1)}, f32[128,128]{1,0:T(8,128)S(1)}, /*index=5*/f32[5,32,32]{2,1,0:T(8,128)S(1)}) custom-call(f32[640,128]{1,0:T(8,128)} %bitcast.22, s32[4,8,8]{2,1,0:T(8,128)} %bitcast.27, s32[1,128]{1,0:T(1,128)} %bitcast.28, ...), custom_call_target="tpu_custom_call" | custom-call | tf_op jit(solution)/shard_map/pallas_call | solution.py:355
  2.4 2.7 %collective-permute-start.6 = (f32[648,128]{1,0:T(8,128)S(1)}, f32[648,128]{1,0:T(8,128)S(1)}, u32[]{:S(2)}, u32[]{:S(2)}) collective-permute-start(f32[648,128]{1,0:T(8,128)S(1)} %get-tuple-element.35.refs_5_), channel_id=1, source_target_pairs={{0,8},{8,0},{16,24},{24,16},{1,9},{9,1},{17,25},{25,17},{2,10},{10... | collective-permute-start | bytes 995336 | tf_op jit(solution)/shard_map/ppermute | solution.py:370
  5.1 2.6 %collective-permute-start = (f32[648,128]{1,0:T(8,128)S(1)}, f32[648,128]{1,0:T(8,128)S(1)}, u32[]{:S(2)}, u32[]{:S(2)}) collective-permute-start(f32[648,128]{1,0:T(8,128)S(1)} %get-tuple-element.35.refs_5_), channel_id=1, source_target_pairs={{0,16},{8,24},{16,0},{24,8},{1,17},{9,25},{17,1},{25,9},{2,18},{10... | collective-permute-start | bytes 995336 | tf_op jit(solution)/shard_map/ppermute | solution.py:370
  7.7 0.0 collective-permute-start.1
  7.7 0.0 collective-permute-done.2.refs_2_
  7.7 0.4 shard_map.78
  8.1 1.6 %collective-permute-start.3 = (f32[224,128]{1,0:T(8,128)S(1)}, f32[224,128]{1,0:T(8,128)S(1)}, u32[]{:S(2)}, u32[]{:S(2)}) collective-permute-start(f32[224,128]{1,0:T(8,128)S(1)} %get-tuple-element.40), channel_id=1, source_target_pairs={{0,2},{1,3},{2,0},{3,1},{4,6},{5,7},{6,4},{7,5},{8,10},{9,11},{10,... | collective-permute-start | bytes 344072 | tf_op jit(solution)/shard_map/ppermute | solution.py:370
  9.7 1.5 %collective-permute-start.4 = (f32[224,128]{1,0:T(8,128)S(1)}, f32[224,128]{1,0:T(8,128)S(1)}, u32[]{:S(2)}, u32[]{:S(2)}) collective-permute-start(f32[224,128]{1,0:T(8,128)S(1)} %get-tuple-element.41), channel_id=1, source_target_pairs={{0,4},{1,5},{2,6},{3,7},{4,0},{5,1},{6,2},{7,3},{8,12},{9,13},{10,... | collective-permute-start | bytes 344072 | tf_op jit(solution)/shard_map/ppermute | solution.py:370
  11.2 0.0 collective-permute-done.1.refs_6_.refs_2_.refs_1_
  11.2 0.5 collective-permute-start.5
  11.6 2.1 %collective-permute-done.3.refs_3_.refs_2_ = f32[224,128]{1,0:T(8,128)S(1)} collective-permute-done((f32[224,128]{1,0:T(8,128)S(1)}, f32[224,128]{1,0:T(8,128)S(1)}, u32[]{:S(2)}, u32[]{:S(2)}) %collective-permute-start.3) | collective-permute-done | bytes 114720 | tf_op jit(solution)/shard_map/ppermute | solution.py:370
  13.7 3.7 %collective-permute-done.4.refs_4_.refs_3_ = f32[224,128]{1,0:T(8,128)S(1)} collective-permute-done((f32[224,128]{1,0:T(8,128)S(1)}, f32[224,128]{1,0:T(8,128)S(1)}, u32[]{:S(2)}, u32[]{:S(2)}) %collective-permute-start.4) | collective-permute-done | bytes 114720 | tf_op jit(solution)/shard_map/ppermute | solution.py:370
  17.4 0.0 collective-permute-done.5.refs_5_.refs_4_
  17.4 0.5 shard_map.79
  17.9 1.3 %collective-permute-start.10 = (f32[2,4,6,8,128]{4,3,2,1,0:T(8,128)S(1)}, f32[2,4,6,8,128]{4,3,2,1,0:T(8,128)S(1)}, u32[]{:S(2)}, u32[]{:S(2)}) collective-permute-start(f32[2,4,6,8,128]{4,3,2,1,0:T(8,128)S(1)} %get-tuple-element.48), channel_id=1, source_target_pairs={{0,2},{1,3},{2,0},{3,1},{4,6},{5,7},{6,4},{7,5},{8,10},{9,11},{10,... | collective-permute-start | bytes 589832 | tf_op jit(solution)/shard_map/ppermute | solution.py:370
  19.2 0.2 collective-permute-start.9
  19.4 0.8 %collective-permute-start.11 = (f32[2,4,6,8,128]{4,3,2,1,0:T(8,128)S(1)}, f32[2,4,6,8,128]{4,3,2,1,0:T(8,128)S(1)}, u32[]{:S(2)}, u32[]{:S(2)}) collective-permute-start(f32[2,4,6,8,128]{4,3,2,1,0:T(8,128)S(1)} %get-tuple-element.49), channel_id=1, source_target_pairs={{0,4},{1,5},{2,6},{3,7},{4,0},{5,1},{6,2},{7,3},{8,12},{9,13},{10,... | collective-permute-start | bytes 589832 | tf_op jit(solution)/shard_map/ppermute | solution.py:370
  20.2 0.3 collective-permute-done.6.refs_4_.refs_6_
  20.6 2.6 %collective-permute-start.12 = (f32[2,4,6,8,128]{4,3,2,1,0:T(8,128)S(1)}, f32[2,4,6,8,128]{4,3,2,1,0:T(8,128)S(1)}, u32[]{:S(2)}, u32[]{:S(2)}) collective-permute-start(f32[2,4,6,8,128]{4,3,2,1,0:T(8,128)S(1)} %get-tuple-element.50), channel_id=1, source_target_pairs={{0,6},{1,7},{2,4},{3,5},{4,2},{5,3},{6,0},{7,1},{8,14},{9,15},{10,... | collective-permute-start | bytes 589832 | tf_op jit(solution)/shard_map/ppermute | solution.py:370
  23.2 4.3 %collective-permute-done.refs_0_.refs_7_ = f32[648,128]{1,0:T(8,128)S(1)} collective-permute-done((f32[648,128]{1,0:T(8,128)S(1)}, f32[648,128]{1,0:T(8,128)S(1)}, u32[]{:S(2)}, u32[]{:S(2)}) %collective-permute-start) | collective-permute-done | bytes 331808 | tf_op jit(solution)/shard_map/ppermute | solution.py:370
  27.4 0.3 shard_map.80
  27.7 0.4 collective-permute-start.8
  28.1 0.0 collective-permute-done.10.refs_1_
  28.1 0.0 collective-permute-start.7
  28.1 1.5 %collective-permute-done.11.refs_2_ = f32[2,4,6,8,128]{4,3,2,1,0:T(8,128)S(1)} collective-permute-done((f32[2,4,6,8,128]{4,3,2,1,0:T(8,128)S(1)}, f32[2,4,6,8,128]{4,3,2,1,0:T(8,128)S(1)}, u32[]{:S(2)}, u32[]{:S(2)}) %collective-permute-start.11) | collective-permute-done | bytes 196640 | tf_op jit(solution)/shard_map/ppermute | solution.py:370
  29.7 0.0 collective-permute-done.12.refs_3_
  29.7 1.9 %collective-permute-start.16 = (f32[6,2,4,8,128]{4,3,2,1,0:T(8,128)S(1)}, f32[6,2,4,8,128]{4,3,2,1,0:T(8,128)S(1)}, u32[]{:S(2)}, u32[]{:S(2)}) collective-permute-start(f32[6,2,4,8,128]{4,3,2,1,0:T(8,128)S(1)} %shard_map.81.refs_10_), channel_id=1, source_target_pairs={{0,16},{8,24},{16,0},{24,8},{1,17},{9,25},{17,1},{25,9},{2,18},{10... | collective-permute-start | bytes 589832 | tf_op jit(solution)/shard_map/ppermute | solution.py:370
  31.6 0.0 collective-permute-done.9.refs_9_
  31.6 0.0 collective-permute-done.7.refs_0_
  31.6 1.1 %collective-permute-done.8.refs_8_ = f32[256,128]{1,0:T(8,128)S(1)} collective-permute-done((f32[256,128]{1,0:T(8,128)S(1)}, f32[256,128]{1,0:T(8,128)S(1)}, u32[]{:S(2)}, u32[]{:S(2)}) %collective-permute-start.8) | collective-permute-done | bytes 131104 | tf_op jit(solution)/shard_map/ppermute | solution.py:370
  32.8 0.5 shard_map.82
  33.3 1.6 %collective-permute-start.13 = (f32[2,4,5,8,128]{4,3,2,1,0:T(8,128)S(1)}, f32[2,4,5,8,128]{4,3,2,1,0:T(8,128)S(1)}, u32[]{:S(2)}, u32[]{:S(2)}) collective-permute-start(f32[2,4,5,8,128]{4,3,2,1,0:T(8,128)S(1)} %get-tuple-element.52), channel_id=1, source_target_pairs={{0,2},{1,3},{2,0},{3,1},{4,6},{5,7},{6,4},{7,5},{8,10},{9,11},{10,... | collective-permute-start | bytes 491528 | tf_op jit(solution)/shard_map/ppermute | solution.py:370
  34.8 1.5 %collective-permute-start.14 = (f32[2,4,5,8,128]{4,3,2,1,0:T(8,128)S(1)}, f32[2,4,5,8,128]{4,3,2,1,0:T(8,128)S(1)}, u32[]{:S(2)}, u32[]{:S(2)}) collective-permute-start(f32[2,4,5,8,128]{4,3,2,1,0:T(8,128)S(1)} %get-tuple-element.53), channel_id=1, source_target_pairs={{0,4},{1,5},{2,6},{3,7},{4,0},{5,1},{6,2},{7,3},{8,12},{9,13},{10,... | collective-permute-start | bytes 491528 | tf_op jit(solution)/shard_map/ppermute | solution.py:370
  36.4 0.5 collective-permute-start.15
  36.8 0.1 shard_map.84
  36.9 1.2 %collective-permute-start.20 = (f32[6,2,4,8,128]{4,3,2,1,0:T(8,128)S(1)}, f32[6,2,4,8,128]{4,3,2,1,0:T(8,128)S(1)}, u32[]{:S(2)}, u32[]{:S(2)}) collective-permute-start(f32[6,2,4,8,128]{4,3,2,1,0:T(8,128)S(1)} %get-tuple-element.60), channel_id=1, source_target_pairs={{0,8},{8,0},{16,24},{24,16},{1,9},{9,1},{17,25},{25,17},{2,10},{10... | collective-permute-start | bytes 589832 | tf_op jit(solution)/shard_map/ppermute | solution.py:370
  38.1 1.9 %collective-permute-done.13.refs_2_ = f32[2,4,5,8,128]{4,3,2,1,0:T(8,128)S(1)} collective-permute-done((f32[2,4,5,8,128]{4,3,2,1,0:T(8,128)S(1)}, f32[2,4,5,8,128]{4,3,2,1,0:T(8,128)S(1)}, u32[]{:S(2)}, u32[]{:S(2)}) %collective-permute-start.13) | collective-permute-done | bytes 163872 | tf_op jit(solution)/shard_map/ppermute | solution.py:370
  40.0 3.3 %collective-permute-start.21 = (f32[6,2,4,8,128]{4,3,2,1,0:T(8,128)S(1)}, f32[6,2,4,8,128]{4,3,2,1,0:T(8,128)S(1)}, u32[]{:S(2)}, u32[]{:S(2)}) collective-permute-start(f32[6,2,4,8,128]{4,3,2,1,0:T(8,128)S(1)} %get-tuple-element.61), channel_id=1, source_target_pairs={{0,24},{8,16},{16,8},{24,0},{1,25},{9,17},{17,9},{25,1},{2,26},{10... | collective-permute-start | bytes 589832 | tf_op jit(solution)/shard_map/ppermute | solution.py:370
  43.2 0.4 collective-permute-done.14.refs_3_
  43.6 0.0 collective-permute-done.15.refs_4_
  43.6 0.7 %collective-permute-done.16.refs_5_.refs_4_ = f32[6,2,4,8,128]{4,3,2,1,0:T(8,128)S(1)} collective-permute-done((f32[6,2,4,8,128]{4,3,2,1,0:T(8,128)S(1)}, f32[6,2,4,8,128]{4,3,2,1,0:T(8,128)S(1)}, u32[]{:S(2)}, u32[]{:S(2)}) %collective-permute-start.16) | collective-permute-done | bytes 196640 | tf_op jit(solution)/shard_map/ppermute | solution.py:370
  44.4 0.4 shard_map.83
  44.8 0.9 %collective-permute-start.17 = (f32[5,2,32,128]{3,2,1,0:T(8,128)S(1)}, f32[5,2,32,128]{3,2,1,0:T(8,128)S(1)}, u32[]{:S(2)}, u32[]{:S(2)}) collective-permute-start(f32[5,2,32,128]{3,2,1,0:T(8,128)S(1)} %get-tuple-element.56), channel_id=1, source_target_pairs={{0,2},{1,3},{2,0},{3,1},{4,6},{5,7},{6,4},{7,5},{8,10},{9,11},{10,... | collective-permute-start | bytes 491528 | tf_op jit(solution)/shard_map/ppermute | solution.py:370
  45.7 1.5 %collective-permute-start.18 = (f32[5,2,32,128]{3,2,1,0:T(8,128)S(1)}, f32[5,2,32,128]{3,2,1,0:T(8,128)S(1)}, u32[]{:S(2)}, u32[]{:S(2)}) collective-permute-start(f32[5,2,32,128]{3,2,1,0:T(8,128)S(1)} %get-tuple-element.57), channel_id=1, source_target_pairs={{0,4},{1,5},{2,6},{3,7},{4,0},{5,1},{6,2},{7,3},{8,12},{9,13},{10,... | collective-permute-start | bytes 491528 | tf_op jit(solution)/shard_map/ppermute | solution.py:370
  47.3 1.1 %collective-permute-start.19 = (f32[5,2,32,128]{3,2,1,0:T(8,128)S(1)}, f32[5,2,32,128]{3,2,1,0:T(8,128)S(1)}, u32[]{:S(2)}, u32[]{:S(2)}) collective-permute-start(f32[5,2,32,128]{3,2,1,0:T(8,128)S(1)} %get-tuple-element.58), channel_id=1, source_target_pairs={{0,6},{1,7},{2,4},{3,5},{4,2},{5,3},{6,0},{7,1},{8,14},{9,15},{10,... | collective-permute-start | bytes 491528 | tf_op jit(solution)/shard_map/ppermute | solution.py:370
  48.4 1.1 %collective-permute-done.20.refs_3_ = f32[6,2,4,8,128]{4,3,2,1,0:T(8,128)S(1)} collective-permute-done((f32[6,2,4,8,128]{4,3,2,1,0:T(8,128)S(1)}, f32[6,2,4,8,128]{4,3,2,1,0:T(8,128)S(1)}, u32[]{:S(2)}, u32[]{:S(2)}) %collective-permute-start.20) | collective-permute-done | bytes 196640 | tf_op jit(solution)/shard_map/ppermute | solution.py:370
  49.5 0.0 collective-permute-done.21.refs_5_
  49.5 0.9 %collective-permute-done.17.refs_6_.refs_2_ = f32[5,2,32,128]{3,2,1,0:T(8,128)S(1)} collective-permute-done((f32[5,2,32,128]{3,2,1,0:T(8,128)S(1)}, f32[5,2,32,128]{3,2,1,0:T(8,128)S(1)}, u32[]{:S(2)}, u32[]{:S(2)}) %collective-permute-start.17) | collective-permute-done | bytes 163872 | tf_op jit(solution)/shard_map/ppermute | solution.py:370
  50.4 0.5 shard_map.85
  50.9 0.1 collective-permute-start.23
  51.0 0.9 %collective-permute-done.18.refs_3_ = f32[5,2,32,128]{3,2,1,0:T(8,128)S(1)} collective-permute-done((f32[5,2,32,128]{3,2,1,0:T(8,128)S(1)}, f32[5,2,32,128]{3,2,1,0:T(8,128)S(1)}, u32[]{:S(2)}, u32[]{:S(2)}) %collective-permute-start.18) | collective-permute-done | bytes 163872 | tf_op jit(solution)/shard_map/ppermute | solution.py:370
  51.9 1.6 %collective-permute-done.19.refs_4_ = f32[5,2,32,128]{3,2,1,0:T(8,128)S(1)} collective-permute-done((f32[5,2,32,128]{3,2,1,0:T(8,128)S(1)}, f32[5,2,32,128]{3,2,1,0:T(8,128)S(1)}, u32[]{:S(2)}, u32[]{:S(2)}) %collective-permute-start.19) | collective-permute-done | bytes 163872 | tf_op jit(solution)/shard_map/ppermute | solution.py:370
  53.5 0.3 shard_map.86
  53.8 0.1 collective-permute-start.22
  53.9 0.0 collective-permute-done.23
  54.0 0.0 copy-start
  54.0 1.5 %collective-permute-done.22.refs_1_ = f32[640,128]{1,0:T(8,128)S(1)} collective-permute-done((f32[640,128]{1,0:T(8,128)S(1)}, f32[640,128]{1,0:T(8,128)S(1)}, u32[]{:S(2)}, u32[]{:S(2)}) %collective-permute-start.22) | collective-permute-done | bytes 327712 | tf_op jit(solution)/shard_map/ppermute | solution.py:370
  55.5 0.8 %shard_map.87 = f32[640,128]{1,0:T(8,128)} custom-call(f32[640,128]{1,0:T(8,128)S(1)} %get-tuple-element.63.refs_0_, f32[640,128]{1,0:T(8,128)S(1)} %collective-permute-done.22.refs_1_, f32[4,5,32,128]{3,2,1,0:T(8,128)S(1)} %add.3.refs_2_), custom_call_target="tpu_custom_call" | custom-call | tf_op jit(solution)/shard_map/pallas_call | solution.py:355
  56.3 0.0 copy-done
  (2 shorter events, 0.1 us)
Async XLA Ops:
  0.6 7.1 %collective-permute-start.2 = (f32[640,128]{1,0:T(8,128)}, f32[640,128]{1,0:T(8,128)S(1)}, u32[]{:S(2)}, u32[]{:S(2)}) collective-permute-start(f32[640,128]{1,0:T(8,128)} %bitcast.23), channel_id=1, source_target_pairs={{0,1},{1,0},{2,3},{3,2},{4,5},{5,4},{6,7},{7,6},{8,9},{9,8},{10,11... | collective-permute-start | bytes 983048 | tf_op jit(solution)/shard_map/ppermute | solution.py:370
  2.4 18.1 %collective-permute-start.6 = (f32[648,128]{1,0:T(8,128)S(1)}, f32[648,128]{1,0:T(8,128)S(1)}, u32[]{:S(2)}, u32[]{:S(2)}) collective-permute-start(f32[648,128]{1,0:T(8,128)S(1)} %get-tuple-element.35.refs_5_), channel_id=1, source_target_pairs={{0,8},{8,0},{16,24},{24,16},{1,9},{9,1},{17,25},{25,17},{2,10},{10... | collective-permute-start | bytes 995336 | tf_op jit(solution)/shard_map/ppermute | solution.py:370
  5.1 22.3 %collective-permute-start = (f32[648,128]{1,0:T(8,128)S(1)}, f32[648,128]{1,0:T(8,128)S(1)}, u32[]{:S(2)}, u32[]{:S(2)}) collective-permute-start(f32[648,128]{1,0:T(8,128)S(1)} %get-tuple-element.35.refs_5_), channel_id=1, source_target_pairs={{0,16},{8,24},{16,0},{24,8},{1,17},{9,25},{17,1},{25,9},{2,18},{10... | collective-permute-start | bytes 995336 | tf_op jit(solution)/shard_map/ppermute | solution.py:370
  7.7 3.5 %collective-permute-start.1 = (f32[8,128]{1,0:T(8,128)S(1)}, f32[8,128]{1,0:T(8,128)S(1)}, u32[]{:S(2)}, u32[]{:S(2)}) collective-permute-start(f32[8,128]{1,0:T(8,128)S(1)} %get-tuple-element.36.refs_4_.refs_0_.refs_1_), channel_id=1, source_target_pairs={{0,1},{1,0},{2,3},{3,2},{4,5},{5,4},{6,7},{7,6},{8,9},{9,8},{10,11... | collective-permute-start | bytes 12296 | tf_op jit(solution)/shard_map/ppermute | solution.py:370
  8.1 5.6 %collective-permute-start.3 = (f32[224,128]{1,0:T(8,128)S(1)}, f32[224,128]{1,0:T(8,128)S(1)}, u32[]{:S(2)}, u32[]{:S(2)}) collective-permute-start(f32[224,128]{1,0:T(8,128)S(1)} %get-tuple-element.40), channel_id=1, source_target_pairs={{0,2},{1,3},{2,0},{3,1},{4,6},{5,7},{6,4},{7,5},{8,10},{9,11},{10,... | collective-permute-start | bytes 344072 | tf_op jit(solution)/shard_map/ppermute | solution.py:370
  9.7 7.7 %collective-permute-start.4 = (f32[224,128]{1,0:T(8,128)S(1)}, f32[224,128]{1,0:T(8,128)S(1)}, u32[]{:S(2)}, u32[]{:S(2)}) collective-permute-start(f32[224,128]{1,0:T(8,128)S(1)} %get-tuple-element.41), channel_id=1, source_target_pairs={{0,4},{1,5},{2,6},{3,7},{4,0},{5,1},{6,2},{7,3},{8,12},{9,13},{10,... | collective-permute-start | bytes 344072 | tf_op jit(solution)/shard_map/ppermute | solution.py:370
  11.2 6.2 %collective-permute-start.5 = (f32[224,128]{1,0:T(8,128)S(1)}, f32[224,128]{1,0:T(8,128)S(1)}, u32[]{:S(2)}, u32[]{:S(2)}) collective-permute-start(f32[224,128]{1,0:T(8,128)S(1)} %get-tuple-element.42), channel_id=1, source_target_pairs={{0,6},{1,7},{2,4},{3,5},{4,2},{5,3},{6,0},{7,1},{8,14},{9,15},{10,... | collective-permute-start | bytes 344072 | tf_op jit(solution)/shard_map/ppermute | solution.py:370
  17.9 10.2 %collective-permute-start.10 = (f32[2,4,6,8,128]{4,3,2,1,0:T(8,128)S(1)}, f32[2,4,6,8,128]{4,3,2,1,0:T(8,128)S(1)}, u32[]{:S(2)}, u32[]{:S(2)}) collective-permute-start(f32[2,4,6,8,128]{4,3,2,1,0:T(8,128)S(1)} %get-tuple-element.48), channel_id=1, source_target_pairs={{0,2},{1,3},{2,0},{3,1},{4,6},{5,7},{6,4},{7,5},{8,10},{9,11},{10,... | collective-permute-start | bytes 589832 | tf_op jit(solution)/shard_map/ppermute | solution.py:370
  19.2 12.4 %collective-permute-start.9 = (f32[392,128]{1,0:T(8,128)S(1)}, f32[392,128]{1,0:T(8,128)S(1)}, u32[]{:S(2)}, u32[]{:S(2)}) collective-permute-start(f32[392,128]{1,0:T(8,128)S(1)} %get-tuple-element.47), channel_id=1, source_target_pairs={{0,24},{8,16},{16,8},{24,0},{1,25},{9,17},{17,9},{25,1},{2,26},{10... | collective-permute-start | bytes 602120 | tf_op jit(solution)/shard_map/ppermute | solution.py:370
  19.4 10.2 %collective-permute-start.11 = (f32[2,4,6,8,128]{4,3,2,1,0:T(8,128)S(1)}, f32[2,4,6,8,128]{4,3,2,1,0:T(8,128)S(1)}, u32[]{:S(2)}, u32[]{:S(2)}) collective-permute-start(f32[2,4,6,8,128]{4,3,2,1,0:T(8,128)S(1)} %get-tuple-element.49), channel_id=1, source_target_pairs={{0,4},{1,5},{2,6},{3,7},{4,0},{5,1},{6,2},{7,3},{8,12},{9,13},{10,... | collective-permute-start | bytes 589832 | tf_op jit(solution)/shard_map/ppermute | solution.py:370
  20.6 9.1 %collective-permute-start.12 = (f32[2,4,6,8,128]{4,3,2,1,0:T(8,128)S(1)}, f32[2,4,6,8,128]{4,3,2,1,0:T(8,128)S(1)}, u32[]{:S(2)}, u32[]{:S(2)}) collective-permute-start(f32[2,4,6,8,128]{4,3,2,1,0:T(8,128)S(1)} %get-tuple-element.50), channel_id=1, source_target_pairs={{0,6},{1,7},{2,4},{3,5},{4,2},{5,3},{6,0},{7,1},{8,14},{9,15},{10,... | collective-permute-start | bytes 589832 | tf_op jit(solution)/shard_map/ppermute | solution.py:370
  27.7 5.0 %collective-permute-start.8 = (f32[256,128]{1,0:T(8,128)S(1)}, f32[256,128]{1,0:T(8,128)S(1)}, u32[]{:S(2)}, u32[]{:S(2)}) collective-permute-start(f32[256,128]{1,0:T(8,128)S(1)} %get-tuple-element.46), channel_id=1, source_target_pairs={{0,8},{8,0},{16,24},{24,16},{1,9},{9,1},{17,25},{25,17},{2,10},{10... | collective-permute-start | bytes 393224 | tf_op jit(solution)/shard_map/ppermute | solution.py:370
  28.1 3.5 %collective-permute-start.7 = (f32[4,32,128]{2,1,0:T(8,128)S(1)}, f32[4,32,128]{2,1,0:T(8,128)S(1)}, u32[]{:S(2)}, u32[]{:S(2)}) collective-permute-start(f32[4,32,128]{2,1,0:T(8,128)S(1)} %get-tuple-element.45), channel_id=1, source_target_pairs={{0,1},{1,0},{2,3},{3,2},{4,5},{5,4},{6,7},{7,6},{8,9},{9,8},{10,11... | collective-permute-start | bytes 196616 | tf_op jit(solution)/shard_map/ppermute | solution.py:370
  29.7 14.7 %collective-permute-start.16 = (f32[6,2,4,8,128]{4,3,2,1,0:T(8,128)S(1)}, f32[6,2,4,8,128]{4,3,2,1,0:T(8,128)S(1)}, u32[]{:S(2)}, u32[]{:S(2)}) collective-permute-start(f32[6,2,4,8,128]{4,3,2,1,0:T(8,128)S(1)} %shard_map.81.refs_10_), channel_id=1, source_target_pairs={{0,16},{8,24},{16,0},{24,8},{1,17},{9,25},{17,1},{25,9},{2,18},{10... | collective-permute-start | bytes 589832 | tf_op jit(solution)/shard_map/ppermute | solution.py:370
  33.3 6.7 %collective-permute-start.13 = (f32[2,4,5,8,128]{4,3,2,1,0:T(8,128)S(1)}, f32[2,4,5,8,128]{4,3,2,1,0:T(8,128)S(1)}, u32[]{:S(2)}, u32[]{:S(2)}) collective-permute-start(f32[2,4,5,8,128]{4,3,2,1,0:T(8,128)S(1)} %get-tuple-element.52), channel_id=1, source_target_pairs={{0,2},{1,3},{2,0},{3,1},{4,6},{5,7},{6,4},{7,5},{8,10},{9,11},{10,... | collective-permute-start | bytes 491528 | tf_op jit(solution)/shard_map/ppermute | solution.py:370
  34.8 8.8 %collective-permute-start.14 = (f32[2,4,5,8,128]{4,3,2,1,0:T(8,128)S(1)}, f32[2,4,5,8,128]{4,3,2,1,0:T(8,128)S(1)}, u32[]{:S(2)}, u32[]{:S(2)}) collective-permute-start(f32[2,4,5,8,128]{4,3,2,1,0:T(8,128)S(1)} %get-tuple-element.53), channel_id=1, source_target_pairs={{0,4},{1,5},{2,6},{3,7},{4,0},{5,1},{6,2},{7,3},{8,12},{9,13},{10,... | collective-permute-start | bytes 491528 | tf_op jit(solution)/shard_map/ppermute | solution.py:370
  36.4 7.3 %collective-permute-start.15 = (f32[2,4,5,8,128]{4,3,2,1,0:T(8,128)S(1)}, f32[2,4,5,8,128]{4,3,2,1,0:T(8,128)S(1)}, u32[]{:S(2)}, u32[]{:S(2)}) collective-permute-start(f32[2,4,5,8,128]{4,3,2,1,0:T(8,128)S(1)} %get-tuple-element.54), channel_id=1, source_target_pairs={{0,6},{1,7},{2,4},{3,5},{4,2},{5,3},{6,0},{7,1},{8,14},{9,15},{10,... | collective-permute-start | bytes 491528 | tf_op jit(solution)/shard_map/ppermute | solution.py:370
  36.9 12.6 %collective-permute-start.20 = (f32[6,2,4,8,128]{4,3,2,1,0:T(8,128)S(1)}, f32[6,2,4,8,128]{4,3,2,1,0:T(8,128)S(1)}, u32[]{:S(2)}, u32[]{:S(2)}) collective-permute-start(f32[6,2,4,8,128]{4,3,2,1,0:T(8,128)S(1)} %get-tuple-element.60), channel_id=1, source_target_pairs={{0,8},{8,0},{16,24},{24,16},{1,9},{9,1},{17,25},{25,17},{2,10},{10... | collective-permute-start | bytes 589832 | tf_op jit(solution)/shard_map/ppermute | solution.py:370
  40.0 9.5 %collective-permute-start.21 = (f32[6,2,4,8,128]{4,3,2,1,0:T(8,128)S(1)}, f32[6,2,4,8,128]{4,3,2,1,0:T(8,128)S(1)}, u32[]{:S(2)}, u32[]{:S(2)}) collective-permute-start(f32[6,2,4,8,128]{4,3,2,1,0:T(8,128)S(1)} %get-tuple-element.61), channel_id=1, source_target_pairs={{0,24},{8,16},{16,8},{24,0},{1,25},{9,17},{17,9},{25,1},{2,26},{10... | collective-permute-start | bytes 589832 | tf_op jit(solution)/shard_map/ppermute | solution.py:370
  44.8 5.6 %collective-permute-start.17 = (f32[5,2,32,128]{3,2,1,0:T(8,128)S(1)}, f32[5,2,32,128]{3,2,1,0:T(8,128)S(1)}, u32[]{:S(2)}, u32[]{:S(2)}) collective-permute-start(f32[5,2,32,128]{3,2,1,0:T(8,128)S(1)} %get-tuple-element.56), channel_id=1, source_target_pairs={{0,2},{1,3},{2,0},{3,1},{4,6},{5,7},{6,4},{7,5},{8,10},{9,11},{10,... | collective-permute-start | bytes 491528 | tf_op jit(solution)/shard_map/ppermute | solution.py:370
  45.7 6.2 %collective-permute-start.18 = (f32[5,2,32,128]{3,2,1,0:T(8,128)S(1)}, f32[5,2,32,128]{3,2,1,0:T(8,128)S(1)}, u32[]{:S(2)}, u32[]{:S(2)}) collective-permute-start(f32[5,2,32,128]{3,2,1,0:T(8,128)S(1)} %get-tuple-element.57), channel_id=1, source_target_pairs={{0,4},{1,5},{2,6},{3,7},{4,0},{5,1},{6,2},{7,3},{8,12},{9,13},{10,... | collective-permute-start | bytes 491528 | tf_op jit(solution)/shard_map/ppermute | solution.py:370
  47.3 6.2 %collective-permute-start.19 = (f32[5,2,32,128]{3,2,1,0:T(8,128)S(1)}, f32[5,2,32,128]{3,2,1,0:T(8,128)S(1)}, u32[]{:S(2)}, u32[]{:S(2)}) collective-permute-start(f32[5,2,32,128]{3,2,1,0:T(8,128)S(1)} %get-tuple-element.58), channel_id=1, source_target_pairs={{0,6},{1,7},{2,4},{3,5},{4,2},{5,3},{6,0},{7,1},{8,14},{9,15},{10,... | collective-permute-start | bytes 491528 | tf_op jit(solution)/shard_map/ppermute | solution.py:370
  50.9 3.0 %collective-permute-start.23 = (f32[4,5,32,128]{3,2,1,0:T(8,128)S(1)}, f32[4,5,32,128]{3,2,1,0:T(8,128)S(1)}, u32[]{:S(2)}, u32[]{:S(2)}) collective-permute-start(f32[4,5,32,128]{3,2,1,0:T(8,128)S(1)} %get-tuple-element.62.refs_5_), channel_id=1, source_target_pairs={{0,1},{1,0},{2,3},{3,2},{4,5},{5,4},{6,7},{7,6},{8,9},{9,8},{10,11... | collective-permute-start | bytes 983048 | tf_op jit(solution)/shard_map/ppermute | solution.py:370
  53.8 1.7 %collective-permute-start.22 = (f32[640,128]{1,0:T(8,128)S(1)}, f32[640,128]{1,0:T(8,128)S(1)}, u32[]{:S(2)}, u32[]{:S(2)}) collective-permute-start(f32[640,128]{1,0:T(8,128)S(1)} %get-tuple-element.64), channel_id=1, source_target_pairs={{0,1},{1,0},{2,3},{3,2},{4,5},{5,4},{6,7},{7,6},{8,9},{9,8},{10,11... | collective-permute-start | bytes 983048 | tf_op jit(solution)/shard_map/ppermute | solution.py:370
  54.0 2.3 %copy-start = (f32[4,5,32,128]{3,2,1,0:T(8,128)}, f32[4,5,32,128]{3,2,1,0:T(8,128)S(1)}, u32[]{:S(2)}) copy-start(f32[4,5,32,128]{3,2,1,0:T(8,128)S(1)} %add.3.refs_2_) | copy-start | bytes 983044
